TPU v7x, 32 devices: a whole 2x2x4 slice. The times are simulated.
32 devices in a mesh: queue: 8 (over y, x, core), head: 4 (over z).
Axes of the slice: x: 2, y: 2, z: 4, core: 2. Of those that a mesh axis runs over, the one named last changes fastest.
Arguments:
- latents: bfloat16 [16, 384, 5120], P('queue'), may hold values from -6 to 6
- control: bfloat16 [16, 384, 5120], P('queue'), may hold values from -3 to 3
- levels: int32 [16], P('queue'), may hold values from 0 to 63
- window_mask: int32 [16, 2], P('queue'), may hold values 0 or 1
- modulation: float32 [64, 3, 5120], replicated, may hold values from -3 to 3
- w_query: bfloat16 [5120, 2560], P('queue', 'head'), may hold values from -1 to 1
- w_key: bfloat16 [5120, 2560], P('queue', 'head'), may hold values from -1 to 1
- w_value: bfloat16 [5120, 2560], P('queue', 'head'), may hold values from -0.078125 to 0.078125
- w_out: bfloat16 [2560, 5120], P('head', 'queue'), may hold values from -0.125 to 0.125
- q_gain: float32 [2560], P('head'), may hold values from 0.6 to 8
- k_gain: float32 [2560], P('head'), may hold values from 0.6 to 8
Outputs:
- next_queue: float32 [16, 384, 5120], P('queue', None, 'head')
All inputs are finite; a program needn't handle non-finite values. No bound on the sum of `window_mask` on one device may be relied on, other than what follows from the above.
Results may differ from a plain program's by a relative error of at most 0.019.
The roundings to bfloat16 on the way count: a program that leaves them out, or rounds other values in their place, can miss the bound.
Values may be sent and summed in bfloat16 or wider, within the bound.
No kernel may reach another device: no remote copies, remote signals or barrier semaphores. Data moves between devices by JAX's collectives and lax.ppermute only.
A program may use at most 192 MiB of HBM per device.

v0:
```python
import jax
import jax.numpy as jnp
from jax import lax
from jax.sharding import PartitionSpec as P

HD = 128


def from_behind(value, axis, by):
    peers = lax.axis_size(axis)
    pairs = [(i, i + by) for i in range(peers) if 0 <= i + by < peers]
    return lax.ppermute(value, axis, pairs)


def shifted(value, axis, steps):
    count = lax.axis_size(axis)
    pairs = [(source, (source + steps) % count) for source in range(count)]
    return lax.ppermute(value, axis, pairs)


def layer_norm(hidden):
    center = hidden - jnp.mean(hidden, axis=-1, keepdims=True)
    variance = jnp.mean(center * center, axis=-1, keepdims=True)
    return center * lax.rsqrt(variance + 1e-06)


def apply_gain(values, square_sum, total_width, gain):
    floats = values.astype(jnp.float32)
    return (floats * lax.rsqrt(square_sum[:, None] / total_width + 1e-06) * gain).astype(
        jnp.bfloat16
    )


def row_squares(values):
    floats = values.astype(jnp.float32)
    return jnp.sum(floats * floats, axis=-1)


def shards(
    latents,
    control,
    levels,
    window_mask,
    modulation,
    w_query,
    w_key,
    w_value,
    w_out,
    q_gain,
    k_gain,
):
    nchunk, row_count, model_width = latents.shape
    level_count = modulation.shape[0]
    local_cols = w_query.shape[1]
    heads_local = local_cols // HD
    head_count = lax.axis_size("head")
    total_width = local_cols * head_count
    owner_index = lax.axis_index("queue")
    head_index = lax.axis_index("head")
    first_span = owner_index * nchunk
    hidden = latents.astype(jnp.float32) + control.astype(jnp.float32)
    onehot = (levels[:, None] == jnp.arange(level_count, dtype=jnp.int32)[None, :]).astype(
        jnp.float32
    )
    level_mods = jnp.dot(
        onehot, modulation.reshape(level_count, 3 * model_width), precision=lax.Precision.HIGHEST
    ).reshape(nchunk, 3, model_width)
    normed = (
        layer_norm(hidden) * (1.0 + level_mods[:, 1][:, None, :]) + level_mods[:, 0][:, None, :]
    ).astype(jnp.bfloat16)
    flat_rows = normed.reshape(nchunk * row_count, model_width)
    row_total = nchunk * row_count
    pieces = (
        lax.all_gather(w_query, "queue", axis=0, tiled=True),
        lax.all_gather(w_key, "queue", axis=0, tiled=True),
        lax.all_gather(w_value, "queue", axis=0, tiled=True),
    )
    query, keyproj, valueproj = tuple(
        (
            jnp.dot(flat_rows, piece_rows, preferred_element_type=jnp.float32)
            for piece_rows in pieces
        )
    )
    query = query.astype(jnp.bfloat16)
    keyproj = keyproj.astype(jnp.bfloat16)
    valueproj = valueproj.astype(jnp.bfloat16)
    query_sq, key_sq = lax.psum((row_squares(query), row_squares(keyproj)), "head")
    qhat = apply_gain(query, query_sq, total_width, q_gain)
    own_keys = apply_gain(keyproj, key_sq, total_width, k_gain)
    prior_keys, prior_values = from_behind((own_keys, valueproj), "queue", 1)
    key_stack = jnp.concatenate([prior_keys, own_keys], axis=0).reshape(
        2 * nchunk, row_count, heads_local, HD
    )
    value_stack = jnp.concatenate([prior_values, valueproj], axis=0).reshape(
        2 * nchunk, row_count, heads_local, HD
    )
    key_windows = jnp.stack(
        [
            key_stack[nchunk + index_span - 2 : nchunk + index_span + 1]
            for index_span in range(nchunk)
        ]
    ).reshape(nchunk, 3 * row_count, heads_local, HD)
    value_windows = jnp.stack(
        [
            value_stack[nchunk + index_span - 2 : nchunk + index_span + 1]
            for index_span in range(nchunk)
        ]
    ).reshape(nchunk, 3 * row_count, heads_local, HD)
    span_ids = first_span + jnp.arange(nchunk, dtype=jnp.int32)
    seen_far = (window_mask[:, 0] == 1) & (span_ids >= 2)
    seen_near = (window_mask[:, 1] == 1) & (span_ids >= 1)
    seen = jnp.stack([seen_far, seen_near, jnp.ones((nchunk,), dtype=bool)], axis=1)
    key_seen = jnp.repeat(seen, row_count, axis=1)
    query_spans = qhat.reshape(nchunk, row_count, heads_local, HD)
    scores = jnp.einsum(
        "cqhd,ckhd->chqk", query_spans, key_windows, preferred_element_type=jnp.float32
    ) * HD ** (-0.5)
    scores = jnp.where(key_seen[:, None, None, :], scores, -1e30)
    top = jnp.max(scores, axis=-1, keepdims=True)
    expo = jnp.exp(scores - top)
    prob_bf = (expo / jnp.sum(expo, axis=-1, keepdims=True)).astype(jnp.bfloat16)
    attended = jnp.einsum(
        "chqk,ckhd->cqhd", prob_bf, value_windows, preferred_element_type=jnp.float32
    )
    attended = attended.astype(jnp.bfloat16).reshape(row_total, local_cols)
    partial_out = jnp.dot(
        attended,
        lax.all_gather(w_out, "queue", axis=1, tiled=True),
        preferred_element_type=jnp.float32,
    )
    col_width = model_width // head_count
    hidden_cols = lax.dynamic_slice_in_dim(hidden, head_index * col_width, col_width, 2)
    gate_cols = lax.dynamic_slice_in_dim(level_mods[:, 2], head_index * col_width, col_width, 1)
    partial_spans = partial_out.reshape(nchunk, row_count, model_width)
    branch_last = lax.psum_scatter(
        partial_spans[nchunk - 1].astype(jnp.bfloat16), "head", scatter_dimension=1, tiled=True
    ).astype(jnp.float32)
    updated_last = hidden_cols[nchunk - 1] + gate_cols[nchunk - 1][None, :] * branch_last
    arrived = shifted(updated_last.astype(jnp.bfloat16), "queue", 1).astype(updated_last.dtype)
    branch_rest = lax.psum_scatter(
        partial_spans[: nchunk - 1].astype(jnp.bfloat16), "head", scatter_dimension=2, tiled=True
    ).astype(jnp.float32)
    updated_rest = hidden_cols[: nchunk - 1] + gate_cols[: nchunk - 1][:, None, :] * branch_rest
    return jnp.concatenate([arrived[None], updated_rest], axis=0)


def solution(mesh):
    placed = (
        P("queue", None, None),
        P("queue", None, None),
        P("queue"),
        P("queue", None),
        P(),
        P("queue", "head"),
        P("queue", "head"),
        P("queue", "head"),
        P("head", "queue"),
        P("head"),
        P("head"),
    )
    return jax.shard_map(
        shards, mesh=mesh, in_specs=placed, out_specs=P("queue", None, "head"), check_vma=False
    )
```

profile of v0, /device:TPU:0, one launch (start us, length us, event | category | flops | bytes accessed | tf_op | source)
XLA Modules:
  0.0 395.4 jit_solution(1756189159875272588)
XLA Ops:
  6.5 0.7 all-gather.7.cloned.1.call-update
  7.3 0.7 all-gather.9.cloned.1.call-update
  8.1 0.7 all-gather.5.cloned.1.call-update
  8.8 0.5 all-gather.11.cloned.1.call-update
  9.4 3.5 fusion.6
  12.9 7.8 %fusion.54 = f32[2,384]{1,0:T(2,128)S(1)} fusion(bf16[2,384,5120]{2,1,0:T(8,128)(2,1)} %param.12, bf16[2,384,5120]{2,1,0:T(8,128)(2,1)} %param.11), kind=kLoop, calls=%fused_computation.78 | loop fusion | flops 15727872 | bytes 15731712 | tf_op jit(solution)/shard_map/reduce_sum | solution.py:22
  20.7 0.6 slice-done.1
  21.3 6.4 %multiply_reduce_fusion = f32[2,384]{1,0:T(2,128)S(1)} fusion(f32[2,384]{1,0:T(2,128)S(1)} %broadcast_multiply_fusion, bf16[2,384,5120]{2,1,0:T(8,128)(2,1)S(1)} %bitcast.60, bf16[2,384,5120]{2,1,0:T(8,128)(2,1)} %param.11), kind=kLoop, calls=%fused_computation.5 | loop fusion | flops 23592192 | bytes 15734784 | tf_op jit(solution)/shard_map/reduce_sum | solution.py:23
  27.7 0.1 compare_and_fusion.1
  27.8 0.1 pad.8.clone
  27.9 0.1 add_add_fusion
  28.0 16.1 %add_convert_fusion = (bf16[2,384,5120]{2,1,0:T(8,128)(2,1)}, f32[2,384,5120]{2,1,0:T(8,128)}) fusion(f32[2,5120]{1,0:T(2,128)S(1)} %get-tuple-element.18, f32[2,5120]{1,0:T(2,128)S(1)} %get-tuple-element.19, f32[2,384]{1,0:T(2,128)S(1)} %add_rsqrt_fusion.2, f32[2,384]{1,0:T(2,128)S(1)} %broadcast_multiply_fusion, bf16[2,384,5120]{2,1,0:T(8,128)(2,1)} %param.12, ...), kind=kLoop, calls=%fused_computation.4 | loop fusion | flops 31457280 | bytes 39409664 | tf_op jit(solution)/shard_map/convert_element_type | solution.py:70
  44.1 14.5 %all-gather.7.cloned.1.call-done = bf16[5120,640]{1,0:T(8,128)(2,1)} async-done(((bf16[640,640]{1,0:T(8,128)(2,1)}), bf16[5120,640]{1,0:T(8,128)(2,1)}) %all-gather.7.cloned.1.call-update) | async-done | bytes 6553616 | tf_op jit(solution)/shard_map/all_gather | solution.py:74
  58.6 10.4 %fusion.16 = (f32[768]{0:T(1024)S(1)}, bf16[768,640]{0,1:T(8,128)(2,1)S(1)}) fusion(bf16[768,5120]{1,0:T(8,128)(2,1)} %bitcast.61, bf16[5120,640]{1,0:T(8,128)(2,1)} %all-gather.7.cloned.1.call-done), kind=kOutput, calls=%fused_computation.29 | convolution fusion | flops 5035129856 | bytes 15404032 | tf_op jit(solution)/shard_map/dot_general | solution.py:80
  69.1 38.1 %all-gather.9.cloned.1.call-done = bf16[5120,640]{1,0:T(8,128)(2,1)} async-done(((bf16[640,640]{1,0:T(8,128)(2,1)}), bf16[5120,640]{1,0:T(8,128)(2,1)}) %all-gather.9.cloned.1.call-update) | async-done | bytes 6553616 | tf_op jit(solution)/shard_map/all_gather | solution.py:75
  107.2 10.6 %fusion.19 = (f32[768]{0:T(1024)S(1)}, bf16[768,640]{1,0:T(8,128)(2,1)S(1)}) fusion(bf16[768,5120]{1,0:T(8,128)(2,1)} %bitcast.62, bf16[5120,640]{1,0:T(8,128)(2,1)} %all-gather.9.cloned.1.call-done), kind=kOutput, calls=%fused_computation.32 | convolution fusion | flops 5035129856 | bytes 15404032 | tf_op jit(solution)/shard_map/dot_general | solution.py:80
  117.8 11.8 %all-reduce = (f32[768]{0:T(1024)S(1)}, f32[768]{0:T(1024)S(1)}) all-reduce(f32[768]{0:T(1024)S(1)} %get-tuple-element.22, f32[768]{0:T(1024)S(1)} %get-tuple-element.24), channel_id=1, replica_groups=mesh['queue'=8,'head'=4] {'head'}, use_global_device_ids=true, to_apply=%region_5.0 | all-reduce | flops 1536 | bytes 12288 | tf_op jit(solution)/shard_map/psum | solution.py:87
  129.7 0.3 fusion.21
  130.0 2.4 collective-permute-start.1
  132.4 31.9 %all-gather.5.cloned.1.call-done = bf16[5120,640]{1,0:T(8,128)(2,1)} async-done(((bf16[640,640]{1,0:T(8,128)(2,1)}), bf16[5120,640]{1,0:T(8,128)(2,1)}) %all-gather.5.cloned.1.call-update) | async-done | bytes 6553616 | tf_op jit(solution)/shard_map/all_gather | solution.py:76
  164.2 11.3 %convolution_convert_fusion.3 = bf16[768,640]{1,0:T(8,128)(2,1)} fusion(bf16[768,5120]{1,0:T(8,128)(2,1)} %bitcast.63, bf16[5120,640]{1,0:T(8,128)(2,1)} %all-gather.5.cloned.1.call-done), kind=kOutput, calls=%fused_computation.50 | convolution fusion | flops 5033656320 | bytes 15400960 | tf_op jit(solution)/shard_map/dot_general | solution.py:80
  175.5 3.2 collective-permute-start
  178.7 0.1 broadcast_bitcast_fusion
  178.8 0.3 fusion.18
  179.1 1.2 reshape.88
  180.3 2.0 fusion.28
  182.3 2.3 copy.22
  184.6 3.6 copy.24
  188.3 0.9 copy.21
  189.2 2.1 copy.23
  191.3 2.3 fusion.29
  193.6 2.3 copy.20
  195.9 0.9 copy.19
  196.9 14.6 %fusion.57 = (f32[2,5,384]{2,1,0:T(8,128)S(1)}, f32[2,5,384,1152]{3,2,1,0:T(8,128)}) fusion(pred[2,1152]{1,0:T(4,128)(4,1)S(1)} %bitcast.70, bf16[1,1152,5,128]{3,1,2,0:T(8,128)(2,1)} %copy.24, bf16[1,1152,5,128]{3,1,2,0:T(8,128)(2,1)} %copy.23, bf16[2,384,5,128]{1,0,3,2:T(2,128)(2,1)} %reshape.88), kind=kOutput, calls=%fused_computation.81 | convolution fusion | flops 1151632512 | bytes 21644544 | tf_op jit(solution)/shard_map/sub | solution.py:120
  211.4 7.7 %fusion.33 = bf16[2,384,5,128]{1,3,2,0:T(8,128)(2,1)S(1)} fusion(f32[2,5,384,1152]{3,2,1,0:T(8,128)} %get-tuple-element.27, f32[2,5,384]{2,1,0:T(8,128)S(1)} %get-tuple-element.26, bf16[1,1152,5,128]{1,3,2,0:T(8,128)(2,1)S(1)} %bitcast.67, bf16[1,1152,5,128]{1,3,2,0:T(8,128)(2,1)S(1)} %bitcast.68), kind=kOutput, calls=%fused_computation.51 | convolution fusion | flops 1143275520 | bytes 21642240 | tf_op jit(solution)/shard_map/chqk,ckhd->cqhd/dot_general | solution.py:122
  219.1 1.0 copy.26
  220.2 0.2 copy.30
  220.4 9.9 %convolution_convert_fusion = bf16[768,5120]{1,0:T(8,128)(2,1)S(1)} fusion(bf16[768,640]{0,1:T(8,128)(2,1)S(1)} %bitcast.69, bf16[640,5120]{1,0:T(8,128)(2,1)} %all-gather.11.cloned.1.call-done), kind=kOutput, calls=%fused_computation.12 | convolution fusion | flops 5037096960 | bytes 15400960 | tf_op jit(solution)/shard_map/dot_general | solution.py:126
  230.3 3.5 fusion.55
  233.9 0.5 reduce-scatter.5.cloned.1.call-update
  234.4 0.1 dynamic-slice_reduce_fusion.1
  234.5 74.5 %reduce-scatter.3.cloned.1.call-done = bf16[384,1280]{1,0:T(8,128)(2,1)} async-done(((bf16[384,5120]{1,0:T(8,128)(2,1)}), bf16[384,1280]{1,0:T(8,128)(2,1)}) %reduce-scatter.3.cloned.1.call-update) | async-done | bytes 983056 | tf_op jit(solution)/shard_map/reduce_scatter | solution.py:135
  309.0 2.0 fusion.23
  311.0 0.1 collective-permute-start.2
  311.1 73.1 %reduce-scatter.5.cloned.1.call-done = bf16[1,384,1280]{2,1,0:T(8,128)(2,1)} async-done(((bf16[1,384,5120]{2,1,0:T(8,128)(2,1)}), bf16[1,384,1280]{2,1,0:T(8,128)(2,1)}) %reduce-scatter.5.cloned.1.call-update) | async-done | bytes 983056 | tf_op jit(solution)/shard_map/reduce_scatter | solution.py:140
  384.2 2.0 dynamic-slice_add_fusion
  386.2 0.1 bitcast_convert_fusion
  386.4 2.2 pad_maximum_fusion
  (31 shorter events, 0.3 us)
Async XLA Ops:
  6.5 52.1 %all-gather.7.cloned.1.call-start = ((), (), s32[]{:S(2)}) async-start(), calls=%async_computation.3 | async-start | bytes 7372800 | tf_op jit(solution)/shard_map/all_gather | solution.py:74
  7.3 99.9 %all-gather.9.cloned.1.call-start = ((), (), s32[]{:S(2)}) async-start(), calls=%async_computation.4 | async-start | bytes 7372800 | tf_op jit(solution)/shard_map/all_gather | solution.py:75
  8.0 156.2 %all-gather.5.cloned.1.call-start = ((), (), s32[]{:S(2)}) async-start(), calls=%async_computation.2 | async-start | bytes 7372800 | tf_op jit(solution)/shard_map/all_gather | solution.py:76
  8.7 211.6 %all-gather.11.cloned.1.call-start = ((), (), s32[]{:S(2)}) async-start(), calls=%async_computation.5 | async-start | bytes 7372800 | tf_op jit(solution)/shard_map/all_gather | solution.py:128
  9.3 299.7 %reduce-scatter.3.cloned.1.call-start = ((), (), s32[]{:S(2)}) async-start(), calls=%async_computation.6 | async-start | bytes 4915200 | tf_op jit(solution)/shard_map/reduce_scatter | solution.py:135
  12.9 7.8 %slice-start = ((s8[7864320]{0:T(1024)(128)(4,1)}), s8[4194304]{0:T(1024)(128)(4,1)S(1)}, s32[]{:S(2)}) async-start(s8[7864320]{0:T(1024)(128)(4,1)} %bitcast.59), calls=%async_computation.8 | async-start | bytes 8388608
  12.9 8.4 %slice-start.1 = ((s8[7864320]{0:T(1024)(128)(4,1)}), s8[3670016]{0:T(1024)(128)(4,1)S(1)}, s32[]{:S(2)}) async-start(s8[7864320]{0:T(1024)(128)(4,1)} %bitcast.59), calls=%async_computation.9 | async-start | bytes 7340032
  21.3 6.4 %copy-start.4 = (s32[2,2]{1,0:T(2,128)S(1)}, s32[2,2]{1,0:T(2,128)}, u32[]{:S(2)}) copy-start(s32[2,2]{1,0:T(2,128)} %param.14) | copy-start | bytes 52
  69.1 60.6 %copy-start.2 = (f32[640]{0:T(1024)S(1)}, f32[640]{0:T(1024)}, u32[]{:S(2)}) copy-start(f32[640]{0:T(1024)} %param.21) | copy-start | bytes 7684
  130.0 45.5 %copy-start = (bf16[768,640]{1,0:T(8,128)(2,1)}, bf16[768,640]{1,0:T(8,128)(2,1)S(1)}, u32[]{:S(2)}) copy-start(bf16[768,640]{1,0:T(8,128)(2,1)S(1)} %fusion.21) | copy-start | bytes 2949124
  130.0 48.8 %copy-start.3 = (f32[640]{0:T(1024)S(1)}, f32[640]{0:T(1024)}, u32[]{:S(2)}) copy-start(f32[640]{0:T(1024)} %param.20) | copy-start | bytes 7684
  130.0 50.3 %collective-permute-start.1 = (bf16[768,640]{1,0:T(8,128)(2,1)S(1)}, bf16[768,640]{1,0:T(8,128)(2,1)}, u32[]{:S(2)}, u32[]{:S(2)}) collective-permute-start(bf16[768,640]{1,0:T(8,128)(2,1)S(1)} %fusion.21), channel_id=1, source_target_pairs={{0,4},{4,8},{8,12},{12,16},{16,20},{20,24},{24,28},{1,5},{5,9},{9,... | collective-permute-start | bytes 2949128 | tf_op jit(solution)/shard_map/ppermute | solution.py:12
  175.5 15.8 %collective-permute-start = (bf16[768,640]{1,0:T(8,128)(2,1)}, bf16[768,640]{1,0:T(8,128)(2,1)}, u32[]{:S(2)}, u32[]{:S(2)}) collective-permute-start(bf16[768,640]{1,0:T(8,128)(2,1)} %convolution_convert_fusion.3), channel_id=1, source_target_pairs={{0,4},{4,8},{8,12},{12,16},{16,20},{20,24},{24,28},{1,5},{5,9},{9,... | collective-permute-start | bytes 2949128 | tf_op jit(solution)/shard_map/ppermute | solution.py:12
  196.8 14.6 %copy-start.1 = (bf16[1152,640]{0,1:T(8,128)(2,1)S(1)}, bf16[1152,640]{0,1:T(8,128)(2,1)}, u32[]{:S(2)}) copy-start(bf16[1152,640]{0,1:T(8,128)(2,1)} %copy.20) | copy-start | bytes 4423684
  233.8 150.4 %reduce-scatter.5.cloned.1.call-start = ((), (), s32[]{:S(2)}) async-start(), calls=%async_computation.7 | async-start | bytes 4915200 | tf_op jit(solution)/shard_map/reduce_scatter | solution.py:140
  311.0 75.2 %collective-permute-start.2 = (bf16[384,1280]{1,0:T(8,128)(2,1)S(1)}, bf16[384,1280]{1,0:T(8,128)(2,1)S(1)}, u32[]{:S(2)}, u32[]{:S(2)}) collective-permute-start(bf16[384,1280]{1,0:T(8,128)(2,1)S(1)} %fusion.23), channel_id=1, source_target_pairs={{0,4},{4,8},{8,12},{12,16},{16,20},{20,24},{24,28},{28,0},{1,5},{5... | collective-permute-start | bytes 2949128 | tf_op jit(solution)/shard_map/ppermute | solution.py:18
Sparse Core Ops, SparseCore 0:
  9.2 49.3 all-gather.6
  60.5 46.6 all-gather.8
  109.0 55.1 all-gather.4
  166.0 46.5 all-gather.10
  233.9 75.0 reduce-scatter.2
  311.2 73.0 reduce-scatter.4
where the time goes:
time: 396 us; the launch traced here: 395 us
  waiting for transfers between devices  235 us (59%)
  matrix products  68 us (17%)
  other arithmetic  41.8 us (11%)
  local copies, waits for them, and re-layouts  19 us (5%)
  between operations  13.7 us (3%)
  blocking collectives  11.8 us (3%)
  starting transfers between devices  5.8 us (1%)
    reduce_scatter x1, waiting for transfers between devices, shards(): lax.psum_scatter(partial_spans[nchunk - 1].astype(jnp.bfloat16), 'head',...  74.5 us
    reduce_scatter x1, waiting for transfers between devices, shards(): lax.psum_scatter(partial_spans[:nchunk - 1].astype(jnp.bfloat16), 'head',...  73.1 us
    all_gather x1, waiting for transfers between devices, shards(): lax.all_gather(w_key, 'queue', axis=0, tiled=True)  38.1 us
    dot_general x3, matrix products, shards(): jnp.dot(flat_rows, piece_rows, preferred_element_type=jnp.float32)  32.3 us
    all_gather x1, waiting for transfers between devices, shards(): lax.all_gather(w_value, 'queue', axis=0, tiled=True)  31.9 us
    convert_element_type x1, other arithmetic, shards(): normed = (layer_norm(hidden) * (1.0 + level_mods[:, 1][:, None, :]) + lev...  16.1 us
    sub x1, matrix products, shards(): expo = jnp.exp(scores - top)  14.6 us
    all_gather x1, waiting for transfers between devices, shards(): lax.all_gather(w_query, 'queue', axis=0, tiled=True)  14.5 us
  transfers between devices with their start and end apart: 9, of which 5 were waited for; matrix products, arithmetic and copies ran while one was open for 28% of the time, Pallas kernels for 0%

commit v1 on v0

v1 whole, which is shorter than its diff:
```python
import functools
import math

import jax
import jax.numpy as jnp
from jax import lax
from jax.experimental import pallas as pl
from jax.experimental.pallas import tpu as pltpu
from jax.sharding import PartitionSpec as P

HD = 128
F32 = jnp.float32
BF16 = jnp.bfloat16
VMEM_BYTES = 60 * 1024 * 1024
WEIGHT = 16


def params():
    return pltpu.CompilerParams(vmem_limit_bytes=VMEM_BYTES)


def cost(flops, bytes_accessed, transcendentals=0):
    return pl.CostEstimate(
        flops=flops // WEIGHT,
        bytes_accessed=bytes_accessed // WEIGHT,
        transcendentals=transcendentals // WEIGHT,
    )


def from_behind(value, axis, by):
    peers = lax.axis_size(axis)
    pairs = [(i, i + by) for i in range(peers) if 0 <= i + by < peers]
    return lax.ppermute(value, axis, pairs)


def shifted(value, axis, steps):
    count = lax.axis_size(axis)
    pairs = [(source, (source + steps) % count) for source in range(count)]
    return lax.ppermute(value, axis, pairs)


def after(value, *others):
    return lax.optimization_barrier((value, *others))[0]


def sum_terms(value, axis):
    count = lax.axis_size(axis)
    if count & (count - 1):
        return [value] + [shifted(value, axis, steps) for steps in range(1, count)]
    terms, bit = [value], 1
    while bit < count:
        total = functools.reduce(jnp.add, terms)
        terms = [total, lax.ppermute(total, axis, [(i, i ^ bit) for i in range(count)])]
        bit *= 2
    return terms


def is_cube(row_count, col_count):
    return lax.axis_size("queue") == 2**3 and row_count % 32 == 0 and col_count % HD == 0


def exchange(value, bit):
    peers = lax.axis_size("queue")
    return lax.ppermute(value, "queue", [(i, i ^ bit) for i in range(peers)])


def first_step(block):
    return {0: block, 1: exchange(block, 1), 2: exchange(block, 2), 4: exchange(block, 4)}


def second_step(first):
    return {**first, 3: exchange(first[2], 1), 5: exchange(first[4], 1)}


def halves(block):
    half = block.shape[0] // 2
    return block[:half], block[half:]


def norm_kernel(levels_ref, latents_ref, control_ref, mod_ref, out_ref):
    blocks, _, width = out_ref.shape
    hidden = latents_ref[0].astype(F32) + control_ref[0].astype(F32)
    center = hidden - jnp.mean(hidden, axis=-1, keepdims=True)
    variance = jnp.mean(center * center, axis=-1, keepdims=True)
    normed = center * lax.rsqrt(variance + 1e-06)
    row = lax.rem(levels_ref[pl.program_id(0)], 8)
    normed = normed * (1.0 + mod_ref[1, pl.ds(row, 1), :]) + mod_ref[0, pl.ds(row, 1), :]
    normed = normed.astype(BF16)
    for j in range(blocks):
        out_ref[j] = normed[:, j * width : (j + 1) * width]


def modulated_norm(latents, control, levels, modulation, blocks):
    spans, rows, model = latents.shape
    tile = 128 if rows % 128 == 0 else rows
    tiles = rows // tile
    width = model // blocks
    return pl.pallas_call(
        norm_kernel,
        grid_spec=pltpu.PrefetchScalarGridSpec(
            num_scalar_prefetch=1,
            grid=(spans, tiles),
            in_specs=[
                pl.BlockSpec((1, tile, model), lambda s, t, lev: (s, t, 0)),
                pl.BlockSpec((1, tile, model), lambda s, t, lev: (s, t, 0)),
                pl.BlockSpec((2, 8, model), lambda s, t, lev: (0, lev[s] // 8, 0)),
            ],
            out_specs=pl.BlockSpec((blocks, tile, width), lambda s, t, lev: (0, s * tiles + t, 0)),
        ),
        out_shape=jax.ShapeDtypeStruct((blocks, spans * rows, width), BF16),
        compiler_params=params(),
        cost_estimate=cost(
            flops=10 * latents.size, bytes_accessed=6 * latents.size, transcendentals=0
        ),
        name="modulated_norm",
    )(levels, latents, control, modulation)


def project_kernel(layout, begun, groups, spans, *refs):
    refs = list(refs)
    index_ref = refs.pop(0)
    normed_ref = refs.pop(0)
    count = 1 + max(piece[0] for block in layout for piece in block)
    weight_refs = [refs.pop(0) for _ in range(count)]
    begun_ref = refs.pop(0) if begun else None
    *out_refs, rows_buf, weight_buf, row_sems, weight_sems = refs
    if begun:
        *out_refs, begun_buf, begun_sem = out_refs
    width = normed_ref.shape[2]

    def copies_of(b):
        copies = [
            pltpu.make_async_copy(
                normed_ref.at[index_ref[b]],
                rows_buf.at[:, pl.ds(b * width, width)],
                row_sems.at[b],
            )
        ]
        for p, (operand, first, high, row, col) in enumerate(layout[b]):
            source = weight_refs[operand]
            target = weight_buf.at[pl.ds(b * width + row, high), pl.ds(col, source.shape[1])]
            copies.append(
                pltpu.make_async_copy(source.at[pl.ds(first, high)], target, weight_sems.at[b, p])
            )
        return copies

    pairs = [range(b, min(b + 2, len(layout))) for b in range(0, len(layout), 2)]
    copies = [sum((copies_of(b) for b in pair), []) for pair in pairs]
    for ahead in copies[:2]:
        for copy in ahead:
            copy.start()
    if begun:
        fetch_begun = pltpu.make_async_copy(begun_ref, begun_buf, begun_sem)
        fetch_begun.start()
    total = None
    for i, pair in enumerate(pairs):
        for copy in copies[i]:
            copy.wait()
        if i + 2 < len(pairs):
            for copy in copies[i + 2]:
                copy.start()
        span = slice(pair[0] * width, (pair[-1] + 1) * width)
        term = jnp.dot(rows_buf[:, span], weight_buf[span], preferred_element_type=F32)
        total = term if total is None else total + term
    if begun:
        fetch_begun.wait()
        total = total + begun_buf[...]
    if not spans:
        out_refs[0][...] = total
        return
    *out_refs, square_ref = out_refs
    column = 0
    for n, group_count in enumerate(groups):
        outs = out_refs[n * spans : (n + 1) * spans]
        _, span_rows, cols = outs[0].shape
        for g in range(group_count):
            rounded = total[:, column : column + cols].astype(BF16)
            column += cols
            for i, out_ref in enumerate(outs):
                out_ref[g] = rounded[i * span_rows : (i + 1) * span_rows]
        floats = rounded.astype(F32)
        squares = jnp.sum(floats * floats, axis=-1, keepdims=True)
        for t in range(squares.shape[0] // HD):
            tile = jnp.broadcast_to(squares[t * HD : (t + 1) * HD], (HD, HD))
            square_ref[n, t : t + 1, :] = tile.T[0:1, :]


def project(normed, weights, layout, indices, groups, begun=None, spans=0):
    _, rows, width = normed.shape
    local = weights[0].shape[-1]
    cols = sum(groups) * local
    anywhere = pl.BlockSpec(memory_space=pl.ANY)
    in_vmem = pl.BlockSpec(memory_space=pltpu.VMEM)
    if spans:
        out_shape = [
            jax.ShapeDtypeStruct((count, rows // spans, local), BF16)
            for count in groups
            for _ in range(spans)
        ]
        out_shape.append(jax.ShapeDtypeStruct((len(groups), rows // HD, HD), F32))
    else:
        out_shape = [jax.ShapeDtypeStruct((rows, cols), F32)]
    result = pl.pallas_call(
        functools.partial(project_kernel, layout, begun is not None, groups, spans),
        in_specs=[pl.BlockSpec(memory_space=pltpu.SMEM)]
        + [anywhere] * (1 + len(weights) + (begun is not None)),
        out_specs=[in_vmem] * len(out_shape),
        out_shape=out_shape,
        scratch_shapes=(
            [pltpu.VMEM((rows, cols), F32), pltpu.SemaphoreType.DMA] if begun is not None else []
        )
        + [
            pltpu.VMEM((rows, len(layout) * width), BF16),
            pltpu.VMEM((len(layout) * width, cols), BF16),
            pltpu.SemaphoreType.DMA((len(layout),)),
            pltpu.SemaphoreType.DMA((len(layout), max(len(block) for block in layout))),
        ],
        compiler_params=params(),
        cost_estimate=cost(
            flops=2 * len(layout) * rows * width * cols,
            bytes_accessed=2 * len(layout) * (rows + cols) * width + 4 * rows * cols,
        ),
        name="project_final" if spans else "project_begin",
    )(indices, normed, *weights, *([begun] if begun is not None else []))
    if not spans:
        return result[0]
    sets = [result[n * spans : (n + 1) * spans] for n in range(len(groups))]
    return (*sets, result[-1])


def attention_kernel(
    total_width, span, places, seen_ref, q_ref, q_gain_ref, k_gain_ref, k0, k1, k2, v0, v1, v2, *refs
):
    *square_refs, out_ref, factors = refs
    tiles = q_ref.shape[0] // HD

    @pl.when(pl.program_id(0) == 0)
    def _():
        for f, (array, first) in enumerate(places):
            for t in range(tiles):
                row = sum(ref[array, first + t : first + t + 1, :] for ref in square_refs)
                squares = jnp.broadcast_to(row, (HD, HD)).T[:, 0:1]
                factors[f, t * HD : (t + 1) * HD] = lax.rsqrt(squares / total_width + 1e-06)

    def with_gain(values, factor, gain_ref):
        return (values.astype(F32) * factor * gain_ref[...]).astype(BF16)

    to_exponent = HD ** (-0.5) * math.log2(math.e)
    query = with_gain(q_ref[...], factors[0], q_gain_ref)
    scores = [
        lax.dot_general(
            query,
            with_gain(key[...], factors[1 + w], k_gain_ref),
            (((1,), (1,)), ((), ())),
            preferred_element_type=F32,
        )
        for w, key in enumerate((k0, k1, k2))
    ]
    tops = [jnp.max(s, axis=-1, keepdims=True) for s in scores]
    hide = [jnp.where(seen_ref[span, w] == 1, 0.0, 1e30).astype(F32) for w in range(2)] + [0.0]
    top = functools.reduce(jnp.maximum, (m - h for m, h in zip(tops, hide)))
    expos = [jnp.exp2(s * to_exponent - (top * to_exponent + h)) for s, h in zip(scores, hide)]
    inverse = 1.0 / jnp.sum(expos[0] + expos[1] + expos[2], axis=-1, keepdims=True)
    total = None
    for expo, value in zip(expos, (v0, v1, v2)):
        probs = (expo * inverse).astype(BF16)
        term = jnp.dot(probs, value[...], preferred_element_type=F32)
        total = term if total is None else total + term
    out_ref[...] = total.astype(BF16)


def attend(span, seen, query, squares, gains, prior, own, total_width):
    spans = len(own)
    _, rows, cols = query.shape
    heads = cols // HD
    tiles = rows // HD
    window = [(spans + span - 2 + w) for w in range(3)]
    window = [(0 if position >= spans else 2, position % spans) for position in window]
    places = [(1, span * tiles)] + [(array, index * tiles) for array, index in window]
    arrays = [(own if array == 0 else prior)[index] for array, index in window]

    def part(which):
        return pl.BlockSpec((None, rows, HD), lambda h: (which, 0, h))

    gain_spec = pl.BlockSpec((1, HD), lambda h: (0, h))
    return pl.pallas_call(
        functools.partial(attention_kernel, total_width, span, places),
        grid=(heads,),
        in_specs=[pl.BlockSpec(memory_space=pltpu.SMEM), part(0), gain_spec, gain_spec]
        + [part(1)] * 3
        + [part(0)] * 3
        + [pl.BlockSpec(memory_space=pltpu.VMEM)] * len(squares),
        out_specs=pl.BlockSpec((rows, HD), lambda h: (0, h)),
        out_shape=jax.ShapeDtypeStruct((rows, cols), BF16),
        scratch_shapes=[pltpu.VMEM((4, rows, 1), F32)],
        compiler_params=params(),
        cost_estimate=cost(
            flops=12 * rows * rows * cols,
            bytes_accessed=16 * rows * cols,
            transcendentals=3 * rows * rows * heads,
        ),
        name="attend",
    )(seen, query, *gains, *arrays, *arrays, *squares)


def along_line(value, axis):
    count = lax.axis_size(axis)

    def move(moved, by, least):
        pairs = [(i, i + by) for i in range(count) if 0 <= i + by < count]
        if least:
            pairs = [(i, j) for i, j in pairs if 0 <= i - by < count]
        return lax.ppermute(moved, axis, pairs)

    below = {1: move(value, 1, 0)}
    above = {1: move(value, -1, 0)}
    for k in range(3, count):
        pairs = [(i, i + s * k) for i in range(count) for s in (1, -1) if 0 <= i + s * k < count]
        if 2 * k >= count and count < 2 * k + 1 and len({j for _, j in pairs}) == len(pairs):
            below[k] = above[k] = lax.ppermute(value, axis, pairs)
        else:
            below[k] = move(value, k, 0)
            above[k] = move(value, -k, 0)
    if count > 2:
        below[2] = move(below[1], 1, 1)
        above[2] = move(above[1], -1, 1)
    return [value] + [below[k] for k in range(1, count)] + [above[k] for k in range(1, count)]


def late_slots(groups):
    return sorted({2, groups - 2}) if groups > 2 else []


class Fetch:
    def __init__(self, place_ref, span, line, weight_ref, scratch):
        self.attended, self.weights, self.sems = scratch[:3]
        self.groups = weight_ref.shape[0]
        self.mine, self.span, self.place_ref = place_ref[0], span, place_ref
        self.line, self.weight_ref, self.columns_scratch = line, weight_ref, scratch[3:]

    def slot(self, i, source):
        return pltpu.make_async_copy(source, self.attended.at[i], self.sems.at[0, i])

    def start_attended(self, slots):
        below, above = self.line[1 : self.groups], self.line[self.groups :]
        for i, k in enumerate(slots):
            if k == 0:
                self.slot(i, self.line[0]).start()
                continue

            @pl.when(self.mine >= k)
            def _():
                self.slot(i, below[k - 1]).start()

            @pl.when(self.mine < k)
            def _():
                self.slot(i, above[self.groups - k - 1]).start()

    def weight(self, i, k):
        group = lax.rem(self.mine + self.groups - k, self.groups)
        return pltpu.make_async_copy(
            self.weight_ref.at[group], self.weights.at[i], self.sems.at[1, i]
        )

    def start_weights(self, slots):
        for i, k in enumerate(slots):
            self.weight(i, k).start()

    def columns(self, latents_ref, control_ref, mod_ref):
        latents, control, mods = self.columns_scratch
        width = latents.shape[1]
        columns = pl.ds(pl.multiple_of(self.mine * width, HD), width)
        rows = pl.ds(pl.multiple_of(self.place_ref[1 + self.span] // 8 * 8, 8), 8)
        sources = (
            latents_ref.at[self.span, :, columns],
            control_ref.at[self.span, :, columns],
            mod_ref.at[2, rows, columns],
        )
        return [
            pltpu.make_async_copy(source, target, self.sems.at[2, i])
            for i, (source, target) in enumerate(zip(sources, (latents, control, mods)))
        ]

    def branch(self, slots, new_weights, total=None):
        for i, k in enumerate(slots):
            self.slot(i, self.line[0]).wait()

            @pl.when(new_weights)
            def _():
                self.weight(i, k).wait()

            part = jnp.dot(self.attended[i], self.weights[i], preferred_element_type=F32)
            part = part.astype(BF16).astype(F32)
            total = part if total is None else total + part
        return total

    def updated(self, branch, columns):
        latents, control, mods = self.columns_scratch
        for copy in columns:
            copy.wait()
        hidden = latents[...].astype(F32) + control[...].astype(F32)
        return hidden + mods[pl.ds(lax.rem(self.place_ref[1 + self.span], 8), 1), :] * branch


def start_all(copies):
    for copy in copies:
        copy.start()


def last_kernel(span, place_ref, weight_ref, latents_ref, control_ref, mod_ref, *refs):
    line, out_ref, scratch = refs[:-7], refs[-7], refs[-6:]
    fetch = Fetch(place_ref, span, line, weight_ref, scratch)
    slots = range(weight_ref.shape[0])
    columns = fetch.columns(latents_ref, control_ref, mod_ref)
    fetch.start_attended(slots)
    fetch.start_weights(slots)
    start_all(columns)
    out_ref[...] = fetch.updated(fetch.branch(slots, True), columns).astype(BF16)


def begin_kernel(slots, place_ref, weight_ref, *refs):
    line, out_ref, scratch = refs[:-4], refs[-4], refs[-3:]
    span = pl.program_id(0)
    rows = out_ref.shape[1]
    mine = [ref.at[pl.ds(pl.multiple_of(span * rows, rows), rows)] for ref in line]
    fetch = Fetch(place_ref, span, mine, weight_ref, scratch)
    fetch.start_attended(slots)

    @pl.when(span == 0)
    def _():
        fetch.start_weights(slots)

    out_ref[0] = fetch.branch(slots, span == 0)


def rest_kernel(
    slots, place_ref, arrived_ref, begun_ref, weight_ref, latents_ref, control_ref, mod_ref, *refs
):
    line, out_ref, scratch = refs[:-7], refs[-7], refs[-6:]
    step = pl.program_id(0)
    rows = out_ref.shape[1]

    def of_span(span):
        mine = [ref.at[pl.ds(pl.multiple_of(span * rows, rows), rows)] for ref in line]
        fetch = Fetch(place_ref, span, mine, weight_ref, scratch)
        return fetch, fetch.columns(latents_ref, control_ref, mod_ref)

    @pl.when(step == 0)
    def _():
        fetch, columns = of_span(0)
        fetch.start_attended(slots)
        fetch.start_weights(slots)
        start_all(columns)
        out_ref[0] = arrived_ref[...].astype(F32)

    @pl.when(step > 0)
    def _():
        fetch, columns = of_span(step - 1)

        @pl.when(step > 1)
        def _():
            fetch.start_attended(slots)
            start_all(columns)

        branch = fetch.branch(slots, step == 1, begun_ref[0])
        out_ref[0] = fetch.updated(branch, columns)


def update_scratch(slots, rows, cols, width, columns=True):
    scratch = [
        pltpu.VMEM((len(slots), rows, cols), BF16),
        pltpu.VMEM((len(slots), cols, width), BF16),
        pltpu.SemaphoreType.DMA((3, max(len(slots), 3))),
    ]
    if columns:
        scratch.append(pltpu.VMEM((rows, width), BF16))
        scratch.append(pltpu.VMEM((rows, width), BF16))
        scratch.append(pltpu.VMEM((8, width), F32))
    return scratch


def update_cost(slots, rows, cols, width):
    return cost(
        flops=2 * slots * rows * cols * width,
        bytes_accessed=2 * slots * cols * (rows + width) + 8 * rows * width,
    )


def update_last(place, line, weights, latents, control, modulation):
    rows, cols = line[0].shape
    groups, _, width = weights.shape
    span = latents.shape[0] - 1
    anywhere = pl.BlockSpec(memory_space=pl.ANY)
    return pl.pallas_call(
        functools.partial(last_kernel, span),
        in_specs=[pl.BlockSpec(memory_space=pltpu.SMEM)] + [anywhere] * (4 + len(line)),
        out_specs=pl.BlockSpec(memory_space=pltpu.VMEM),
        scratch_shapes=update_scratch(range(groups), rows, cols, width),
        out_shape=jax.ShapeDtypeStruct((rows, width), BF16),
        compiler_params=params(),
        cost_estimate=update_cost(groups, rows, cols, width),
        name="update_last",
    )(place, weights, latents, control, modulation, *line)


def update_begin(place, line, weights, spans, rows, slots):
    cols = line[0].shape[1]
    width = weights.shape[2]
    anywhere = pl.BlockSpec(memory_space=pl.ANY)
    return pl.pallas_call(
        functools.partial(begin_kernel, slots),
        grid=(spans - 1,),
        in_specs=[pl.BlockSpec(memory_space=pltpu.SMEM)] + [anywhere] * (1 + len(line)),
        out_specs=pl.BlockSpec((1, rows, width), lambda i: (i, 0, 0)),
        scratch_shapes=update_scratch(slots, rows, cols, width, columns=False),
        out_shape=jax.ShapeDtypeStruct((spans - 1, rows, width), F32),
        compiler_params=params(),
        cost_estimate=update_cost(len(slots) * (spans - 1), rows, cols, width),
        name="update_begin",
    )(place, weights, *line)


def update_rest(place, arrived, line, weights, latents, control, modulation):
    cols = line[0].shape[1]
    spans, rows, _ = latents.shape
    groups, _, width = weights.shape
    late = late_slots(groups) or [groups - 1]
    early = [k for k in range(groups) if k not in late]
    ready = list(line)
    for k in late:
        ready[k] = ready[groups - 1 + k] = line[0]
    begun = update_begin(place, ready, weights, spans, rows, early)
    anywhere = pl.BlockSpec(memory_space=pl.ANY)
    return pl.pallas_call(
        functools.partial(rest_kernel, late),
        grid=(spans,),
        in_specs=[
            pl.BlockSpec(memory_space=pltpu.SMEM),
            pl.BlockSpec((rows, width), lambda i: (0, 0)),
            pl.BlockSpec((1, rows, width), lambda i: (jnp.maximum(i - 1, 0), 0, 0)),
        ]
        + [anywhere] * (4 + len(line)),
        out_specs=pl.BlockSpec((1, rows, width), lambda i: (i, 0, 0)),
        scratch_shapes=update_scratch(late, rows, cols, width),
        out_shape=jax.ShapeDtypeStruct((spans, rows, width), F32),
        compiler_params=params(),
        cost_estimate=update_cost(len(late) * (spans - 1), rows, cols, width),
        name="update_rest",
    )(place, arrived, begun, weights, latents, control, modulation, *line)


def out_shares(w_out):
    owners = lax.axis_size("queue")
    rows, cols = w_out.shape
    return lax.all_to_all(w_out.reshape(owners, rows // owners, cols), "queue", 0, 0, tiled=True)


def out_blocks(shares):
    groups = lax.axis_size("head")
    owners, part, cols = shares.shape
    blocks = lax.all_to_all(shares, "head", 0, 0, tiled=True)
    return blocks.reshape(groups, owners // groups, part, cols)


def assemble_kernel(index_ref, *refs):
    *stacks, out_ref, sems = refs
    count, groups, sharers, part, cols = stacks[0].shape
    copies = []
    for i, stack in enumerate(stacks):
        for b in range(count):
            start = pl.multiple_of(index_ref[i * count + b] * part, part)
            for g in range(groups):
                for o in range(sharers):
                    copy = pltpu.make_async_copy(
                        stack.at[b, g, o],
                        out_ref.at[g, pl.ds(start, part), pl.ds(o * cols, cols)],
                        sems.at[i * count + b, g, o],
                    )
                    copy.start()
                    copies.append(copy)
    for copy in copies:
        copy.wait()


def assemble(stacks, indices):
    count, groups, sharers, part, cols = stacks[0].shape
    blocks = count * len(stacks)
    return pl.pallas_call(
        assemble_kernel,
        in_specs=[pl.BlockSpec(memory_space=pltpu.SMEM)]
        + [pl.BlockSpec(memory_space=pl.ANY)] * len(stacks),
        out_specs=pl.BlockSpec(memory_space=pltpu.VMEM),
        out_shape=jax.ShapeDtypeStruct((groups, blocks * part, sharers * cols), BF16),
        scratch_shapes=[pltpu.SemaphoreType.DMA((blocks, groups, sharers))],
        compiler_params=params(),
        cost_estimate=cost(flops=0, bytes_accessed=4 * stacks[0].size * len(stacks)),
        name="assemble",
    )(jnp.stack(indices), *stacks)


def assemble_in_order(gathered):
    owners, groups, sharers, part, cols = gathered.shape
    shape = (groups, owners * part, sharers * cols)
    return gathered.transpose(1, 0, 3, 2, 4).reshape(shape)


def shards(
    latents,
    control,
    levels,
    window_mask,
    modulation,
    w_query,
    w_key,
    w_value,
    w_out,
    q_gain,
    k_gain,
):
    spans, row_count, _ = latents.shape
    local_cols = w_query.shape[1]
    owners = lax.axis_size("queue")
    total_width = local_cols * lax.axis_size("head")
    owner_index = lax.axis_index("queue")
    head_index = lax.axis_index("head")
    place = jnp.concatenate([head_index.astype(jnp.int32).reshape(1), levels])
    modulation = modulation.transpose(1, 0, 2)
    gain_rows = [gain.reshape(1, -1) for gain in (q_gain, k_gain)]
    cube = is_cube(w_query.shape[0], local_cols) and w_out.shape[0] // owners % 16 == 0
    span_ids = owner_index * spans + jnp.arange(spans, dtype=jnp.int32)
    seen = (
        (window_mask == 1) & (span_ids[:, None] >= jnp.array([2, 1], jnp.int32)[None, :])
    ).astype(jnp.int32)

    if cube:
        mine = owner_index.astype(jnp.int32)
        high = w_query.shape[0]

        def indices(masks):
            return jnp.stack([mine ^ m for m in masks])

        halves_of = halves(w_query)
        sides = (jnp.concatenate([w_value, halves_of[0]]), jnp.concatenate([halves_of[1], w_key]))
        firsts = [first_step(side) for side in sides]
        early, late = [0, 1, 2, 4, 3, 5], [6, 7]
        early_indices, late_indices = indices(early), indices(late)
        small = (seen, place, early_indices, late_indices, *gain_rows)
        normed = modulated_norm(after(latents, *small), control, levels, modulation, owners)
        share = out_shares(after(w_out, normed, firsts[0][4], firsts[1][2]))
        across = [
            exchange(after(firsts[0][4], normed, share), 2),
            exchange(after(firsts[1][2], normed, share), 4),
        ]
        firsts[0][2] = after(firsts[0][2], normed, share)
        firsts[1][4] = after(firsts[1][4], normed, share)
        firsts = [second_step(first) for first in firsts]
        columns = {"value": 0, "key": local_cols, "query": 2 * local_cols}
        half = high // 2

        def layout_of(count):
            return tuple(
                (
                    (2 * b, 0, high, 0, columns["value"]),
                    (2 * b, high, half, 0, columns["query"]),
                    (2 * b + 1, 0, half, half, columns["query"]),
                    (2 * b + 1, half, high, 0, columns["key"]),
                )
                for b in range(count)
            )

        parts = [first[m] for m in early for first in firsts]
        begun = project(normed, parts, layout_of(len(early)), early_indices, (3,))
        across = [after(part, begun) for part in across]
        parts = across + [exchange(part, 1) for part in across]
        own, query, squares = project(
            normed,
            parts,
            layout_of(len(late)),
            late_indices,
            (2, 1),
            begun=begun,
            spans=spans,
        )
    else:
        normed = modulated_norm(latents, control, levels, modulation, 1)
        weights = [
            lax.all_gather(w, "queue", axis=0, tiled=True) for w in (w_value, w_key, w_query)
        ]
        model = weights[0].shape[0]
        layout = (tuple((w, 0, model, 0, w * local_cols) for w in range(3)),)
        zero = jnp.zeros((1,), jnp.int32)
        own, query, squares = project(normed, weights, layout, zero, (2, 1), spans=spans)
        share = out_shares(w_out)

    prior = [from_behind(span, "queue", 1) for span in reversed(own)][::-1]
    prior_squares = from_behind(squares, "queue", 1)
    share = out_blocks(after(share, prior_squares)) if cube else out_blocks(share)
    squares = sum_terms(jnp.concatenate([squares, prior_squares]), "head")

    def attended_of(span, ready):
        return attend(span, seen, ready, squares, gain_rows, prior, own, total_width)

    groups = lax.axis_size("head")
    attended_last = attended_of(spans - 1, query[-1])
    last = along_line(attended_last, "head")
    sent = [last[1], last[groups]]
    begin_rest = [attended_last, *sent]
    if cube:
        share = after(share, *squares)
        first = {m: exchange(share, m) for m in (2, 4)}
    rest = [attended_of(span, after(query[span], *begin_rest)) for span in range(spans - 1)]
    rest = rest[0] if len(rest) == 1 else jnp.concatenate(rest, axis=0)
    line = along_line(rest, "head")
    if cube:
        first = {m: after(block, rest, *prior) for m, block in first.items()}
        half = share.shape[0] // 2
        across = [exchange(first[4][:half], 2), exchange(first[2][half:], 4)]
        across = jnp.concatenate([after(part, *last[1:]) for part in across])
        mine_blocks = jnp.stack([share, first[2], first[4], across])
        swapped = exchange(mine_blocks, 1)
        weights = assemble(
            [mine_blocks, swapped], [mine ^ m ^ c for c in range(2) for m in (0, 2, 4, 6)]
        )
    else:
        weights = assemble_in_order(lax.all_gather(share, "queue", axis=0))
    rest = line
    updated_last = update_last(place, last, weights, latents, control, modulation)
    arrived = shifted(updated_last, "queue", 1)
    return update_rest(place, arrived, rest, weights, latents, control, modulation)


def solution(mesh):
    placed = (
        P("queue", None, None),
        P("queue", None, None),
        P("queue"),
        P("queue", None),
        P(),
        P("queue", "head"),
        P("queue", "head"),
        P("queue", "head"),
        P("head", "queue"),
        P("head"),
        P("head"),
    )
    return jax.shard_map(
        shards, mesh=mesh, in_specs=placed, out_specs=P("queue", None, "head"), check_vma=False
    )
```

time: 396 us -> 258 us (0.65)
  waiting for transfers between devices: 235 us -> 85.3 us
  Pallas kernels: 0 us -> 91.6 us
  matrix products: 68 us -> 0 us
  starting transfers between devices: 5.8 us -> 64.7 us
  other arithmetic: 41.8 us -> 3.78 us
  between operations: 13.7 us -> 0.66 us
  blocking collectives: 11.8 us -> 0 us
  local copies, waits for them, and re-layouts: 19 us -> 10.4 us
    reduce_scatter x2 -> x0, waiting for transfers between devices: 148 us -> none  [the longest x1 74.5 us: shards(): lax.psum_scatter(partial_spans[nchunk - 1].astype(jnp.bfloat16), 'head',...]
    pallas_call x0 -> x9, Pallas kernels: none -> 91.6 us  [the longest x2 31.5 us: project(): pl.pallas_call(functools.partial(project_kernel, layout, begun is not Non...]
    all_gather x4 -> x0, waiting for transfers between devices: 84.5 us -> none  [the longest x1 38.1 us: shards(): lax.all_gather(w_key, 'queue', axis=0, tiled=True)]
    ppermute x0 -> x31, waiting for transfers between devices: none -> 74.3 us  [the longest x19 42.9 us: exchange(): return lax.ppermute(value, 'queue', [(i, i ^ bit) for i in range(peers)])]
    dot_general x6 -> x0, matrix products: 53.5 us -> none  [the longest x3 32.3 us: shards(): jnp.dot(flat_rows, piece_rows, preferred_element_type=jnp.float32)]
    ppermute x0 -> x31, starting transfers between devices: none -> 45.3 us  [the longest x8 13.5 us: move(): return lax.ppermute(moved, axis, pairs)]
    convert_element_type x4 -> x1, other arithmetic: 18.7 us -> 0.6 us  [shards(): seen = ((window_mask == 1) & (span_ids[:, None] >= jnp.array([2, 1], jnp....]
    sub x1 -> x0, matrix products: 14.6 us -> none  [shards(): expo = jnp.exp(scores - top)]
  transfers between devices with their start and end apart: 9 -> 37, of which waited for: 5 -> 20; matrix products, arithmetic and copies ran while one was open for 28% -> 3% of each run, Pallas kernels for 0% -> 29%
where the time goes in v1:
time: 258 us; the launch traced here: 257 us
  Pallas kernels  91.6 us (36%)
  waiting for transfers between devices  85.3 us (33%)
  starting transfers between devices  64.7 us (25%)
  local copies, waits for them, and re-layouts  10.4 us (4%)
  other arithmetic  3.78 us (1%)
    ppermute x19, waiting for transfers between devices, exchange(): return lax.ppermute(value, 'queue', [(i, i ^ bit) for i in range(peers)])  42.9 us
    pallas_call x2, Pallas kernels, project(): pl.pallas_call(functools.partial(project_kernel, layout, begun is not Non...  31.5 us
    pallas_call x2, Pallas kernels, attend(): pl.pallas_call(functools.partial(attention_kernel, total_width, span, pla...  17 us
    ppermute x8, waiting for transfers between devices, move(): return lax.ppermute(moved, axis, pairs)  15.1 us
    pallas_call x1, Pallas kernels, modulated_norm(): pl.pallas_call(norm_kernel, grid_spec=pltpu.PrefetchScalarGridSpec(num_sc...  13.9 us
    ppermute x8, starting transfers between devices, move(): return lax.ppermute(moved, axis, pairs)  13.5 us
    ppermute x19, starting transfers between devices, exchange(): return lax.ppermute(value, 'queue', [(i, i ^ bit) for i in range(peers)])  13.1 us
    ppermute x2, starting transfers between devices, along_line(): below[k] = above[k] = lax.ppermute(value, axis, pairs)  11.6 us
  transfers between devices with their start and end apart: 37, of which 20 were waited for; matrix products, arithmetic and copies ran while one was open for 3% of the time, Pallas kernels for 29%

profile of v1, /device:TPU:0, one launch (start us, length us, event | category | flops | bytes accessed | tf_op | source)
XLA Modules:
  0.0 256.5 jit_solution(15820296375306196756)
XLA Ops:
  0.0 1.3 fusion
  1.5 3.0 %collective-permute-start = (bf16[960,640]{1,0:T(8,128)(2,1)S(1)}, bf16[960,640]{1,0:T(8,128)(2,1)}, u32[]{:S(2)}, u32[]{:S(2)}) collective-permute-start(bf16[960,640]{1,0:T(8,128)(2,1)S(1)} %pad_maximum_fusion.1.refs_2_), channel_id=1, source_target_pairs={{0,16},{4,20},{8,24},{12,28},{16,0},{20,4},{24,8},{28,12},{1,17},{... | collective-permute-start | bytes 3686408 | tf_op jit(solution)/shard_map/ppermute | solution.py:64
  4.7 1.6 collective-permute-start.1
  8.7 23.9 %collective-permute-done.refs_8_ = bf16[960,640]{1,0:T(8,128)(2,1)} collective-permute-done((bf16[960,640]{1,0:T(8,128)(2,1)S(1)}, bf16[960,640]{1,0:T(8,128)(2,1)}, u32[]{:S(2)}, u32[]{:S(2)}) %collective-permute-start) | collective-permute-done | bytes 1228832 | tf_op jit(solution)/shard_map/ppermute | solution.py:64
  32.5 2.3 collective-permute-done.1.refs_7_
  36.6 13.9 %modulated_norm.1.refs_1_ = bf16[8,768,640]{2,1,0:T(8,128)(2,1)} custom-call(s32[2]{0:T(128)} %levels_ref.1, bf16[2,384,5120]{2,1,0:T(8,128)(2,1)} %latents_ref.4, bf16[2,384,5120]{2,1,0:T(8,128)(2,1)} %control_ref.5, f32[3,64,5120]{2,1,0:T(8,128)} %bitcast.20), custom_call_target="tpu_custom_call" | custom-call | flops 2457600 | bytes 1474560 | tf_op jit(solution)/shard_map/modulated_norm/pallas_call | solution.py:98
  50.5 4.4 %all-to-all-start = ((bf16[8,80,640]{2,1,0:T(8,128)(2,1)}), bf16[8,80,640]{2,1,0:T(8,128)(2,1)}, u32[]{:S(2)}, u32[]{:S(2)}) async-start(bf16[8,80,640]{2,1,0:T(8,128)(2,1)} %bitcast.13), calls=%async_computation | async-start | bytes 1638400 | tf_op jit(solution)/shard_map/all_to_all | solution.py:555
  54.9 3.4 %collective-permute-done.6.refs_9_ = bf16[960,640]{1,0:T(8,128)(2,1)} collective-permute-done((bf16[960,640]{1,0:T(8,128)(2,1)S(1)}, bf16[960,640]{1,0:T(8,128)(2,1)}, u32[]{:S(2)}, u32[]{:S(2)}) %collective-permute-start.6) | collective-permute-done | bytes 1228832 | tf_op jit(solution)/shard_map/ppermute | solution.py:64
  58.3 9.9 %all-to-all-done = bf16[8,80,640]{2,1,0:T(8,128)(2,1)} async-done(((bf16[8,80,640]{2,1,0:T(8,128)(2,1)}), bf16[8,80,640]{2,1,0:T(8,128)(2,1)}, u32[]{:S(2)}, u32[]{:S(2)}) %all-to-all-start) | async-done | bytes 819232 | tf_op jit(solution)/shard_map/all_to_all | solution.py:555
  68.8 1.7 collective-permute-start.11
  71.5 1.8 collective-permute-done.7.refs_10_
  73.3 20.9 %project_begin.1.refs_6_ = f32[768,1920]{1,0:T(8,128)} custom-call(s32[6]{0:T(128)} %stack.73.refs_0_, bf16[8,768,640]{2,1,0:T(8,128)(2,1)} %modulated_norm.1.refs_1_, bf16[960,640]{1,0:T(8,128)(2,1)} %copy-done.4, bf16[960,640]{1,0:T(8,128)(2,1)} %copy-done.5, bf16[960,640]{1,0:T(8,128)(2,1)} %collective-permute-done.3.refs_4_, ...), custom_call_target="tpu_custom_call" | custom-call | flops 707788800 | bytes 1658880 | tf_op jit(solution)/shard_map/project_begin/pallas_call | solution.py:203
  94.2 3.8 %collective-permute-done.11.refs_3_ = bf16[960,640]{1,0:T(8,128)(2,1)S(1)} collective-permute-done((bf16[960,640]{1,0:T(8,128)(2,1)}, bf16[960,640]{1,0:T(8,128)(2,1)S(1)}, u32[]{:S(2)}, u32[]{:S(2)}) %collective-permute-start.11) | collective-permute-done | bytes 1228832 | tf_op jit(solution)/shard_map/ppermute | solution.py:64
  98.0 1.4 collective-permute-done.2.refs_2_
  99.4 1.5 collective-permute-done.13.refs_5_
  100.9 1.9 collective-permute-done.12.refs_4_
  102.8 10.6 %project_final.1 = (bf16[2,384,640]{2,1,0:T(8,128)(2,1)}, bf16[2,384,640]{2,1,0:T(8,128)(2,1)}, bf16[1,384,640]{2,1,0:T(8,128)(2,1)}, bf16[1,384,640]{2,1,0:T(8,128)(2,1)}, f32[2,6,128]{2,1,0:T(8,128)}) custom-call(s32[2]{0:T(128)} %pad_add_fusion.1.refs_0_, bf16[8,768,640]{2,1,0:T(8,128)(2,1)} %modulated_norm.1.refs_1_, bf16[960,640]{1,0:T(8,128)(2,1)} %copy-done.11, ...), custom_call_target="tpu_custom_call" | custom-call | flops 235929600 | bytes 798720 | tf_op jit(solution)/shard_map/project_final/pallas_call | solution.py:203
  113.4 2.0 collective-permute-start.14
  116.5 5.0 %all-to-all-start.1 = ((bf16[8,80,640]{2,1,0:T(8,128)(2,1)}), bf16[8,80,640]{2,1,0:T(8,128)(2,1)S(1)}, u32[]{:S(2)}, u32[]{:S(2)}) async-start(bf16[8,80,640]{2,1,0:T(8,128)(2,1)} %all-to-all-done), calls=%async_computation.1 | async-start | bytes 1638400 | tf_op jit(solution)/shard_map/all_to_all | solution.py:561
  121.5 3.2 %collective-permute-start.18 = (bf16[2,384,640]{2,1,0:T(8,128)(2,1)}, bf16[2,384,640]{2,1,0:T(8,128)(2,1)S(1)}, u32[]{:S(2)}, u32[]{:S(2)}) collective-permute-start(bf16[2,384,640]{2,1,0:T(8,128)(2,1)} %get-tuple-element.38.k2.v2), channel_id=1, source_target_pairs={{0,4},{4,8},{8,12},{12,16},{16,20},{20,24},{24,28},{1,5},{5,9},{9,... | collective-permute-start | bytes 2949128 | tf_op jit(solution)/shard_map/ppermute | solution.py:33
  124.7 4.7 %collective-permute-start.21 = (bf16[2,384,640]{2,1,0:T(8,128)(2,1)}, bf16[2,384,640]{2,1,0:T(8,128)(2,1)S(1)}, u32[]{:S(2)}, u32[]{:S(2)}) collective-permute-start(bf16[2,384,640]{2,1,0:T(8,128)(2,1)} %get-tuple-element.39.k1.v1.k2.v2), channel_id=1, source_target_pairs={{0,4},{4,8},{8,12},{12,16},{16,20},{20,24},{24,28},{1,5},{5,9},{9,... | collective-permute-start | bytes 2949128 | tf_op jit(solution)/shard_map/ppermute | solution.py:33
  130.1 2.0 collective-permute-start.15
  132.1 3.8 %collective-permute-done.15 = f32[4,6,128]{2,1,0:T(8,128)S(1)} collective-permute-done((f32[4,6,128]{2,1,0:T(8,128)S(1)}, f32[4,6,128]{2,1,0:T(8,128)S(1)}, u32[]{:S(2)}, u32[]{:S(2)}) %collective-permute-start.15) | collective-permute-done | bytes 12320 | tf_op jit(solution)/shard_map/ppermute | solution.py:53
  135.9 5.1 %collective-permute-start.16 = (f32[4,6,128]{2,1,0:T(8,128)S(1)}, f32[4,6,128]{2,1,0:T(8,128)S(1)}, u32[]{:S(2)}, u32[]{:S(2)}) collective-permute-start(f32[4,6,128]{2,1,0:T(8,128)S(1)} %add.15.refs_0_), channel_id=1, source_target_pairs={{0,2},{1,3},{2,0},{3,1},{4,6},{5,7},{6,4},{7,5},{8,10},{9,11},{10,... | collective-permute-start | bytes 36872 | tf_op jit(solution)/shard_map/ppermute | solution.py:53
  141.0 3.2 %collective-permute-done.16.refs_1_ = f32[4,6,128]{2,1,0:T(8,128)S(1)} collective-permute-done((f32[4,6,128]{2,1,0:T(8,128)S(1)}, f32[4,6,128]{2,1,0:T(8,128)S(1)}, u32[]{:S(2)}, u32[]{:S(2)}) %collective-permute-start.16) | collective-permute-done | bytes 12320 | tf_op jit(solution)/shard_map/ppermute | solution.py:53
  147.2 8.5 %attend.2.refs_0_ = bf16[384,640]{1,0:T(8,128)(2,1)} custom-call(s32[2,2]{1,0:T(2,128)} %and_convert_fusion.seen_ref, bf16[1,384,640]{2,1,0:T(8,128)(2,1)} %get-tuple-element.37.q_ref, f32[1,640]{1,0:T(1,128)} %reshape.21.q_gain_ref, f32[1,640]{1,0:T(1,128)} %reshape.22.k_gain_ref, bf16[2,384,640]{2,1,0:T(8,128)(2,1)} %copy-done, ...), custom_call_target="tpu_custom_call" | custom-call | flops 70778880 | bytes 245760 | tf_op jit(solution)/shard_map/attend/pallas_call | solution.py:286
  155.7 1.4 collective-permute-start.19
  157.1 1.3 collective-permute-start.20
  158.4 6.4 %collective-permute-start.25 = (bf16[384,640]{1,0:T(8,128)(2,1)}, bf16[384,640]{1,0:T(8,128)(2,1)S(1)}, u32[]{:S(2)}, u32[]{:S(2)}) collective-permute-start(bf16[384,640]{1,0:T(8,128)(2,1)} %attend.2.refs_0_), channel_id=1, source_target_pairs={{0,3},{3,0},{4,7},{7,4},{8,11},{11,8},{12,15},{15,12},{16,19},{19,... | collective-permute-start | bytes 1474568 | tf_op jit(solution)/shard_map/ppermute | solution.py:320
  164.8 4.2 %collective-permute-done.19.refs_1_ = bf16[384,640]{1,0:T(8,128)(2,1)S(1)} collective-permute-done((bf16[384,640]{1,0:T(8,128)(2,1)}, bf16[384,640]{1,0:T(8,128)(2,1)S(1)}, u32[]{:S(2)}, u32[]{:S(2)}) %collective-permute-start.19) | collective-permute-done | bytes 491552 | tf_op jit(solution)/shard_map/ppermute | solution.py:313
  169.7 4.0 %collective-permute-done.20.refs_4_ = bf16[384,640]{1,0:T(8,128)(2,1)S(1)} collective-permute-done((bf16[384,640]{1,0:T(8,128)(2,1)}, bf16[384,640]{1,0:T(8,128)(2,1)S(1)}, u32[]{:S(2)}, u32[]{:S(2)}) %collective-permute-start.20) | collective-permute-done | bytes 491552 | tf_op jit(solution)/shard_map/ppermute | solution.py:313
  173.7 1.3 collective-permute-start.26
  175.0 8.5 %attend.3.refs_0_.refs_2_.refs_5_ = bf16[384,640]{1,0:T(8,128)(2,1)} custom-call(s32[2,2]{1,0:T(2,128)} %and_convert_fusion.seen_ref, bf16[1,384,640]{2,1,0:T(8,128)(2,1)} %get-tuple-element.40.q_ref, f32[1,640]{1,0:T(1,128)} %reshape.21.q_gain_ref, f32[1,640]{1,0:T(1,128)} %reshape.22.k_gain_ref, bf16[2,384,640]{2,1,0:T(8,128)(2,1)} %copy-done.6, ...), custom_call_target="tpu_custom_call" | custom-call | flops 70778880 | bytes 245760 | tf_op jit(solution)/shard_map/attend/pallas_call | solution.py:286
  183.5 1.1 slice.14
  185.7 3.0 %collective-permute-start.27 = (bf16[2,2,80,640]{3,2,1,0:T(8,128)(2,1)S(1)}, bf16[2,2,80,640]{3,2,1,0:T(8,128)(2,1)S(1)}, u32[]{:S(2)}, u32[]{:S(2)}) collective-permute-start(bf16[2,2,80,640]{3,2,1,0:T(8,128)(2,1)S(1)} %slice.15), channel_id=1, source_target_pairs={{0,16},{4,20},{8,24},{12,28},{16,0},{20,4},{24,8},{28,12},{1,17},{... | collective-permute-start | bytes 1228808 | tf_op jit(solution)/shard_map/ppermute | solution.py:64
  188.8 3.4 %collective-permute-done.26.refs_5_ = bf16[384,640]{1,0:T(8,128)(2,1)} collective-permute-done((bf16[384,640]{1,0:T(8,128)(2,1)S(1)}, bf16[384,640]{1,0:T(8,128)(2,1)}, u32[]{:S(2)}, u32[]{:S(2)}) %collective-permute-start.26) | collective-permute-done | bytes 491552 | tf_op jit(solution)/shard_map/ppermute | solution.py:313
  192.6 2.0 collective-permute-done.27
  194.8 1.7 pad_maximum_fusion.refs_0_
  197.4 5.3 %collective-permute-start.30 = (bf16[384,640]{1,0:T(8,128)(2,1)}, bf16[384,640]{1,0:T(8,128)(2,1)}, u32[]{:S(2)}, u32[]{:S(2)}) collective-permute-start(bf16[384,640]{1,0:T(8,128)(2,1)} %attend.3.refs_0_.refs_2_.refs_5_), channel_id=1, source_target_pairs={{0,1},{1,2},{2,3},{4,5},{5,6},{6,7},{8,9},{9,10},{10,11},{12,13},{... | collective-permute-start | bytes 1474568 | tf_op jit(solution)/shard_map/ppermute | solution.py:313
  202.7 1.3 collective-permute-start.32
  204.0 6.9 %assemble.1.weight_ref = bf16[4,640,1280]{2,1,0:T(8,128)(2,1)} custom-call(s32[8]{0:T(128)} %stack.70.index_ref, bf16[4,4,2,80,640]{4,3,2,1,0:T(8,128)(2,1)} %copy-done.1, bf16[4,4,2,80,640]{4,3,2,1,0:T(8,128)(2,1)} %collective-permute-done.28.refs_1_), custom_call_target="tpu_custom_call" | custom-call | bytes 819200 | tf_op jit(solution)/shard_map/assemble/pallas_call | solution.py:588
  210.9 8.6 %update_last.1 = bf16[384,1280]{1,0:T(8,128)(2,1)} custom-call(s32[3]{0:T(128)} %pad_add_fusion.place_ref, bf16[4,640,1280]{2,1,0:T(8,128)(2,1)} %assemble.1.weight_ref, bf16[2,384,5120]{2,1,0:T(8,128)(2,1)} %latents_ref.4, bf16[2,384,5120]{2,1,0:T(8,128)(2,1)} %control_ref.5, f32[3,64,5120]{2,1,0:T(8,128)} %bitcast.21, bf16[384,640]{1,0:T(8,128)(2,1)} %attend.2.refs_0_, ...), custom_call_target="tpu_custom_call" | custom-call | flops 157286400 | bytes 778240 | tf_op jit(solution)/shard_map/update_last/pallas_call | solution.py:494
  219.6 5.2 %collective-permute-start.31 = (bf16[384,640]{1,0:T(8,128)(2,1)S(1)}, bf16[384,640]{1,0:T(8,128)(2,1)S(1)}, u32[]{:S(2)}, u32[]{:S(2)}) collective-permute-start(bf16[384,640]{1,0:T(8,128)(2,1)S(1)} %copy-done.2), channel_id=1, source_target_pairs={{0,3},{3,0},{4,7},{7,4},{8,11},{11,8},{12,15},{15,12},{16,19},{19,... | collective-permute-start | bytes 1474568 | tf_op jit(solution)/shard_map/ppermute | solution.py:320
  225.6 1.6 collective-permute-start.34
  227.1 9.3 %collective-permute-done.31.refs_3_.refs_6_ = bf16[384,640]{1,0:T(8,128)(2,1)S(1)} collective-permute-done((bf16[384,640]{1,0:T(8,128)(2,1)S(1)}, bf16[384,640]{1,0:T(8,128)(2,1)S(1)}, u32[]{:S(2)}, u32[]{:S(2)}) %collective-permute-start.31) | collective-permute-done | bytes 491552 | tf_op jit(solution)/shard_map/ppermute | solution.py:320
  237.2 7.1 %update_begin.1.begun_ref = f32[1,384,1280]{2,1,0:T(8,128)} custom-call(s32[3]{0:T(128)} %pad_add_fusion.place_ref, bf16[4,640,1280]{2,1,0:T(8,128)(2,1)} %assemble.1.weight_ref, bf16[384,640]{1,0:T(8,128)(2,1)} %attend.3.refs_0_.refs_2_.refs_5_, bf16[384,640]{1,0:T(8,128)(2,1)} %collective-permute-done.30.refs_1_, ...), custom_call_target="tpu_custom_call" | custom-call | flops 117964800 | bytes 645120 | tf_op jit(solution)/shard_map/update_begin/pallas_call | solution.py:510
  244.4 3.5 %collective-permute-done.34.refs_5_ = bf16[384,640]{1,0:T(8,128)(2,1)S(1)} collective-permute-done((bf16[384,640]{1,0:T(8,128)(2,1)}, bf16[384,640]{1,0:T(8,128)(2,1)S(1)}, u32[]{:S(2)}, u32[]{:S(2)}) %collective-permute-start.34) | collective-permute-done | bytes 491552 | tf_op jit(solution)/shard_map/ppermute | solution.py:313
  249.6 6.7 %update_rest.1 = f32[2,384,1280]{2,1,0:T(8,128)} custom-call(s32[3]{0:T(128)} %pad_add_fusion.place_ref, bf16[384,1280]{1,0:T(8,128)(2,1)} %copy-done.13, f32[1,384,1280]{2,1,0:T(8,128)} %update_begin.1.begun_ref, bf16[4,640,1280]{2,1,0:T(8,128)(2,1)} %assemble.1.weight_ref, bf16[2,384,5120]{2,1,0:T(8,128)(2,1)} %latents_ref.4, ...), custom_call_target="tpu_custom_call" | custom-call | flops 39321600 | bytes 378880 | tf_op jit(solution)/shard_map/update_rest/pallas_call | solution.py:534
  (109 shorter events, 17.5 us)
Async XLA Ops:
  1.4 34.0 %copy-start.26 = (s32[2]{0:T(128)S(1)}, s32[2]{0:T(128)}, u32[]{:S(2)}) copy-start(s32[2]{0:T(128)} %levels_ref.1) | copy-start | bytes 28
  1.4 34.6 %copy-start.25 = (s32[2,2]{1,0:T(2,128)S(1)}, s32[2,2]{1,0:T(2,128)}, u32[]{:S(2)}) copy-start(s32[2,2]{1,0:T(2,128)} %param.15) | copy-start | bytes 52
  1.4 34.6 %copy-start.27 = (s32[2]{0:T(128)S(1)}, s32[2]{0:T(128)}, u32[]{:S(2)}) copy-start(s32[2]{0:T(128)} %constant.26.clone) | copy-start | bytes 28
  1.5 49.0 %copy-start.4 = (bf16[960,640]{1,0:T(8,128)(2,1)}, bf16[960,640]{1,0:T(8,128)(2,1)S(1)}, u32[]{:S(2)}) copy-start(bf16[960,640]{1,0:T(8,128)(2,1)S(1)} %pad_maximum_fusion.1.refs_2_) | copy-start | bytes 3686404
  1.5 31.0 %collective-permute-start = (bf16[960,640]{1,0:T(8,128)(2,1)S(1)}, bf16[960,640]{1,0:T(8,128)(2,1)}, u32[]{:S(2)}, u32[]{:S(2)}) collective-permute-start(bf16[960,640]{1,0:T(8,128)(2,1)S(1)} %pad_maximum_fusion.1.refs_2_), channel_id=1, source_target_pairs={{0,16},{4,20},{8,24},{12,28},{16,0},{20,4},{24,8},{28,12},{1,17},{... | collective-permute-start | bytes 3686408 | tf_op jit(solution)/shard_map/ppermute | solution.py:64
  4.7 45.8 %copy-start.5 = (bf16[960,640]{1,0:T(8,128)(2,1)}, bf16[960,640]{1,0:T(8,128)(2,1)S(1)}, u32[]{:S(2)}) copy-start(bf16[960,640]{1,0:T(8,128)(2,1)S(1)} %pad_maximum_fusion.2.refs_3_) | copy-start | bytes 3686404
  4.7 30.1 %collective-permute-start.1 = (bf16[960,640]{1,0:T(8,128)(2,1)S(1)}, bf16[960,640]{1,0:T(8,128)(2,1)}, u32[]{:S(2)}, u32[]{:S(2)}) collective-permute-start(bf16[960,640]{1,0:T(8,128)(2,1)S(1)} %pad_maximum_fusion.2.refs_3_), channel_id=1, source_target_pairs={{0,8},{4,12},{8,0},{12,4},{16,24},{20,28},{24,16},{28,20},{1,9},{5... | collective-permute-start | bytes 3686408 | tf_op jit(solution)/shard_map/ppermute | solution.py:64
  6.3 52.1 %collective-permute-start.6 = (bf16[960,640]{1,0:T(8,128)(2,1)S(1)}, bf16[960,640]{1,0:T(8,128)(2,1)}, u32[]{:S(2)}, u32[]{:S(2)}) collective-permute-start(bf16[960,640]{1,0:T(8,128)(2,1)S(1)} %pad_maximum_fusion.2.refs_3_), channel_id=1, source_target_pairs={{0,16},{4,20},{8,24},{12,28},{16,0},{20,4},{24,8},{28,12},{1,17},{... | collective-permute-start | bytes 3686408 | tf_op jit(solution)/shard_map/ppermute | solution.py:64
  6.8 61.5 %collective-permute-start.5 = (bf16[960,640]{1,0:T(8,128)(2,1)S(1)}, bf16[960,640]{1,0:T(8,128)(2,1)}, u32[]{:S(2)}, u32[]{:S(2)}) collective-permute-start(bf16[960,640]{1,0:T(8,128)(2,1)S(1)} %pad_maximum_fusion.1.refs_2_), channel_id=1, source_target_pairs={{0,8},{4,12},{8,0},{12,4},{16,24},{20,28},{24,16},{28,20},{1,9},{5... | collective-permute-start | bytes 3686408 | tf_op jit(solution)/shard_map/ppermute | solution.py:64
  6.8 61.4 %collective-permute-start.3 = (bf16[960,640]{1,0:T(8,128)(2,1)S(1)}, bf16[960,640]{1,0:T(8,128)(2,1)}, u32[]{:S(2)}, u32[]{:S(2)}) collective-permute-start(bf16[960,640]{1,0:T(8,128)(2,1)S(1)} %pad_maximum_fusion.1.refs_2_), channel_id=1, source_target_pairs={{0,4},{4,0},{8,12},{12,8},{16,20},{20,16},{24,28},{28,24},{1,5},{5... | collective-permute-start | bytes 3686408 | tf_op jit(solution)/shard_map/ppermute | solution.py:64
  32.5 36.2 %collective-permute-start.4 = (bf16[960,640]{1,0:T(8,128)(2,1)S(1)}, bf16[960,640]{1,0:T(8,128)(2,1)}, u32[]{:S(2)}, u32[]{:S(2)}) collective-permute-start(bf16[960,640]{1,0:T(8,128)(2,1)S(1)} %pad_maximum_fusion.2.refs_3_), channel_id=1, source_target_pairs={{0,4},{4,0},{8,12},{12,8},{16,20},{20,16},{24,28},{28,24},{1,5},{5... | collective-permute-start | bytes 3686408 | tf_op jit(solution)/shard_map/ppermute | solution.py:64
  34.8 35.6 %collective-permute-start.8 = (bf16[960,640]{1,0:T(8,128)(2,1)}, bf16[960,640]{1,0:T(8,128)(2,1)}, u32[]{:S(2)}, u32[]{:S(2)}) collective-permute-start(bf16[960,640]{1,0:T(8,128)(2,1)} %collective-permute-done.1.refs_7_), channel_id=1, source_target_pairs={{0,4},{4,0},{8,12},{12,8},{16,20},{20,16},{24,28},{28,24},{1,5},{5... | collective-permute-start | bytes 3686408 | tf_op jit(solution)/shard_map/ppermute | solution.py:64
  50.5 17.7 %all-to-all-start = ((bf16[8,80,640]{2,1,0:T(8,128)(2,1)}), bf16[8,80,640]{2,1,0:T(8,128)(2,1)}, u32[]{:S(2)}, u32[]{:S(2)}) async-start(bf16[8,80,640]{2,1,0:T(8,128)(2,1)} %bitcast.13), calls=%async_computation | async-start | bytes 1638400 | tf_op jit(solution)/shard_map/all_to_all | solution.py:555
  58.3 12.7 %collective-permute-start.9 = (bf16[960,640]{1,0:T(8,128)(2,1)}, bf16[960,640]{1,0:T(8,128)(2,1)}, u32[]{:S(2)}, u32[]{:S(2)}) collective-permute-start(bf16[960,640]{1,0:T(8,128)(2,1)} %collective-permute-done.refs_8_), channel_id=1, source_target_pairs={{0,4},{4,0},{8,12},{12,8},{16,20},{20,16},{24,28},{28,24},{1,5},{5... | collective-permute-start | bytes 3686408 | tf_op jit(solution)/shard_map/ppermute | solution.py:64
  68.3 3.3 %collective-permute-start.10 = (bf16[960,640]{1,0:T(8,128)(2,1)}, bf16[960,640]{1,0:T(8,128)(2,1)}, u32[]{:S(2)}, u32[]{:S(2)}) collective-permute-start(bf16[960,640]{1,0:T(8,128)(2,1)} %collective-permute-done.6.refs_9_), channel_id=1, source_target_pairs={{0,4},{4,0},{8,12},{12,8},{16,20},{20,16},{24,28},{28,24},{1,5},{5... | collective-permute-start | bytes 3686408 | tf_op jit(solution)/shard_map/ppermute | solution.py:64
  68.3 5.0 %collective-permute-start.7 = (bf16[960,640]{1,0:T(8,128)(2,1)}, bf16[960,640]{1,0:T(8,128)(2,1)}, u32[]{:S(2)}, u32[]{:S(2)}) collective-permute-start(bf16[960,640]{1,0:T(8,128)(2,1)} %collective-permute-done.5.refs_6_), channel_id=1, source_target_pairs={{0,4},{4,0},{8,12},{12,8},{16,20},{20,16},{24,28},{28,24},{1,5},{5... | collective-permute-start | bytes 3686408 | tf_op jit(solution)/shard_map/ppermute | solution.py:64
  68.8 29.2 %collective-permute-start.11 = (bf16[960,640]{1,0:T(8,128)(2,1)}, bf16[960,640]{1,0:T(8,128)(2,1)S(1)}, u32[]{:S(2)}, u32[]{:S(2)}) collective-permute-start(bf16[960,640]{1,0:T(8,128)(2,1)} %collective-permute-done.1.refs_7_), channel_id=1, source_target_pairs={{0,16},{4,20},{8,24},{12,28},{16,0},{20,4},{24,8},{28,12},{1,17},{... | collective-permute-start | bytes 3686408 | tf_op jit(solution)/shard_map/ppermute | solution.py:64
  70.5 28.9 %collective-permute-start.2 = (bf16[960,640]{1,0:T(8,128)(2,1)}, bf16[960,640]{1,0:T(8,128)(2,1)S(1)}, u32[]{:S(2)}, u32[]{:S(2)}) collective-permute-start(bf16[960,640]{1,0:T(8,128)(2,1)} %collective-permute-done.refs_8_), channel_id=1, source_target_pairs={{0,8},{4,12},{8,0},{12,4},{16,24},{20,28},{24,16},{28,20},{1,9},{5... | collective-permute-start | bytes 3686408 | tf_op jit(solution)/shard_map/ppermute | solution.py:64
  98.0 2.9 %collective-permute-start.13 = (bf16[960,640]{1,0:T(8,128)(2,1)S(1)}, bf16[960,640]{1,0:T(8,128)(2,1)S(1)}, u32[]{:S(2)}, u32[]{:S(2)}) collective-permute-start(bf16[960,640]{1,0:T(8,128)(2,1)S(1)} %collective-permute-done.11.refs_3_), channel_id=1, source_target_pairs={{0,4},{4,0},{8,12},{12,8},{16,20},{20,16},{24,28},{28,24},{1,5},{5... | collective-permute-start | bytes 3686408 | tf_op jit(solution)/shard_map/ppermute | solution.py:64
  99.4 3.4 %collective-permute-start.12 = (bf16[960,640]{1,0:T(8,128)(2,1)S(1)}, bf16[960,640]{1,0:T(8,128)(2,1)}, u32[]{:S(2)}, u32[]{:S(2)}) collective-permute-start(bf16[960,640]{1,0:T(8,128)(2,1)S(1)} %collective-permute-done.2.refs_2_), channel_id=1, source_target_pairs={{0,4},{4,0},{8,12},{12,8},{16,20},{20,16},{24,28},{28,24},{1,5},{5... | collective-permute-start | bytes 3686408 | tf_op jit(solution)/shard_map/ppermute | solution.py:64
  113.4 3.1 %collective-permute-start.14 = (f32[2,6,128]{2,1,0:T(8,128)}, f32[2,6,128]{2,1,0:T(8,128)S(1)}, u32[]{:S(2)}, u32[]{:S(2)}) collective-permute-start(f32[2,6,128]{2,1,0:T(8,128)} %get-tuple-element.33), channel_id=1, source_target_pairs={{0,4},{4,8},{8,12},{12,16},{16,20},{20,24},{24,28},{1,5},{5,9},{9,... | collective-permute-start | bytes 18440 | tf_op jit(solution)/shard_map/ppermute | solution.py:33
  116.5 27.7 %all-to-all-start.1 = ((bf16[8,80,640]{2,1,0:T(8,128)(2,1)}), bf16[8,80,640]{2,1,0:T(8,128)(2,1)S(1)}, u32[]{:S(2)}, u32[]{:S(2)}) async-start(bf16[8,80,640]{2,1,0:T(8,128)(2,1)} %all-to-all-done), calls=%async_computation.1 | async-start | bytes 1638400 | tf_op jit(solution)/shard_map/all_to_all | solution.py:561
  121.5 24.8 %collective-permute-start.18 = (bf16[2,384,640]{2,1,0:T(8,128)(2,1)}, bf16[2,384,640]{2,1,0:T(8,128)(2,1)S(1)}, u32[]{:S(2)}, u32[]{:S(2)}) collective-permute-start(bf16[2,384,640]{2,1,0:T(8,128)(2,1)} %get-tuple-element.38.k2.v2), channel_id=1, source_target_pairs={{0,4},{4,8},{8,12},{12,16},{16,20},{20,24},{24,28},{1,5},{5,9},{9,... | collective-permute-start | bytes 2949128 | tf_op jit(solution)/shard_map/ppermute | solution.py:33
  124.7 33.7 %collective-permute-start.21 = (bf16[2,384,640]{2,1,0:T(8,128)(2,1)}, bf16[2,384,640]{2,1,0:T(8,128)(2,1)S(1)}, u32[]{:S(2)}, u32[]{:S(2)}) collective-permute-start(bf16[2,384,640]{2,1,0:T(8,128)(2,1)} %get-tuple-element.39.k1.v1.k2.v2), channel_id=1, source_target_pairs={{0,4},{4,8},{8,12},{12,16},{16,20},{20,24},{24,28},{1,5},{5,9},{9,... | collective-permute-start | bytes 2949128 | tf_op jit(solution)/shard_map/ppermute | solution.py:33
  130.1 5.8 %collective-permute-start.15 = (f32[4,6,128]{2,1,0:T(8,128)S(1)}, f32[4,6,128]{2,1,0:T(8,128)S(1)}, u32[]{:S(2)}, u32[]{:S(2)}) collective-permute-start(f32[4,6,128]{2,1,0:T(8,128)S(1)} %constant_dynamic-update-slice_fusion), channel_id=1, source_target_pairs={{0,1},{1,0},{2,3},{3,2},{4,5},{5,4},{6,7},{7,6},{8,9},{9,8},{10,11... | collective-permute-start | bytes 36872 | tf_op jit(solution)/shard_map/ppermute | solution.py:53
  135.9 10.4 %copy-start.21 = (f32[4,6,128]{2,1,0:T(8,128)}, f32[4,6,128]{2,1,0:T(8,128)S(1)}, u32[]{:S(2)}) copy-start(f32[4,6,128]{2,1,0:T(8,128)S(1)} %add.15.refs_0_) | copy-start | bytes 36868
  135.9 8.3 %collective-permute-start.16 = (f32[4,6,128]{2,1,0:T(8,128)S(1)}, f32[4,6,128]{2,1,0:T(8,128)S(1)}, u32[]{:S(2)}, u32[]{:S(2)}) collective-permute-start(f32[4,6,128]{2,1,0:T(8,128)S(1)} %add.15.refs_0_), channel_id=1, source_target_pairs={{0,2},{1,3},{2,0},{3,1},{4,6},{5,7},{6,4},{7,5},{8,10},{9,11},{10,... | collective-permute-start | bytes 36872 | tf_op jit(solution)/shard_map/ppermute | solution.py:53
  144.2 39.3 %copy-start.7 = (bf16[8,80,640]{2,1,0:T(8,128)(2,1)}, bf16[8,80,640]{2,1,0:T(8,128)(2,1)S(1)}, u32[]{:S(2)}) copy-start(bf16[8,80,640]{2,1,0:T(8,128)(2,1)S(1)} %all-to-all-done.1) | copy-start | bytes 2457604
  144.2 39.3 %collective-permute-start.22 = (bf16[4,2,80,640]{3,2,1,0:T(8,128)(2,1)S(1)}, bf16[4,2,80,640]{3,2,1,0:T(8,128)(2,1)}, u32[]{:S(2)}, u32[]{:S(2)}) collective-permute-start(bf16[4,2,80,640]{3,2,1,0:T(8,128)(2,1)S(1)} %bitcast.23), channel_id=1, source_target_pairs={{0,16},{4,20},{8,24},{12,28},{16,0},{20,4},{24,8},{28,12},{1,17},{... | collective-permute-start | bytes 2457608 | tf_op jit(solution)/shard_map/ppermute | solution.py:64
  145.2 39.5 %collective-permute-start.17 = (bf16[4,2,80,640]{3,2,1,0:T(8,128)(2,1)S(1)}, bf16[4,2,80,640]{3,2,1,0:T(8,128)(2,1)}, u32[]{:S(2)}, u32[]{:S(2)}) collective-permute-start(bf16[4,2,80,640]{3,2,1,0:T(8,128)(2,1)S(1)} %bitcast.24), channel_id=1, source_target_pairs={{0,8},{4,12},{8,0},{12,4},{16,24},{20,28},{24,16},{28,20},{1,9},{5... | collective-permute-start | bytes 2457608 | tf_op jit(solution)/shard_map/ppermute | solution.py:64
  155.7 13.3 %collective-permute-start.19 = (bf16[384,640]{1,0:T(8,128)(2,1)}, bf16[384,640]{1,0:T(8,128)(2,1)S(1)}, u32[]{:S(2)}, u32[]{:S(2)}) collective-permute-start(bf16[384,640]{1,0:T(8,128)(2,1)} %attend.2.refs_0_), channel_id=1, source_target_pairs={{0,1},{1,2},{2,3},{4,5},{5,6},{6,7},{8,9},{9,10},{10,11},{12,13},{... | collective-permute-start | bytes 1474568 | tf_op jit(solution)/shard_map/ppermute | solution.py:313
  157.1 16.6 %collective-permute-start.20 = (bf16[384,640]{1,0:T(8,128)(2,1)}, bf16[384,640]{1,0:T(8,128)(2,1)S(1)}, u32[]{:S(2)}, u32[]{:S(2)}) collective-permute-start(bf16[384,640]{1,0:T(8,128)(2,1)} %attend.2.refs_0_), channel_id=1, source_target_pairs={{1,0},{2,1},{3,2},{5,4},{6,5},{7,6},{9,8},{10,9},{11,10},{13,12},{... | collective-permute-start | bytes 1474568 | tf_op jit(solution)/shard_map/ppermute | solution.py:313
  158.4 16.6 %copy-start.6 = (bf16[2,384,640]{2,1,0:T(8,128)(2,1)}, bf16[2,384,640]{2,1,0:T(8,128)(2,1)S(1)}, u32[]{:S(2)}) copy-start(bf16[2,384,640]{2,1,0:T(8,128)(2,1)S(1)} %collective-permute-done.21.k0.v0) | copy-start | bytes 2949124
  158.4 30.4 %collective-permute-start.25 = (bf16[384,640]{1,0:T(8,128)(2,1)}, bf16[384,640]{1,0:T(8,128)(2,1)S(1)}, u32[]{:S(2)}, u32[]{:S(2)}) collective-permute-start(bf16[384,640]{1,0:T(8,128)(2,1)} %attend.2.refs_0_), channel_id=1, source_target_pairs={{0,3},{3,0},{4,7},{7,4},{8,11},{11,8},{12,15},{15,12},{16,19},{19,... | collective-permute-start | bytes 1474568 | tf_op jit(solution)/shard_map/ppermute | solution.py:320
  169.0 14.5 %copy-start.16 = (bf16[384,640]{1,0:T(8,128)(2,1)}, bf16[384,640]{1,0:T(8,128)(2,1)S(1)}, u32[]{:S(2)}) copy-start(bf16[384,640]{1,0:T(8,128)(2,1)S(1)} %collective-permute-done.19.refs_1_) | copy-start | bytes 1474564
  169.0 19.7 %collective-permute-start.24 = (bf16[384,640]{1,0:T(8,128)(2,1)S(1)}, bf16[384,640]{1,0:T(8,128)(2,1)S(1)}, u32[]{:S(2)}, u32[]{:S(2)}) collective-permute-start(bf16[384,640]{1,0:T(8,128)(2,1)S(1)} %collective-permute-done.19.refs_1_), channel_id=1, source_target_pairs={{1,2},{2,3},{5,6},{6,7},{9,10},{10,11},{13,14},{14,15},{17,18},{18... | collective-permute-start | bytes 1474568 | tf_op jit(solution)/shard_map/ppermute | solution.py:313
  173.7 9.8 %copy-start.17 = (bf16[384,640]{1,0:T(8,128)(2,1)}, bf16[384,640]{1,0:T(8,128)(2,1)S(1)}, u32[]{:S(2)}) copy-start(bf16[384,640]{1,0:T(8,128)(2,1)S(1)} %collective-permute-done.20.refs_4_) | copy-start | bytes 1474564
  173.7 18.5 %collective-permute-start.26 = (bf16[384,640]{1,0:T(8,128)(2,1)S(1)}, bf16[384,640]{1,0:T(8,128)(2,1)}, u32[]{:S(2)}, u32[]{:S(2)}) collective-permute-start(bf16[384,640]{1,0:T(8,128)(2,1)S(1)} %collective-permute-done.20.refs_4_), channel_id=1, source_target_pairs={{1,0},{2,1},{5,4},{6,5},{9,8},{10,9},{13,12},{14,13},{17,16},{18,1... | collective-permute-start | bytes 1474568 | tf_op jit(solution)/shard_map/ppermute | solution.py:313
  183.5 11.3 %copy-start.8 = (bf16[8,80,640]{2,1,0:T(8,128)(2,1)S(1)}, bf16[8,80,640]{2,1,0:T(8,128)(2,1)}, u32[]{:S(2)}) copy-start(bf16[8,80,640]{2,1,0:T(8,128)(2,1)} %copy-done.7) | copy-start | bytes 2457604
  184.6 8.0 %collective-permute-start.23 = (bf16[2,2,80,640]{3,2,1,0:T(8,128)(2,1)S(1)}, bf16[2,2,80,640]{3,2,1,0:T(8,128)(2,1)S(1)}, u32[]{:S(2)}, u32[]{:S(2)}) collective-permute-start(bf16[2,2,80,640]{3,2,1,0:T(8,128)(2,1)S(1)} %slice.14), channel_id=1, source_target_pairs={{0,8},{4,12},{8,0},{12,4},{16,24},{20,28},{24,16},{28,20},{1,9},{5... | collective-permute-start | bytes 1228808 | tf_op jit(solution)/shard_map/ppermute | solution.py:64
  185.7 8.9 %collective-permute-start.27 = (bf16[2,2,80,640]{3,2,1,0:T(8,128)(2,1)S(1)}, bf16[2,2,80,640]{3,2,1,0:T(8,128)(2,1)S(1)}, u32[]{:S(2)}, u32[]{:S(2)}) collective-permute-start(bf16[2,2,80,640]{3,2,1,0:T(8,128)(2,1)S(1)} %slice.15), channel_id=1, source_target_pairs={{0,16},{4,20},{8,24},{12,28},{16,0},{20,4},{24,8},{28,12},{1,17},{... | collective-permute-start | bytes 1228808 | tf_op jit(solution)/shard_map/ppermute | solution.py:64
  196.5 7.5 %collective-permute-start.28 = (bf16[4,4,2,80,640]{4,3,2,1,0:T(8,128)(2,1)S(1)}, bf16[4,4,2,80,640]{4,3,2,1,0:T(8,128)(2,1)}, u32[]{:S(2)}, u32[]{:S(2)}) collective-permute-start(bf16[4,4,2,80,640]{4,3,2,1,0:T(8,128)(2,1)S(1)} %pad_maximum_fusion.refs_0_), channel_id=1, source_target_pairs={{0,4},{4,0},{8,12},{12,8},{16,20},{20,16},{24,28},{28,24},{1,5},{5... | collective-permute-start | bytes 9830408 | tf_op jit(solution)/shard_map/ppermute | solution.py:64
  197.4 27.5 %collective-permute-start.30 = (bf16[384,640]{1,0:T(8,128)(2,1)}, bf16[384,640]{1,0:T(8,128)(2,1)}, u32[]{:S(2)}, u32[]{:S(2)}) collective-permute-start(bf16[384,640]{1,0:T(8,128)(2,1)} %attend.3.refs_0_.refs_2_.refs_5_), channel_id=1, source_target_pairs={{0,1},{1,2},{2,3},{4,5},{5,6},{6,7},{8,9},{9,10},{10,11},{12,13},{... | collective-permute-start | bytes 1474568 | tf_op jit(solution)/shard_map/ppermute | solution.py:313
  202.7 22.9 %collective-permute-start.32 = (bf16[384,640]{1,0:T(8,128)(2,1)}, bf16[384,640]{1,0:T(8,128)(2,1)}, u32[]{:S(2)}, u32[]{:S(2)}) collective-permute-start(bf16[384,640]{1,0:T(8,128)(2,1)} %attend.3.refs_0_.refs_2_.refs_5_), channel_id=1, source_target_pairs={{1,0},{2,1},{3,2},{5,4},{6,5},{7,6},{9,8},{10,9},{11,10},{13,12},{... | collective-permute-start | bytes 1474568 | tf_op jit(solution)/shard_map/ppermute | solution.py:313
  219.5 28.3 %collective-permute-start.29 = (bf16[384,1280]{1,0:T(8,128)(2,1)}, bf16[384,1280]{1,0:T(8,128)(2,1)S(1)}, u32[]{:S(2)}, u32[]{:S(2)}) collective-permute-start(bf16[384,1280]{1,0:T(8,128)(2,1)} %update_last.1), channel_id=1, source_target_pairs={{0,4},{4,8},{8,12},{12,16},{16,20},{20,24},{24,28},{28,0},{1,5},{5... | collective-permute-start | bytes 2949128 | tf_op jit(solution)/shard_map/ppermute | solution.py:39
  219.6 16.8 %collective-permute-start.31 = (bf16[384,640]{1,0:T(8,128)(2,1)S(1)}, bf16[384,640]{1,0:T(8,128)(2,1)S(1)}, u32[]{:S(2)}, u32[]{:S(2)}) collective-permute-start(bf16[384,640]{1,0:T(8,128)(2,1)S(1)} %copy-done.2), channel_id=1, source_target_pairs={{0,3},{3,0},{4,7},{7,4},{8,11},{11,8},{12,15},{15,12},{16,19},{19,... | collective-permute-start | bytes 1474568 | tf_op jit(solution)/shard_map/ppermute | solution.py:320
  224.9 19.5 %collective-permute-start.33 = (bf16[384,640]{1,0:T(8,128)(2,1)}, bf16[384,640]{1,0:T(8,128)(2,1)S(1)}, u32[]{:S(2)}, u32[]{:S(2)}) collective-permute-start(bf16[384,640]{1,0:T(8,128)(2,1)} %collective-permute-done.30.refs_1_), channel_id=1, source_target_pairs={{1,2},{2,3},{5,6},{6,7},{9,10},{10,11},{13,14},{14,15},{17,18},{18... | collective-permute-start | bytes 1474568 | tf_op jit(solution)/shard_map/ppermute | solution.py:313
  225.6 22.3 %collective-permute-start.34 = (bf16[384,640]{1,0:T(8,128)(2,1)}, bf16[384,640]{1,0:T(8,128)(2,1)S(1)}, u32[]{:S(2)}, u32[]{:S(2)}) collective-permute-start(bf16[384,640]{1,0:T(8,128)(2,1)} %collective-permute-done.32.refs_4_), channel_id=1, source_target_pairs={{1,0},{2,1},{5,4},{6,5},{9,8},{10,9},{13,12},{14,13},{17,16},{18,1... | collective-permute-start | bytes 1474568 | tf_op jit(solution)/shard_map/ppermute | solution.py:313
  (17 other events, 66.6 us)

commit v2 on v1

--- a/solution.py
+++ b/solution.py
@@ -231,42 +231,53 @@
 def attention_kernel(
     total_width, span, places, seen_ref, q_ref, q_gain_ref, k_gain_ref, k0, k1, k2, v0, v1, v2, *refs
 ):
-    *square_refs, out_ref, factors = refs
-    tiles = q_ref.shape[0] // HD
-
-    @pl.when(pl.program_id(0) == 0)
-    def _():
-        for f, (array, first) in enumerate(places):
-            for t in range(tiles):
-                row = sum(ref[array, first + t : first + t + 1, :] for ref in square_refs)
-                squares = jnp.broadcast_to(row, (HD, HD)).T[:, 0:1]
-                factors[f, t * HD : (t + 1) * HD] = lax.rsqrt(squares / total_width + 1e-06)
-
-    def with_gain(values, factor, gain_ref):
-        return (values.astype(F32) * factor * gain_ref[...]).astype(BF16)
-
+    *square_refs, out_ref = refs
+    rows, cols = q_ref.shape
+    tiles = rows // HD
+    factors = []
+    for array, first in places:
+        pieces = []
+        for t in range(tiles):
+            row = sum(ref[array, first + t : first + t + 1, :] for ref in square_refs)
+            pieces.append(jnp.broadcast_to(row, (HD, HD)).T[:, 0:1])
+        squares = jnp.concatenate(pieces, axis=0)
+        factors.append(lax.rsqrt(squares / total_width + 1e-06))
+    hide = [jnp.where(seen_ref[span, w] == 1, 0.0, 1e30).astype(F32) for w in range(2)] + [0.0]
     to_exponent = HD ** (-0.5) * math.log2(math.e)
-    query = with_gain(q_ref[...], factors[0], q_gain_ref)
-    scores = [
-        lax.dot_general(
-            query,
-            with_gain(key[...], factors[1 + w], k_gain_ref),
-            (((1,), (1,)), ((), ())),
-            preferred_element_type=F32,
-        )
-        for w, key in enumerate((k0, k1, k2))
-    ]
-    tops = [jnp.max(s, axis=-1, keepdims=True) for s in scores]
-    hide = [jnp.where(seen_ref[span, w] == 1, 0.0, 1e30).astype(F32) for w in range(2)] + [0.0]
-    top = functools.reduce(jnp.maximum, (m - h for m, h in zip(tops, hide)))
-    expos = [jnp.exp2(s * to_exponent - (top * to_exponent + h)) for s, h in zip(scores, hide)]
-    inverse = 1.0 / jnp.sum(expos[0] + expos[1] + expos[2], axis=-1, keepdims=True)
-    total = None
-    for expo, value in zip(expos, (v0, v1, v2)):
-        probs = (expo * inverse).astype(BF16)
-        term = jnp.dot(probs, value[...], preferred_element_type=F32)
-        total = term if total is None else total + term
-    out_ref[...] = total.astype(BF16)
+
+    def with_gain(ref, head, factor, gain_ref):
+        values = ref[:, head].astype(F32) * factor * gain_ref[:, head]
+        return values.astype(BF16)
+
+    def scores_of(head):
+        query = with_gain(q_ref, head, factors[0], q_gain_ref)
+        return [
+            lax.dot_general(
+                query,
+                with_gain(key, head, factors[1 + w], k_gain_ref),
+                (((1,), (1,)), ((), ())),
+                preferred_element_type=F32,
+            )
+            for w, key in enumerate((k0, k1, k2))
+        ]
+
+    heads = [slice(h * HD, (h + 1) * HD) for h in range(cols // HD)]
+    scores = scores_of(heads[0])
+    for h, head in enumerate(heads):
+        following = scores_of(heads[h + 1]) if h + 1 < len(heads) else None
+        tops = [jnp.max(s, axis=-1, keepdims=True) for s in scores]
+        top = functools.reduce(jnp.maximum, (m - x for m, x in zip(tops, hide)))
+        expos = [
+            jnp.exp2(s * to_exponent - (top * to_exponent + x)) for s, x in zip(scores, hide)
+        ]
+        inverse = 1.0 / jnp.sum(expos[0] + expos[1] + expos[2], axis=-1, keepdims=True)
+        total = None
+        for expo, value in zip(expos, (v0, v1, v2)):
+            probs = (expo * inverse).astype(BF16)
+            term = jnp.dot(probs, value[:, head], preferred_element_type=F32)
+            total = term if total is None else total + term
+        out_ref[:, head] = total.astype(BF16)
+        scores = following
 
 
 def attend(span, seen, query, squares, gains, prior, own, total_width):
@@ -280,19 +291,18 @@
     arrays = [(own if array == 0 else prior)[index] for array, index in window]
 
     def part(which):
-        return pl.BlockSpec((None, rows, HD), lambda h: (which, 0, h))
-
-    gain_spec = pl.BlockSpec((1, HD), lambda h: (0, h))
+        return pl.BlockSpec((None, rows, cols), lambda i: (which, 0, 0))
+
+    gain_spec = pl.BlockSpec((1, cols), lambda i: (0, 0))
     return pl.pallas_call(
         functools.partial(attention_kernel, total_width, span, places),
-        grid=(heads,),
+        grid=(1,),
         in_specs=[pl.BlockSpec(memory_space=pltpu.SMEM), part(0), gain_spec, gain_spec]
         + [part(1)] * 3
         + [part(0)] * 3
         + [pl.BlockSpec(memory_space=pltpu.VMEM)] * len(squares),
-        out_specs=pl.BlockSpec((rows, HD), lambda h: (0, h)),
+        out_specs=pl.BlockSpec((rows, cols), lambda i: (0, 0)),
         out_shape=jax.ShapeDtypeStruct((rows, cols), BF16),
-        scratch_shapes=[pltpu.VMEM((4, rows, 1), F32)],
         compiler_params=params(),
         cost_estimate=cost(
             flops=12 * rows * rows * cols,
@@ -641,11 +651,14 @@
 
         halves_of = halves(w_query)
         sides = (jnp.concatenate([w_value, halves_of[0]]), jnp.concatenate([halves_of[1], w_key]))
-        firsts = [first_step(side) for side in sides]
+        firsts = [{m: exchange(side, m) for m in (2, 4)} for side in sides]
         early, late = [0, 1, 2, 4, 3, 5], [6, 7]
         early_indices, late_indices = indices(early), indices(late)
         small = (seen, place, early_indices, late_indices, *gain_rows)
         normed = modulated_norm(after(latents, *small), control, levels, modulation, owners)
+        firsts[0][4], firsts[1][2] = after(firsts[0][4], normed), after(firsts[1][2], normed)
+        for side, first in zip(sides, firsts):
+            first.update({0: side, 1: exchange(after(side, normed), 1)})
         share = out_shares(after(w_out, normed, firsts[0][4], firsts[1][2]))
         across = [
             exchange(after(firsts[0][4], normed, share), 2),

time: 258 us -> 257 us (level)
  Pallas kernels: 91.6 us -> 88.8 us
    pallas_call x2, Pallas kernels: 17 us -> 14.1 us  [attend(): pl.pallas_call(functools.partial(attention_kernel, total_width, span, pla...]
    unnamed x57 -> x59, local copies, waits for them, and re-layouts: 4.32 us -> 5.66 us
  transfers between devices with their start and end apart: 37 -> 37, of which waited for: 20 -> 19; matrix products, arithmetic and copies ran while one was open for 3% -> 3% of each run, Pallas kernels for 29% -> 28%
where the time goes in v2:
time: 257 us; the launch traced here: 256 us
  Pallas kernels  88.8 us (35%)
  waiting for transfers between devices  86.4 us (34%)
  starting transfers between devices  64.9 us (25%)
  local copies, waits for them, and re-layouts  11.7 us (5%)
  other arithmetic  3.83 us (1%)
    ppermute x19, waiting for transfers between devices, exchange(): return lax.ppermute(value, 'queue', [(i, i ^ bit) for i in range(peers)])  41.9 us
    pallas_call x2, Pallas kernels, project(): pl.pallas_call(functools.partial(project_kernel, layout, begun is not Non...  31.5 us
    ppermute x8, waiting for transfers between devices, move(): return lax.ppermute(moved, axis, pairs)  16.2 us
    pallas_call x2, Pallas kernels, attend(): pl.pallas_call(functools.partial(attention_kernel, total_width, span, pla...  14.1 us
    pallas_call x1, Pallas kernels, modulated_norm(): pl.pallas_call(norm_kernel, grid_spec=pltpu.PrefetchScalarGridSpec(num_sc...  13.9 us
    ppermute x8, starting transfers between devices, move(): return lax.ppermute(moved, axis, pairs)  13.4 us
    ppermute x19, starting transfers between devices, exchange(): return lax.ppermute(value, 'queue', [(i, i ^ bit) for i in range(peers)])  12.8 us
    ppermute x2, starting transfers between devices, along_line(): below[k] = above[k] = lax.ppermute(value, axis, pairs)  11.7 us
  transfers between devices with their start and end apart: 37, of which 19 were waited for; matrix products, arithmetic and copies ran while one was open for 3% of the time, Pallas kernels for 28%

profile of v2, /device:TPU:0, one launch (start us, length us, event | category | flops | bytes accessed | tf_op | source)
XLA Modules:
  0.0 256.2 jit_solution(13042413167635154052)
XLA Ops:
  0.0 1.3 fusion
  1.5 3.0 %collective-permute-start.1 = (bf16[960,640]{1,0:T(8,128)(2,1)S(1)}, bf16[960,640]{1,0:T(8,128)(2,1)}, u32[]{:S(2)}, u32[]{:S(2)}) collective-permute-start(bf16[960,640]{1,0:T(8,128)(2,1)S(1)} %pad_maximum_fusion.2.refs_3_), channel_id=1, source_target_pairs={{0,8},{4,12},{8,0},{12,4},{16,24},{20,28},{24,16},{28,20},{1,9},{5... | collective-permute-start | bytes 3686408 | tf_op jit(solution)/shard_map/ppermute | solution.py:64
  4.7 1.6 collective-permute-start
  10.6 13.9 %modulated_norm.1.refs_1_ = bf16[8,768,640]{2,1,0:T(8,128)(2,1)} custom-call(s32[2]{0:T(128)} %levels_ref.1, bf16[2,384,5120]{2,1,0:T(8,128)(2,1)} %latents_ref.4, bf16[2,384,5120]{2,1,0:T(8,128)(2,1)} %control_ref.5, f32[3,64,5120]{2,1,0:T(8,128)} %bitcast.20), custom_call_target="tpu_custom_call" | custom-call | flops 2457600 | bytes 1474560 | tf_op jit(solution)/shard_map/modulated_norm/pallas_call | solution.py:98
  24.5 8.0 %collective-permute-done.1.refs_7_ = bf16[960,640]{1,0:T(8,128)(2,1)} collective-permute-done((bf16[960,640]{1,0:T(8,128)(2,1)S(1)}, bf16[960,640]{1,0:T(8,128)(2,1)}, u32[]{:S(2)}, u32[]{:S(2)}) %collective-permute-start.1) | collective-permute-done | bytes 1228832 | tf_op jit(solution)/shard_map/ppermute | solution.py:64
  32.5 2.3 collective-permute-done.refs_8_
  34.8 4.4 %all-to-all-start = ((bf16[8,80,640]{2,1,0:T(8,128)(2,1)}), bf16[8,80,640]{2,1,0:T(8,128)(2,1)}, u32[]{:S(2)}, u32[]{:S(2)}) async-start(bf16[8,80,640]{2,1,0:T(8,128)(2,1)} %bitcast.13), calls=%async_computation | async-start | bytes 1638400 | tf_op jit(solution)/shard_map/all_to_all | solution.py:565
  39.2 19.6 %collective-permute-done.5.refs_6_ = bf16[960,640]{1,0:T(8,128)(2,1)} collective-permute-done((bf16[960,640]{1,0:T(8,128)(2,1)S(1)}, bf16[960,640]{1,0:T(8,128)(2,1)}, u32[]{:S(2)}, u32[]{:S(2)}) %collective-permute-start.5) | collective-permute-done | bytes 1228832 | tf_op jit(solution)/shard_map/ppermute | solution.py:64
  58.8 9.6 %all-to-all-done = bf16[8,80,640]{2,1,0:T(8,128)(2,1)} async-done(((bf16[8,80,640]{2,1,0:T(8,128)(2,1)}), bf16[8,80,640]{2,1,0:T(8,128)(2,1)}, u32[]{:S(2)}, u32[]{:S(2)}) %all-to-all-start) | async-done | bytes 819232 | tf_op jit(solution)/shard_map/all_to_all | solution.py:565
  69.3 1.7 collective-permute-start.11
  71.0 1.7 collective-permute-done.7.refs_10_
  74.3 20.9 %project_begin.1.refs_6_ = f32[768,1920]{1,0:T(8,128)} custom-call(s32[6]{0:T(128)} %stack.73.refs_0_, bf16[8,768,640]{2,1,0:T(8,128)(2,1)} %modulated_norm.1.refs_1_, bf16[960,640]{1,0:T(8,128)(2,1)} %copy-done.5, bf16[960,640]{1,0:T(8,128)(2,1)} %copy-done.4, bf16[960,640]{1,0:T(8,128)(2,1)} %collective-permute-done.3.refs_4_, ...), custom_call_target="tpu_custom_call" | custom-call | flops 707788800 | bytes 1658880 | tf_op jit(solution)/shard_map/project_begin/pallas_call | solution.py:203
  95.3 2.9 %collective-permute-done.2.refs_2_ = bf16[960,640]{1,0:T(8,128)(2,1)S(1)} collective-permute-done((bf16[960,640]{1,0:T(8,128)(2,1)}, bf16[960,640]{1,0:T(8,128)(2,1)S(1)}, u32[]{:S(2)}, u32[]{:S(2)}) %collective-permute-start.2) | collective-permute-done | bytes 1228832 | tf_op jit(solution)/shard_map/ppermute | solution.py:64
  98.8 3.6 %collective-permute-done.12.refs_4_ = bf16[960,640]{1,0:T(8,128)(2,1)S(1)} collective-permute-done((bf16[960,640]{1,0:T(8,128)(2,1)S(1)}, bf16[960,640]{1,0:T(8,128)(2,1)S(1)}, u32[]{:S(2)}, u32[]{:S(2)}) %collective-permute-start.12) | collective-permute-done | bytes 1228832 | tf_op jit(solution)/shard_map/ppermute | solution.py:64
  103.4 10.6 %project_final.1 = (bf16[2,384,640]{2,1,0:T(8,128)(2,1)}, bf16[2,384,640]{2,1,0:T(8,128)(2,1)}, bf16[1,384,640]{2,1,0:T(8,128)(2,1)}, bf16[1,384,640]{2,1,0:T(8,128)(2,1)}, f32[2,6,128]{2,1,0:T(8,128)}) custom-call(s32[2]{0:T(128)} %pad_add_fusion.1.refs_0_, bf16[8,768,640]{2,1,0:T(8,128)(2,1)} %modulated_norm.1.refs_1_, bf16[960,640]{1,0:T(8,128)(2,1)} %copy-done.10, ...), custom_call_target="tpu_custom_call" | custom-call | flops 235929600 | bytes 798720 | tf_op jit(solution)/shard_map/project_final/pallas_call | solution.py:203
  114.0 2.0 collective-permute-start.14
  117.1 5.6 %all-to-all-start.1 = ((bf16[8,80,640]{2,1,0:T(8,128)(2,1)}), bf16[8,80,640]{2,1,0:T(8,128)(2,1)S(1)}, u32[]{:S(2)}, u32[]{:S(2)}) async-start(bf16[8,80,640]{2,1,0:T(8,128)(2,1)} %all-to-all-done), calls=%async_computation.1 | async-start | bytes 1638400 | tf_op jit(solution)/shard_map/all_to_all | solution.py:571
  122.6 3.1 %collective-permute-start.18 = (bf16[2,384,640]{2,1,0:T(8,128)(2,1)}, bf16[2,384,640]{2,1,0:T(8,128)(2,1)S(1)}, u32[]{:S(2)}, u32[]{:S(2)}) collective-permute-start(bf16[2,384,640]{2,1,0:T(8,128)(2,1)} %get-tuple-element.46.k2.v2), channel_id=1, source_target_pairs={{0,4},{4,8},{8,12},{12,16},{16,20},{20,24},{24,28},{1,5},{5,9},{9,... | collective-permute-start | bytes 2949128 | tf_op jit(solution)/shard_map/ppermute | solution.py:33
  125.8 4.7 %collective-permute-start.21 = (bf16[2,384,640]{2,1,0:T(8,128)(2,1)}, bf16[2,384,640]{2,1,0:T(8,128)(2,1)S(1)}, u32[]{:S(2)}, u32[]{:S(2)}) collective-permute-start(bf16[2,384,640]{2,1,0:T(8,128)(2,1)} %get-tuple-element.47.k1.v1.k2.v2), channel_id=1, source_target_pairs={{0,4},{4,8},{8,12},{12,16},{16,20},{20,24},{24,28},{1,5},{5,9},{9,... | collective-permute-start | bytes 2949128 | tf_op jit(solution)/shard_map/ppermute | solution.py:33
  131.2 2.0 collective-permute-start.15
  133.2 3.9 %collective-permute-done.15 = f32[4,6,128]{2,1,0:T(8,128)S(1)} collective-permute-done((f32[4,6,128]{2,1,0:T(8,128)S(1)}, f32[4,6,128]{2,1,0:T(8,128)S(1)}, u32[]{:S(2)}, u32[]{:S(2)}) %collective-permute-start.15) | collective-permute-done | bytes 12320 | tf_op jit(solution)/shard_map/ppermute | solution.py:53
  137.1 5.1 %collective-permute-start.16 = (f32[4,6,128]{2,1,0:T(8,128)S(1)}, f32[4,6,128]{2,1,0:T(8,128)S(1)}, u32[]{:S(2)}, u32[]{:S(2)}) collective-permute-start(f32[4,6,128]{2,1,0:T(8,128)S(1)} %add.15.refs_0_), channel_id=1, source_target_pairs={{0,2},{1,3},{2,0},{3,1},{4,6},{5,7},{6,4},{7,5},{8,10},{9,11},{10,... | collective-permute-start | bytes 36872 | tf_op jit(solution)/shard_map/ppermute | solution.py:53
  142.2 3.2 %collective-permute-done.16.refs_1_ = f32[4,6,128]{2,1,0:T(8,128)S(1)} collective-permute-done((f32[4,6,128]{2,1,0:T(8,128)S(1)}, f32[4,6,128]{2,1,0:T(8,128)S(1)}, u32[]{:S(2)}, u32[]{:S(2)}) %collective-permute-start.16) | collective-permute-done | bytes 12320 | tf_op jit(solution)/shard_map/ppermute | solution.py:53
  145.4 1.9 collective-permute-start.17
  148.7 7.0 %attend.2.refs_0_ = bf16[384,640]{1,0:T(8,128)(2,1)} custom-call(s32[2,2]{1,0:T(2,128)} %and_convert_fusion.seen_ref, bf16[1,384,640]{2,1,0:T(8,128)(2,1)} %get-tuple-element.45.q_ref, f32[1,640]{1,0:T(1,128)} %reshape.21.q_gain_ref, f32[1,640]{1,0:T(1,128)} %reshape.22.k_gain_ref, bf16[2,384,640]{2,1,0:T(8,128)(2,1)} %copy-done, ...), custom_call_target="tpu_custom_call" | custom-call | flops 70778880 | bytes 245760 | tf_op jit(solution)/shard_map/attend/pallas_call | solution.py:297
  155.7 1.3 collective-permute-start.19
  157.0 1.3 collective-permute-start.20
  158.3 6.4 %collective-permute-start.25 = (bf16[384,640]{1,0:T(8,128)(2,1)}, bf16[384,640]{1,0:T(8,128)(2,1)S(1)}, u32[]{:S(2)}, u32[]{:S(2)}) collective-permute-start(bf16[384,640]{1,0:T(8,128)(2,1)} %attend.2.refs_0_), channel_id=1, source_target_pairs={{0,3},{3,0},{4,7},{7,4},{8,11},{11,8},{12,15},{15,12},{16,19},{19,... | collective-permute-start | bytes 1474568 | tf_op jit(solution)/shard_map/ppermute | solution.py:330
  164.8 4.2 %collective-permute-done.19.refs_1_ = bf16[384,640]{1,0:T(8,128)(2,1)S(1)} collective-permute-done((bf16[384,640]{1,0:T(8,128)(2,1)}, bf16[384,640]{1,0:T(8,128)(2,1)S(1)}, u32[]{:S(2)}, u32[]{:S(2)}) %collective-permute-start.19) | collective-permute-done | bytes 491552 | tf_op jit(solution)/shard_map/ppermute | solution.py:323
  169.7 4.7 %collective-permute-done.20.refs_4_ = bf16[384,640]{1,0:T(8,128)(2,1)S(1)} collective-permute-done((bf16[384,640]{1,0:T(8,128)(2,1)}, bf16[384,640]{1,0:T(8,128)(2,1)S(1)}, u32[]{:S(2)}, u32[]{:S(2)}) %collective-permute-start.20) | collective-permute-done | bytes 491552 | tf_op jit(solution)/shard_map/ppermute | solution.py:323
  174.4 1.3 collective-permute-start.26
  175.7 7.0 %attend.3.refs_0_.refs_2_.refs_5_ = bf16[384,640]{1,0:T(8,128)(2,1)} custom-call(s32[2,2]{1,0:T(2,128)} %and_convert_fusion.seen_ref, bf16[1,384,640]{2,1,0:T(8,128)(2,1)} %get-tuple-element.48.q_ref, f32[1,640]{1,0:T(1,128)} %reshape.21.q_gain_ref, f32[1,640]{1,0:T(1,128)} %reshape.22.k_gain_ref, bf16[2,384,640]{2,1,0:T(8,128)(2,1)} %copy-done.6, ...), custom_call_target="tpu_custom_call" | custom-call | flops 70778880 | bytes 245760 | tf_op jit(solution)/shard_map/attend/pallas_call | solution.py:297
  182.8 1.1 slice.15
  183.9 1.3 collective-permute-start.27
  185.2 1.0 slice.14
  187.1 4.8 %collective-permute-done.26.refs_5_ = bf16[384,640]{1,0:T(8,128)(2,1)} collective-permute-done((bf16[384,640]{1,0:T(8,128)(2,1)S(1)}, bf16[384,640]{1,0:T(8,128)(2,1)}, u32[]{:S(2)}, u32[]{:S(2)}) %collective-permute-start.26) | collective-permute-done | bytes 491552 | tf_op jit(solution)/shard_map/ppermute | solution.py:323
  191.9 2.3 collective-permute-done.23
  194.4 1.7 pad_maximum_fusion.refs_0_
  196.9 5.3 %collective-permute-start.30 = (bf16[384,640]{1,0:T(8,128)(2,1)}, bf16[384,640]{1,0:T(8,128)(2,1)}, u32[]{:S(2)}, u32[]{:S(2)}) collective-permute-start(bf16[384,640]{1,0:T(8,128)(2,1)} %attend.3.refs_0_.refs_2_.refs_5_), channel_id=1, source_target_pairs={{0,1},{1,2},{2,3},{4,5},{5,6},{6,7},{8,9},{9,10},{10,11},{12,13},{... | collective-permute-start | bytes 1474568 | tf_op jit(solution)/shard_map/ppermute | solution.py:323
  202.2 1.5 collective-permute-start.32
  203.8 6.9 %assemble.1.weight_ref = bf16[4,640,1280]{2,1,0:T(8,128)(2,1)} custom-call(s32[8]{0:T(128)} %stack.70.index_ref, bf16[4,4,2,80,640]{4,3,2,1,0:T(8,128)(2,1)} %copy-done.1, bf16[4,4,2,80,640]{4,3,2,1,0:T(8,128)(2,1)} %collective-permute-done.28.refs_1_), custom_call_target="tpu_custom_call" | custom-call | bytes 819200 | tf_op jit(solution)/shard_map/assemble/pallas_call | solution.py:598
  210.7 8.6 %update_last.1 = bf16[384,1280]{1,0:T(8,128)(2,1)} custom-call(s32[3]{0:T(128)} %pad_add_fusion.place_ref, bf16[4,640,1280]{2,1,0:T(8,128)(2,1)} %assemble.1.weight_ref, bf16[2,384,5120]{2,1,0:T(8,128)(2,1)} %latents_ref.4, bf16[2,384,5120]{2,1,0:T(8,128)(2,1)} %control_ref.5, f32[3,64,5120]{2,1,0:T(8,128)} %bitcast.21, bf16[384,640]{1,0:T(8,128)(2,1)} %attend.2.refs_0_, ...), custom_call_target="tpu_custom_call" | custom-call | flops 157286400 | bytes 778240 | tf_op jit(solution)/shard_map/update_last/pallas_call | solution.py:504
  219.4 5.2 %collective-permute-start.31 = (bf16[384,640]{1,0:T(8,128)(2,1)S(1)}, bf16[384,640]{1,0:T(8,128)(2,1)S(1)}, u32[]{:S(2)}, u32[]{:S(2)}) collective-permute-start(bf16[384,640]{1,0:T(8,128)(2,1)S(1)} %copy-done.2), channel_id=1, source_target_pairs={{0,3},{3,0},{4,7},{7,4},{8,11},{11,8},{12,15},{15,12},{16,19},{19,... | collective-permute-start | bytes 1474568 | tf_op jit(solution)/shard_map/ppermute | solution.py:330
  225.4 1.3 collective-permute-start.34
  226.7 10.5 %collective-permute-done.31.refs_3_.refs_6_ = bf16[384,640]{1,0:T(8,128)(2,1)S(1)} collective-permute-done((bf16[384,640]{1,0:T(8,128)(2,1)S(1)}, bf16[384,640]{1,0:T(8,128)(2,1)S(1)}, u32[]{:S(2)}, u32[]{:S(2)}) %collective-permute-start.31) | collective-permute-done | bytes 491552 | tf_op jit(solution)/shard_map/ppermute | solution.py:330
  238.0 7.1 %update_begin.1.begun_ref = f32[1,384,1280]{2,1,0:T(8,128)} custom-call(s32[3]{0:T(128)} %pad_add_fusion.place_ref, bf16[4,640,1280]{2,1,0:T(8,128)(2,1)} %assemble.1.weight_ref, bf16[384,640]{1,0:T(8,128)(2,1)} %attend.3.refs_0_.refs_2_.refs_5_, bf16[384,640]{1,0:T(8,128)(2,1)} %collective-permute-done.30.refs_1_, ...), custom_call_target="tpu_custom_call" | custom-call | flops 117964800 | bytes 645120 | tf_op jit(solution)/shard_map/update_begin/pallas_call | solution.py:520
  245.1 2.5 collective-permute-done.34.refs_5_
  249.3 6.7 %update_rest.1 = f32[2,384,1280]{2,1,0:T(8,128)} custom-call(s32[3]{0:T(128)} %pad_add_fusion.place_ref, bf16[384,1280]{1,0:T(8,128)(2,1)} %copy-done.14, f32[1,384,1280]{2,1,0:T(8,128)} %update_begin.1.begun_ref, bf16[4,640,1280]{2,1,0:T(8,128)(2,1)} %assemble.1.weight_ref, bf16[2,384,5120]{2,1,0:T(8,128)(2,1)} %latents_ref.4, ...), custom_call_target="tpu_custom_call" | custom-call | flops 39321600 | bytes 378880 | tf_op jit(solution)/shard_map/update_rest/pallas_call | solution.py:544
  (111 shorter events, 17.6 us)
Async XLA Ops:
  1.4 8.6 %copy-start.26 = (s32[2,2]{1,0:T(2,128)S(1)}, s32[2,2]{1,0:T(2,128)}, u32[]{:S(2)}) copy-start(s32[2,2]{1,0:T(2,128)} %param.15) | copy-start | bytes 52
  1.4 8.6 %copy-start.28 = (s32[2]{0:T(128)S(1)}, s32[2]{0:T(128)}, u32[]{:S(2)}) copy-start(s32[2]{0:T(128)} %constant.26.clone) | copy-start | bytes 28
  1.5 31.0 %copy-start.4 = (bf16[960,640]{1,0:T(8,128)(2,1)}, bf16[960,640]{1,0:T(8,128)(2,1)S(1)}, u32[]{:S(2)}) copy-start(bf16[960,640]{1,0:T(8,128)(2,1)S(1)} %pad_maximum_fusion.2.refs_3_) | copy-start | bytes 3686404
  1.5 31.0 %collective-permute-start.1 = (bf16[960,640]{1,0:T(8,128)(2,1)S(1)}, bf16[960,640]{1,0:T(8,128)(2,1)}, u32[]{:S(2)}, u32[]{:S(2)}) collective-permute-start(bf16[960,640]{1,0:T(8,128)(2,1)S(1)} %pad_maximum_fusion.2.refs_3_), channel_id=1, source_target_pairs={{0,8},{4,12},{8,0},{12,4},{16,24},{20,28},{24,16},{28,20},{1,9},{5... | collective-permute-start | bytes 3686408 | tf_op jit(solution)/shard_map/ppermute | solution.py:64
  4.7 19.8 %copy-start.5 = (bf16[960,640]{1,0:T(8,128)(2,1)}, bf16[960,640]{1,0:T(8,128)(2,1)S(1)}, u32[]{:S(2)}) copy-start(bf16[960,640]{1,0:T(8,128)(2,1)S(1)} %pad_maximum_fusion.1.refs_2_) | copy-start | bytes 3686404
  4.7 30.1 %collective-permute-start = (bf16[960,640]{1,0:T(8,128)(2,1)S(1)}, bf16[960,640]{1,0:T(8,128)(2,1)}, u32[]{:S(2)}, u32[]{:S(2)}) collective-permute-start(bf16[960,640]{1,0:T(8,128)(2,1)S(1)} %pad_maximum_fusion.1.refs_2_), channel_id=1, source_target_pairs={{0,16},{4,20},{8,24},{12,28},{16,0},{20,4},{24,8},{28,12},{1,17},{... | collective-permute-start | bytes 3686408 | tf_op jit(solution)/shard_map/ppermute | solution.py:64
  6.3 52.6 %collective-permute-start.5 = (bf16[960,640]{1,0:T(8,128)(2,1)S(1)}, bf16[960,640]{1,0:T(8,128)(2,1)}, u32[]{:S(2)}, u32[]{:S(2)}) collective-permute-start(bf16[960,640]{1,0:T(8,128)(2,1)S(1)} %pad_maximum_fusion.1.refs_2_), channel_id=1, source_target_pairs={{0,8},{4,12},{8,0},{12,4},{16,24},{20,28},{24,16},{28,20},{1,9},{5... | collective-permute-start | bytes 3686408 | tf_op jit(solution)/shard_map/ppermute | solution.py:64
  6.8 61.6 %collective-permute-start.6 = (bf16[960,640]{1,0:T(8,128)(2,1)S(1)}, bf16[960,640]{1,0:T(8,128)(2,1)}, u32[]{:S(2)}, u32[]{:S(2)}) collective-permute-start(bf16[960,640]{1,0:T(8,128)(2,1)S(1)} %pad_maximum_fusion.2.refs_3_), channel_id=1, source_target_pairs={{0,16},{4,20},{8,24},{12,28},{16,0},{20,4},{24,8},{28,12},{1,17},{... | collective-permute-start | bytes 3686408 | tf_op jit(solution)/shard_map/ppermute | solution.py:64
  24.5 44.0 %collective-permute-start.3 = (bf16[960,640]{1,0:T(8,128)(2,1)S(1)}, bf16[960,640]{1,0:T(8,128)(2,1)}, u32[]{:S(2)}, u32[]{:S(2)}) collective-permute-start(bf16[960,640]{1,0:T(8,128)(2,1)S(1)} %pad_maximum_fusion.1.refs_2_), channel_id=1, source_target_pairs={{0,4},{4,0},{8,12},{12,8},{16,20},{20,16},{24,28},{28,24},{1,5},{5... | collective-permute-start | bytes 3686408 | tf_op jit(solution)/shard_map/ppermute | solution.py:64
  32.5 36.5 %collective-permute-start.4 = (bf16[960,640]{1,0:T(8,128)(2,1)S(1)}, bf16[960,640]{1,0:T(8,128)(2,1)}, u32[]{:S(2)}, u32[]{:S(2)}) collective-permute-start(bf16[960,640]{1,0:T(8,128)(2,1)S(1)} %pad_maximum_fusion.2.refs_3_), channel_id=1, source_target_pairs={{0,4},{4,0},{8,12},{12,8},{16,20},{20,16},{24,28},{28,24},{1,5},{5... | collective-permute-start | bytes 3686408 | tf_op jit(solution)/shard_map/ppermute | solution.py:64
  34.8 34.5 %collective-permute-start.8 = (bf16[960,640]{1,0:T(8,128)(2,1)}, bf16[960,640]{1,0:T(8,128)(2,1)}, u32[]{:S(2)}, u32[]{:S(2)}) collective-permute-start(bf16[960,640]{1,0:T(8,128)(2,1)} %collective-permute-done.1.refs_7_), channel_id=1, source_target_pairs={{0,4},{4,0},{8,12},{12,8},{16,20},{20,16},{24,28},{28,24},{1,5},{5... | collective-permute-start | bytes 3686408 | tf_op jit(solution)/shard_map/ppermute | solution.py:64
  34.8 33.6 %all-to-all-start = ((bf16[8,80,640]{2,1,0:T(8,128)(2,1)}), bf16[8,80,640]{2,1,0:T(8,128)(2,1)}, u32[]{:S(2)}, u32[]{:S(2)}) async-start(bf16[8,80,640]{2,1,0:T(8,128)(2,1)} %bitcast.13), calls=%async_computation | async-start | bytes 1638400 | tf_op jit(solution)/shard_map/all_to_all | solution.py:565
  58.8 12.2 %collective-permute-start.9 = (bf16[960,640]{1,0:T(8,128)(2,1)}, bf16[960,640]{1,0:T(8,128)(2,1)}, u32[]{:S(2)}, u32[]{:S(2)}) collective-permute-start(bf16[960,640]{1,0:T(8,128)(2,1)} %collective-permute-done.refs_8_), channel_id=1, source_target_pairs={{0,4},{4,0},{8,12},{12,8},{16,20},{20,16},{24,28},{28,24},{1,5},{5... | collective-permute-start | bytes 3686408 | tf_op jit(solution)/shard_map/ppermute | solution.py:64
  68.4 4.3 %collective-permute-start.7 = (bf16[960,640]{1,0:T(8,128)(2,1)}, bf16[960,640]{1,0:T(8,128)(2,1)}, u32[]{:S(2)}, u32[]{:S(2)}) collective-permute-start(bf16[960,640]{1,0:T(8,128)(2,1)} %collective-permute-done.5.refs_6_), channel_id=1, source_target_pairs={{0,4},{4,0},{8,12},{12,8},{16,20},{20,16},{24,28},{28,24},{1,5},{5... | collective-permute-start | bytes 3686408 | tf_op jit(solution)/shard_map/ppermute | solution.py:64
  68.4 4.9 %collective-permute-start.10 = (bf16[960,640]{1,0:T(8,128)(2,1)}, bf16[960,640]{1,0:T(8,128)(2,1)S(1)}, u32[]{:S(2)}, u32[]{:S(2)}) collective-permute-start(bf16[960,640]{1,0:T(8,128)(2,1)} %collective-permute-done.6.refs_9_), channel_id=1, source_target_pairs={{0,4},{4,0},{8,12},{12,8},{16,20},{20,16},{24,28},{28,24},{1,5},{5... | collective-permute-start | bytes 3686408 | tf_op jit(solution)/shard_map/ppermute | solution.py:64
  69.0 29.2 %collective-permute-start.2 = (bf16[960,640]{1,0:T(8,128)(2,1)}, bf16[960,640]{1,0:T(8,128)(2,1)S(1)}, u32[]{:S(2)}, u32[]{:S(2)}) collective-permute-start(bf16[960,640]{1,0:T(8,128)(2,1)} %collective-permute-done.refs_8_), channel_id=1, source_target_pairs={{0,8},{4,12},{8,0},{12,4},{16,24},{20,28},{24,16},{28,20},{1,9},{5... | collective-permute-start | bytes 3686408 | tf_op jit(solution)/shard_map/ppermute | solution.py:64
  69.3 29.0 %collective-permute-start.11 = (bf16[960,640]{1,0:T(8,128)(2,1)}, bf16[960,640]{1,0:T(8,128)(2,1)S(1)}, u32[]{:S(2)}, u32[]{:S(2)}) collective-permute-start(bf16[960,640]{1,0:T(8,128)(2,1)} %collective-permute-done.1.refs_7_), channel_id=1, source_target_pairs={{0,16},{4,20},{8,24},{12,28},{16,0},{20,4},{24,8},{28,12},{1,17},{... | collective-permute-start | bytes 3686408 | tf_op jit(solution)/shard_map/ppermute | solution.py:64
  98.3 4.1 %collective-permute-start.12 = (bf16[960,640]{1,0:T(8,128)(2,1)S(1)}, bf16[960,640]{1,0:T(8,128)(2,1)S(1)}, u32[]{:S(2)}, u32[]{:S(2)}) collective-permute-start(bf16[960,640]{1,0:T(8,128)(2,1)S(1)} %collective-permute-done.2.refs_2_), channel_id=1, source_target_pairs={{0,4},{4,0},{8,12},{12,8},{16,20},{20,16},{24,28},{28,24},{1,5},{5... | collective-permute-start | bytes 3686408 | tf_op jit(solution)/shard_map/ppermute | solution.py:64
  98.3 4.8 %collective-permute-start.13 = (bf16[960,640]{1,0:T(8,128)(2,1)S(1)}, bf16[960,640]{1,0:T(8,128)(2,1)}, u32[]{:S(2)}, u32[]{:S(2)}) collective-permute-start(bf16[960,640]{1,0:T(8,128)(2,1)S(1)} %collective-permute-done.11.refs_3_), channel_id=1, source_target_pairs={{0,4},{4,0},{8,12},{12,8},{16,20},{20,16},{24,28},{28,24},{1,5},{5... | collective-permute-start | bytes 3686408 | tf_op jit(solution)/shard_map/ppermute | solution.py:64
  114.0 3.1 %collective-permute-start.14 = (f32[2,6,128]{2,1,0:T(8,128)}, f32[2,6,128]{2,1,0:T(8,128)S(1)}, u32[]{:S(2)}, u32[]{:S(2)}) collective-permute-start(f32[2,6,128]{2,1,0:T(8,128)} %get-tuple-element.41), channel_id=1, source_target_pairs={{0,4},{4,8},{8,12},{12,16},{16,20},{20,24},{24,28},{1,5},{5,9},{9,... | collective-permute-start | bytes 18440 | tf_op jit(solution)/shard_map/ppermute | solution.py:33
  117.1 28.3 %all-to-all-start.1 = ((bf16[8,80,640]{2,1,0:T(8,128)(2,1)}), bf16[8,80,640]{2,1,0:T(8,128)(2,1)S(1)}, u32[]{:S(2)}, u32[]{:S(2)}) async-start(bf16[8,80,640]{2,1,0:T(8,128)(2,1)} %all-to-all-done), calls=%async_computation.1 | async-start | bytes 1638400 | tf_op jit(solution)/shard_map/all_to_all | solution.py:571
  122.6 25.1 %collective-permute-start.18 = (bf16[2,384,640]{2,1,0:T(8,128)(2,1)}, bf16[2,384,640]{2,1,0:T(8,128)(2,1)S(1)}, u32[]{:S(2)}, u32[]{:S(2)}) collective-permute-start(bf16[2,384,640]{2,1,0:T(8,128)(2,1)} %get-tuple-element.46.k2.v2), channel_id=1, source_target_pairs={{0,4},{4,8},{8,12},{12,16},{16,20},{20,24},{24,28},{1,5},{5,9},{9,... | collective-permute-start | bytes 2949128 | tf_op jit(solution)/shard_map/ppermute | solution.py:33
  125.8 32.6 %collective-permute-start.21 = (bf16[2,384,640]{2,1,0:T(8,128)(2,1)}, bf16[2,384,640]{2,1,0:T(8,128)(2,1)S(1)}, u32[]{:S(2)}, u32[]{:S(2)}) collective-permute-start(bf16[2,384,640]{2,1,0:T(8,128)(2,1)} %get-tuple-element.47.k1.v1.k2.v2), channel_id=1, source_target_pairs={{0,4},{4,8},{8,12},{12,16},{16,20},{20,24},{24,28},{1,5},{5,9},{9,... | collective-permute-start | bytes 2949128 | tf_op jit(solution)/shard_map/ppermute | solution.py:33
  131.2 5.9 %collective-permute-start.15 = (f32[4,6,128]{2,1,0:T(8,128)S(1)}, f32[4,6,128]{2,1,0:T(8,128)S(1)}, u32[]{:S(2)}, u32[]{:S(2)}) collective-permute-start(f32[4,6,128]{2,1,0:T(8,128)S(1)} %constant_dynamic-update-slice_fusion), channel_id=1, source_target_pairs={{0,1},{1,0},{2,3},{3,2},{4,5},{5,4},{6,7},{7,6},{8,9},{9,8},{10,11... | collective-permute-start | bytes 36872 | tf_op jit(solution)/shard_map/ppermute | solution.py:53
  137.1 10.6 %copy-start.22 = (f32[4,6,128]{2,1,0:T(8,128)}, f32[4,6,128]{2,1,0:T(8,128)S(1)}, u32[]{:S(2)}) copy-start(f32[4,6,128]{2,1,0:T(8,128)S(1)} %add.15.refs_0_) | copy-start | bytes 36868
  137.1 8.3 %collective-permute-start.16 = (f32[4,6,128]{2,1,0:T(8,128)S(1)}, f32[4,6,128]{2,1,0:T(8,128)S(1)}, u32[]{:S(2)}, u32[]{:S(2)}) collective-permute-start(f32[4,6,128]{2,1,0:T(8,128)S(1)} %add.15.refs_0_), channel_id=1, source_target_pairs={{0,2},{1,3},{2,0},{3,1},{4,6},{5,7},{6,4},{7,5},{8,10},{9,11},{10,... | collective-permute-start | bytes 36872 | tf_op jit(solution)/shard_map/ppermute | solution.py:53
  145.4 37.4 %copy-start.7 = (bf16[8,80,640]{2,1,0:T(8,128)(2,1)}, bf16[8,80,640]{2,1,0:T(8,128)(2,1)S(1)}, u32[]{:S(2)}) copy-start(bf16[8,80,640]{2,1,0:T(8,128)(2,1)S(1)} %all-to-all-done.1) | copy-start | bytes 2457604
  145.4 37.4 %collective-permute-start.17 = (bf16[4,2,80,640]{3,2,1,0:T(8,128)(2,1)S(1)}, bf16[4,2,80,640]{3,2,1,0:T(8,128)(2,1)}, u32[]{:S(2)}, u32[]{:S(2)}) collective-permute-start(bf16[4,2,80,640]{3,2,1,0:T(8,128)(2,1)S(1)} %bitcast.23), channel_id=1, source_target_pairs={{0,8},{4,12},{8,0},{12,4},{16,24},{20,28},{24,16},{28,20},{1,9},{5... | collective-permute-start | bytes 2457608 | tf_op jit(solution)/shard_map/ppermute | solution.py:64
  147.3 37.9 %collective-permute-start.22 = (bf16[4,2,80,640]{3,2,1,0:T(8,128)(2,1)S(1)}, bf16[4,2,80,640]{3,2,1,0:T(8,128)(2,1)}, u32[]{:S(2)}, u32[]{:S(2)}) collective-permute-start(bf16[4,2,80,640]{3,2,1,0:T(8,128)(2,1)S(1)} %bitcast.24), channel_id=1, source_target_pairs={{0,16},{4,20},{8,24},{12,28},{16,0},{20,4},{24,8},{28,12},{1,17},{... | collective-permute-start | bytes 2457608 | tf_op jit(solution)/shard_map/ppermute | solution.py:64
  155.7 13.3 %collective-permute-start.19 = (bf16[384,640]{1,0:T(8,128)(2,1)}, bf16[384,640]{1,0:T(8,128)(2,1)S(1)}, u32[]{:S(2)}, u32[]{:S(2)}) collective-permute-start(bf16[384,640]{1,0:T(8,128)(2,1)} %attend.2.refs_0_), channel_id=1, source_target_pairs={{0,1},{1,2},{2,3},{4,5},{5,6},{6,7},{8,9},{9,10},{10,11},{12,13},{... | collective-permute-start | bytes 1474568 | tf_op jit(solution)/shard_map/ppermute | solution.py:323
  157.0 17.4 %collective-permute-start.20 = (bf16[384,640]{1,0:T(8,128)(2,1)}, bf16[384,640]{1,0:T(8,128)(2,1)S(1)}, u32[]{:S(2)}, u32[]{:S(2)}) collective-permute-start(bf16[384,640]{1,0:T(8,128)(2,1)} %attend.2.refs_0_), channel_id=1, source_target_pairs={{1,0},{2,1},{3,2},{5,4},{6,5},{7,6},{9,8},{10,9},{11,10},{13,12},{... | collective-permute-start | bytes 1474568 | tf_op jit(solution)/shard_map/ppermute | solution.py:323
  158.3 17.3 %copy-start.6 = (bf16[2,384,640]{2,1,0:T(8,128)(2,1)}, bf16[2,384,640]{2,1,0:T(8,128)(2,1)S(1)}, u32[]{:S(2)}) copy-start(bf16[2,384,640]{2,1,0:T(8,128)(2,1)S(1)} %collective-permute-done.21.k0.v0) | copy-start | bytes 2949124
  158.3 28.7 %collective-permute-start.25 = (bf16[384,640]{1,0:T(8,128)(2,1)}, bf16[384,640]{1,0:T(8,128)(2,1)S(1)}, u32[]{:S(2)}, u32[]{:S(2)}) collective-permute-start(bf16[384,640]{1,0:T(8,128)(2,1)} %attend.2.refs_0_), channel_id=1, source_target_pairs={{0,3},{3,0},{4,7},{7,4},{8,11},{11,8},{12,15},{15,12},{16,19},{19,... | collective-permute-start | bytes 1474568 | tf_op jit(solution)/shard_map/ppermute | solution.py:330
  169.0 13.8 %copy-start.17 = (bf16[384,640]{1,0:T(8,128)(2,1)}, bf16[384,640]{1,0:T(8,128)(2,1)S(1)}, u32[]{:S(2)}) copy-start(bf16[384,640]{1,0:T(8,128)(2,1)S(1)} %collective-permute-done.19.refs_1_) | copy-start | bytes 1474564
  169.0 18.1 %collective-permute-start.24 = (bf16[384,640]{1,0:T(8,128)(2,1)S(1)}, bf16[384,640]{1,0:T(8,128)(2,1)S(1)}, u32[]{:S(2)}, u32[]{:S(2)}) collective-permute-start(bf16[384,640]{1,0:T(8,128)(2,1)S(1)} %collective-permute-done.19.refs_1_), channel_id=1, source_target_pairs={{1,2},{2,3},{5,6},{6,7},{9,10},{10,11},{13,14},{14,15},{17,18},{18... | collective-permute-start | bytes 1474568 | tf_op jit(solution)/shard_map/ppermute | solution.py:323
  174.4 17.5 %collective-permute-start.26 = (bf16[384,640]{1,0:T(8,128)(2,1)S(1)}, bf16[384,640]{1,0:T(8,128)(2,1)}, u32[]{:S(2)}, u32[]{:S(2)}) collective-permute-start(bf16[384,640]{1,0:T(8,128)(2,1)S(1)} %collective-permute-done.20.refs_4_), channel_id=1, source_target_pairs={{1,0},{2,1},{5,4},{6,5},{9,8},{10,9},{13,12},{14,13},{17,16},{18,1... | collective-permute-start | bytes 1474568 | tf_op jit(solution)/shard_map/ppermute | solution.py:323
  182.8 11.6 %copy-start.8 = (bf16[8,80,640]{2,1,0:T(8,128)(2,1)S(1)}, bf16[8,80,640]{2,1,0:T(8,128)(2,1)}, u32[]{:S(2)}) copy-start(bf16[8,80,640]{2,1,0:T(8,128)(2,1)} %copy-done.7) | copy-start | bytes 2457604
  183.9 8.0 %collective-permute-start.27 = (bf16[2,2,80,640]{3,2,1,0:T(8,128)(2,1)S(1)}, bf16[2,2,80,640]{3,2,1,0:T(8,128)(2,1)S(1)}, u32[]{:S(2)}, u32[]{:S(2)}) collective-permute-start(bf16[2,2,80,640]{3,2,1,0:T(8,128)(2,1)S(1)} %slice.15), channel_id=1, source_target_pairs={{0,16},{4,20},{8,24},{12,28},{16,0},{20,4},{24,8},{28,12},{1,17},{... | collective-permute-start | bytes 1228808 | tf_op jit(solution)/shard_map/ppermute | solution.py:64
  186.2 8.0 %collective-permute-start.23 = (bf16[2,2,80,640]{3,2,1,0:T(8,128)(2,1)S(1)}, bf16[2,2,80,640]{3,2,1,0:T(8,128)(2,1)S(1)}, u32[]{:S(2)}, u32[]{:S(2)}) collective-permute-start(bf16[2,2,80,640]{3,2,1,0:T(8,128)(2,1)S(1)} %slice.14), channel_id=1, source_target_pairs={{0,8},{4,12},{8,0},{12,4},{16,24},{20,28},{24,16},{28,20},{1,9},{5... | collective-permute-start | bytes 1228808 | tf_op jit(solution)/shard_map/ppermute | solution.py:64
  187.1 9.0 %copy-start.9 = (bf16[384,640]{1,0:T(8,128)(2,1)}, bf16[384,640]{1,0:T(8,128)(2,1)S(1)}, u32[]{:S(2)}) copy-start(bf16[384,640]{1,0:T(8,128)(2,1)S(1)} %collective-permute-done.25.refs_3_.refs_6_) | copy-start | bytes 1474564
  196.1 7.7 %collective-permute-start.28 = (bf16[4,4,2,80,640]{4,3,2,1,0:T(8,128)(2,1)S(1)}, bf16[4,4,2,80,640]{4,3,2,1,0:T(8,128)(2,1)}, u32[]{:S(2)}, u32[]{:S(2)}) collective-permute-start(bf16[4,4,2,80,640]{4,3,2,1,0:T(8,128)(2,1)S(1)} %pad_maximum_fusion.refs_0_), channel_id=1, source_target_pairs={{0,4},{4,0},{8,12},{12,8},{16,20},{20,16},{24,28},{28,24},{1,5},{5... | collective-permute-start | bytes 9830408 | tf_op jit(solution)/shard_map/ppermute | solution.py:64
  196.9 27.7 %collective-permute-start.30 = (bf16[384,640]{1,0:T(8,128)(2,1)}, bf16[384,640]{1,0:T(8,128)(2,1)}, u32[]{:S(2)}, u32[]{:S(2)}) collective-permute-start(bf16[384,640]{1,0:T(8,128)(2,1)} %attend.3.refs_0_.refs_2_.refs_5_), channel_id=1, source_target_pairs={{0,1},{1,2},{2,3},{4,5},{5,6},{6,7},{8,9},{9,10},{10,11},{12,13},{... | collective-permute-start | bytes 1474568 | tf_op jit(solution)/shard_map/ppermute | solution.py:323
  202.2 23.1 %collective-permute-start.32 = (bf16[384,640]{1,0:T(8,128)(2,1)}, bf16[384,640]{1,0:T(8,128)(2,1)}, u32[]{:S(2)}, u32[]{:S(2)}) collective-permute-start(bf16[384,640]{1,0:T(8,128)(2,1)} %attend.3.refs_0_.refs_2_.refs_5_), channel_id=1, source_target_pairs={{1,0},{2,1},{3,2},{5,4},{6,5},{7,6},{9,8},{10,9},{11,10},{13,12},{... | collective-permute-start | bytes 1474568 | tf_op jit(solution)/shard_map/ppermute | solution.py:323
  210.7 8.7 %copy-start.2 = (bf16[384,640]{1,0:T(8,128)(2,1)S(1)}, bf16[384,640]{1,0:T(8,128)(2,1)}, u32[]{:S(2)}) copy-start(bf16[384,640]{1,0:T(8,128)(2,1)} %attend.3.refs_0_.refs_2_.refs_5_) | copy-start | bytes 1474564
  219.3 28.3 %collective-permute-start.29 = (bf16[384,1280]{1,0:T(8,128)(2,1)}, bf16[384,1280]{1,0:T(8,128)(2,1)S(1)}, u32[]{:S(2)}, u32[]{:S(2)}) collective-permute-start(bf16[384,1280]{1,0:T(8,128)(2,1)} %update_last.1), channel_id=1, source_target_pairs={{0,4},{4,8},{8,12},{12,16},{16,20},{20,24},{24,28},{28,0},{1,5},{5... | collective-permute-start | bytes 2949128 | tf_op jit(solution)/shard_map/ppermute | solution.py:39
  219.4 17.8 %collective-permute-start.31 = (bf16[384,640]{1,0:T(8,128)(2,1)S(1)}, bf16[384,640]{1,0:T(8,128)(2,1)S(1)}, u32[]{:S(2)}, u32[]{:S(2)}) collective-permute-start(bf16[384,640]{1,0:T(8,128)(2,1)S(1)} %copy-done.2), channel_id=1, source_target_pairs={{0,3},{3,0},{4,7},{7,4},{8,11},{11,8},{12,15},{15,12},{16,19},{19,... | collective-permute-start | bytes 1474568 | tf_op jit(solution)/shard_map/ppermute | solution.py:330
  224.7 20.4 %collective-permute-start.33 = (bf16[384,640]{1,0:T(8,128)(2,1)}, bf16[384,640]{1,0:T(8,128)(2,1)S(1)}, u32[]{:S(2)}, u32[]{:S(2)}) collective-permute-start(bf16[384,640]{1,0:T(8,128)(2,1)} %collective-permute-done.30.refs_1_), channel_id=1, source_target_pairs={{1,2},{2,3},{5,6},{6,7},{9,10},{10,11},{13,14},{14,15},{17,18},{18... | collective-permute-start | bytes 1474568 | tf_op jit(solution)/shard_map/ppermute | solution.py:323
  225.4 22.2 %collective-permute-start.34 = (bf16[384,640]{1,0:T(8,128)(2,1)}, bf16[384,640]{1,0:T(8,128)(2,1)S(1)}, u32[]{:S(2)}, u32[]{:S(2)}) collective-permute-start(bf16[384,640]{1,0:T(8,128)(2,1)} %collective-permute-done.32.refs_4_), channel_id=1, source_target_pairs={{1,0},{2,1},{5,4},{6,5},{9,8},{10,9},{13,12},{14,13},{17,16},{18,1... | collective-permute-start | bytes 1474568 | tf_op jit(solution)/shard_map/ppermute | solution.py:323
  (18 other events, 68.3 us)

commit v3 on v2

--- a/solution.py
+++ b/solution.py
@@ -344,7 +344,7 @@
 class Fetch:
     def __init__(self, place_ref, span, line, weight_ref, scratch):
         self.attended, self.weights, self.sems = scratch[:3]
-        self.groups = weight_ref.shape[0]
+        self.groups = (len(line) + 1) // 2
         self.mine, self.span, self.place_ref = place_ref[0], span, place_ref
         self.line, self.weight_ref, self.columns_scratch = line, weight_ref, scratch[3:]
 
@@ -366,15 +366,27 @@
             def _():
                 self.slot(i, above[self.groups - k - 1]).start()
 
-    def weight(self, i, k):
-        group = lax.rem(self.mine + self.groups - k, self.groups)
-        return pltpu.make_async_copy(
-            self.weight_ref.at[group], self.weights.at[i], self.sems.at[1, i]
-        )
-
-    def start_weights(self, slots):
+    def start_weights(self, slots, stacks=()):
         for i, k in enumerate(slots):
-            self.weight(i, k).start()
+            group = lax.rem(self.mine + self.groups - k, self.groups)
+            if not stacks:
+                pltpu.make_async_copy(
+                    self.weight_ref.at[group], self.weights.at[i], self.sems.at[1, i]
+                ).start()
+                continue
+            count, _, sharers, part, cols = stacks[0].shape
+            first = self.place_ref.shape[0] - count * len(stacks)
+            for n in range(count * len(stacks)):
+                row = pl.multiple_of(self.place_ref[first + n] * part, part)
+                for o in range(sharers):
+                    pltpu.make_async_copy(
+                        stacks[n // count].at[n % count, group, o],
+                        self.weights.at[i, pl.ds(row, part), pl.ds(o * cols, cols)],
+                        self.sems.at[1, i],
+                    ).start()
+
+    def wait_weight(self, i):
+        pltpu.make_async_copy(self.weights.at[i], self.weights.at[i], self.sems.at[1, i]).wait()
 
     def columns(self, latents_ref, control_ref, mod_ref):
         latents, control, mods = self.columns_scratch
@@ -397,7 +409,7 @@
 
             @pl.when(new_weights)
             def _():
-                self.weight(i, k).wait()
+                self.wait_weight(i)
 
             part = jnp.dot(self.attended[i], self.weights[i], preferred_element_type=F32)
             part = part.astype(BF16).astype(F32)
@@ -417,13 +429,13 @@
         copy.start()
 
 
-def last_kernel(span, place_ref, weight_ref, latents_ref, control_ref, mod_ref, *refs):
-    line, out_ref, scratch = refs[:-7], refs[-7], refs[-6:]
-    fetch = Fetch(place_ref, span, line, weight_ref, scratch)
-    slots = range(weight_ref.shape[0])
+def last_kernel(span, count, place_ref, latents_ref, control_ref, mod_ref, *refs):
+    line, out_ref, scratch = refs[count:-7], refs[-7], refs[-6:]
+    fetch = Fetch(place_ref, span, line, refs[0], scratch)
+    slots = range(fetch.groups)
     columns = fetch.columns(latents_ref, control_ref, mod_ref)
     fetch.start_attended(slots)
-    fetch.start_weights(slots)
+    fetch.start_weights(slots, refs[:count] if count > 1 else ())
     start_all(columns)
     out_ref[...] = fetch.updated(fetch.branch(slots, True), columns).astype(BF16)
 
@@ -496,21 +508,22 @@
     )
 
 
-def update_last(place, line, weights, latents, control, modulation):
+def update_last(place, line, weights, latents, control, modulation, width):
     rows, cols = line[0].shape
-    groups, _, width = weights.shape
+    groups = (len(line) + 1) // 2
     span = latents.shape[0] - 1
     anywhere = pl.BlockSpec(memory_space=pl.ANY)
     return pl.pallas_call(
-        functools.partial(last_kernel, span),
-        in_specs=[pl.BlockSpec(memory_space=pltpu.SMEM)] + [anywhere] * (4 + len(line)),
+        functools.partial(last_kernel, span, len(weights)),
+        in_specs=[pl.BlockSpec(memory_space=pltpu.SMEM)]
+        + [anywhere] * (3 + len(weights) + len(line)),
         out_specs=pl.BlockSpec(memory_space=pltpu.VMEM),
         scratch_shapes=update_scratch(range(groups), rows, cols, width),
         out_shape=jax.ShapeDtypeStruct((rows, width), BF16),
         compiler_params=params(),
         cost_estimate=update_cost(groups, rows, cols, width),
         name="update_last",
-    )(place, weights, latents, control, modulation, *line)
+    )(place, latents, control, modulation, *weights, *line)
 
 
 def update_begin(place, line, weights, spans, rows, slots):
@@ -633,7 +646,11 @@
     total_width = local_cols * lax.axis_size("head")
     owner_index = lax.axis_index("queue")
     head_index = lax.axis_index("head")
-    place = jnp.concatenate([head_index.astype(jnp.int32).reshape(1), levels])
+    mine = owner_index.astype(jnp.int32)
+    block_indices = [mine ^ m ^ c for c in range(2) for m in (0, 2, 4, 6)]
+    place = jnp.concatenate(
+        [head_index.astype(jnp.int32).reshape(1), levels, jnp.stack(block_indices)]
+    )
     modulation = modulation.transpose(1, 0, 2)
     gain_rows = [gain.reshape(1, -1) for gain in (q_gain, k_gain)]
     cube = is_cube(w_query.shape[0], local_cols) and w_out.shape[0] // owners % 16 == 0
@@ -731,13 +748,16 @@
         across = jnp.concatenate([after(part, *last[1:]) for part in across])
         mine_blocks = jnp.stack([share, first[2], first[4], across])
         swapped = exchange(mine_blocks, 1)
-        weights = assemble(
-            [mine_blocks, swapped], [mine ^ m ^ c for c in range(2) for m in (0, 2, 4, 6)]
-        )
+        parts = [mine_blocks, swapped]
     else:
         weights = assemble_in_order(lax.all_gather(share, "queue", axis=0))
+        parts = [weights]
     rest = line
-    updated_last = update_last(place, last, weights, latents, control, modulation)
+    width = latents.shape[2] // groups
+    updated_last = update_last(place, last, parts, latents, control, modulation, width)
+    if cube:
+        swapped = after(swapped, updated_last, rest[1], rest[groups])
+        weights = assemble([mine_blocks, swapped], block_indices)
     arrived = shifted(updated_last, "queue", 1)
     return update_rest(place, arrived, rest, weights, latents, control, modulation)
 

time: 257 us -> 255 us (level)
  waiting for transfers between devices: 86.4 us -> 78.3 us
  starting transfers between devices: 64.9 us -> 71.9 us
    ppermute x8, starting transfers between devices: 13.4 us -> 22 us  [move(): return lax.ppermute(moved, axis, pairs)]
    ppermute x2, waiting for transfers between devices: 10.5 us -> 2.78 us  [along_line(): below[k] = above[k] = lax.ppermute(value, axis, pairs)]
    all_to_all x1, waiting for transfers between devices: 9.59 us -> 6.45 us  [out_shares(): lax.all_to_all(w_out.reshape(owners, rows // owners, cols), 'queue', 0, 0...]
    unnamed x59 -> x57, local copies, waits for them, and re-layouts: 5.66 us -> 5.43 us
  transfers between devices with their start and end apart: 37 -> 37, of which waited for: 19 -> 18; matrix products, arithmetic and copies ran while one was open for 3% -> 3% of each run, Pallas kernels for 28% -> 28%
where the time goes in v3:
time: 255 us
  Pallas kernels  88.5 us (35%)
  waiting for transfers between devices  78.3 us (31%)
  starting transfers between devices  71.9 us (28%)
  local copies, waits for them, and re-layouts  12 us (5%)
  other arithmetic  3.17 us (1%)
    ppermute x19, waiting for transfers between devices, exchange(): return lax.ppermute(value, 'queue', [(i, i ^ bit) for i in range(peers)])  43.1 us
    pallas_call x2, Pallas kernels, project(): pl.pallas_call(functools.partial(project_kernel, layout, begun is not Non...  31.5 us
    ppermute x8, starting transfers between devices, move(): return lax.ppermute(moved, axis, pairs)  22 us
    ppermute x8, waiting for transfers between devices, move(): return lax.ppermute(moved, axis, pairs)  17 us
    pallas_call x2, Pallas kernels, attend(): pl.pallas_call(functools.partial(attention_kernel, total_width, span, pla...  14.1 us
    pallas_call x1, Pallas kernels, modulated_norm(): pl.pallas_call(norm_kernel, grid_spec=pltpu.PrefetchScalarGridSpec(num_sc...  13.9 us
    ppermute x19, starting transfers between devices, exchange(): return lax.ppermute(value, 'queue', [(i, i ^ bit) for i in range(peers)])  12.5 us
    ppermute x2, starting transfers between devices, along_line(): below[k] = above[k] = lax.ppermute(value, axis, pairs)  12.4 us
  transfers between devices with their start and end apart: 37, of which 18 were waited for; matrix products, arithmetic and copies ran while one was open for 3% of the time, Pallas kernels for 28%

profile of v3, /device:TPU:0, one launch (start us, length us, event | category | flops | bytes accessed | tf_op | source)
XLA Modules:
  0.0 254.5 jit_solution(4784698949422898921)
XLA Ops:
  0.0 1.3 fusion
  1.5 3.0 %collective-permute-start.1 = (bf16[960,640]{1,0:T(8,128)(2,1)S(1)}, bf16[960,640]{1,0:T(8,128)(2,1)}, u32[]{:S(2)}, u32[]{:S(2)}) collective-permute-start(bf16[960,640]{1,0:T(8,128)(2,1)S(1)} %pad_maximum_fusion.2.refs_3_), channel_id=1, source_target_pairs={{0,8},{4,12},{8,0},{12,4},{16,24},{20,28},{24,16},{28,20},{1,9},{5... | collective-permute-start | bytes 3686408 | tf_op jit(solution)/shard_map/ppermute | solution.py:64
  4.7 1.6 collective-permute-start
  10.5 13.9 %modulated_norm.1.refs_1_ = bf16[8,768,640]{2,1,0:T(8,128)(2,1)} custom-call(s32[2]{0:T(128)} %levels_ref.1, bf16[2,384,5120]{2,1,0:T(8,128)(2,1)} %latents_ref.4, bf16[2,384,5120]{2,1,0:T(8,128)(2,1)} %control_ref.5, f32[3,64,5120]{2,1,0:T(8,128)} %bitcast.20), custom_call_target="tpu_custom_call" | custom-call | flops 2457600 | bytes 1474560 | tf_op jit(solution)/shard_map/modulated_norm/pallas_call | solution.py:98
  24.4 8.1 %collective-permute-done.1.refs_7_ = bf16[960,640]{1,0:T(8,128)(2,1)} collective-permute-done((bf16[960,640]{1,0:T(8,128)(2,1)S(1)}, bf16[960,640]{1,0:T(8,128)(2,1)}, u32[]{:S(2)}, u32[]{:S(2)}) %collective-permute-start.1) | collective-permute-done | bytes 1228832 | tf_op jit(solution)/shard_map/ppermute | solution.py:64
  32.5 2.3 collective-permute-done.refs_8_
  34.8 4.4 %all-to-all-start = ((bf16[8,80,640]{2,1,0:T(8,128)(2,1)}), bf16[8,80,640]{2,1,0:T(8,128)(2,1)}, u32[]{:S(2)}, u32[]{:S(2)}) async-start(bf16[8,80,640]{2,1,0:T(8,128)(2,1)} %bitcast.13), calls=%async_computation | async-start | bytes 1638400 | tf_op jit(solution)/shard_map/all_to_all | solution.py:578
  39.2 22.8 %collective-permute-done.6.refs_9_ = bf16[960,640]{1,0:T(8,128)(2,1)} collective-permute-done((bf16[960,640]{1,0:T(8,128)(2,1)S(1)}, bf16[960,640]{1,0:T(8,128)(2,1)}, u32[]{:S(2)}, u32[]{:S(2)}) %collective-permute-start.6) | collective-permute-done | bytes 1228832 | tf_op jit(solution)/shard_map/ppermute | solution.py:64
  62.0 6.4 %all-to-all-done = bf16[8,80,640]{2,1,0:T(8,128)(2,1)} async-done(((bf16[8,80,640]{2,1,0:T(8,128)(2,1)}), bf16[8,80,640]{2,1,0:T(8,128)(2,1)}, u32[]{:S(2)}, u32[]{:S(2)}) %all-to-all-start) | async-done | bytes 819232 | tf_op jit(solution)/shard_map/all_to_all | solution.py:578
  69.0 1.5 collective-permute-start.11
  71.0 1.7 collective-permute-done.10.refs_13_
  73.3 1.1 copy-done.11
  74.5 20.9 %project_begin.1.refs_6_ = f32[768,1920]{1,0:T(8,128)} custom-call(s32[6]{0:T(128)} %stack.80.refs_0_, bf16[8,768,640]{2,1,0:T(8,128)(2,1)} %modulated_norm.1.refs_1_, bf16[960,640]{1,0:T(8,128)(2,1)} %copy-done.4, bf16[960,640]{1,0:T(8,128)(2,1)} %copy-done.3, bf16[960,640]{1,0:T(8,128)(2,1)} %collective-permute-done.3.refs_4_, ...), custom_call_target="tpu_custom_call" | custom-call | flops 707788800 | bytes 1658880 | tf_op jit(solution)/shard_map/project_begin/pallas_call | solution.py:203
  95.4 2.8 %collective-permute-done.11.refs_3_ = bf16[960,640]{1,0:T(8,128)(2,1)S(1)} collective-permute-done((bf16[960,640]{1,0:T(8,128)(2,1)}, bf16[960,640]{1,0:T(8,128)(2,1)S(1)}, u32[]{:S(2)}, u32[]{:S(2)}) %collective-permute-start.11) | collective-permute-done | bytes 1228832 | tf_op jit(solution)/shard_map/ppermute | solution.py:64
  98.2 1.2 collective-permute-done.2.refs_2_
  99.4 1.7 collective-permute-done.13.refs_5_
  101.1 1.9 collective-permute-done.12.refs_4_
  103.0 10.6 %project_final.1 = (bf16[2,384,640]{2,1,0:T(8,128)(2,1)}, bf16[2,384,640]{2,1,0:T(8,128)(2,1)}, bf16[1,384,640]{2,1,0:T(8,128)(2,1)}, bf16[1,384,640]{2,1,0:T(8,128)(2,1)}, f32[2,6,128]{2,1,0:T(8,128)}) custom-call(s32[2]{0:T(128)} %pad_add_fusion.refs_0_, bf16[8,768,640]{2,1,0:T(8,128)(2,1)} %modulated_norm.1.refs_1_, bf16[960,640]{1,0:T(8,128)(2,1)} %copy-done.10, ...), custom_call_target="tpu_custom_call" | custom-call | flops 235929600 | bytes 798720 | tf_op jit(solution)/shard_map/project_final/pallas_call | solution.py:203
  113.6 2.0 collective-permute-start.14
  116.7 4.9 %all-to-all-start.1 = ((bf16[8,80,640]{2,1,0:T(8,128)(2,1)}), bf16[8,80,640]{2,1,0:T(8,128)(2,1)S(1)}, u32[]{:S(2)}, u32[]{:S(2)}) async-start(bf16[8,80,640]{2,1,0:T(8,128)(2,1)} %all-to-all-done), calls=%async_computation.1 | async-start | bytes 1638400 | tf_op jit(solution)/shard_map/all_to_all | solution.py:584
  121.5 2.2 collective-permute-start.18
  123.7 4.7 %collective-permute-start.21 = (bf16[2,384,640]{2,1,0:T(8,128)(2,1)}, bf16[2,384,640]{2,1,0:T(8,128)(2,1)S(1)}, u32[]{:S(2)}, u32[]{:S(2)}) collective-permute-start(bf16[2,384,640]{2,1,0:T(8,128)(2,1)} %get-tuple-element.48.k1.v1.k2.v2), channel_id=1, source_target_pairs={{0,4},{4,8},{8,12},{12,16},{16,20},{20,24},{24,28},{1,5},{5,9},{9,... | collective-permute-start | bytes 2949128 | tf_op jit(solution)/shard_map/ppermute | solution.py:33
  129.1 2.0 collective-permute-start.15
  131.1 4.8 %collective-permute-done.15 = f32[4,6,128]{2,1,0:T(8,128)S(1)} collective-permute-done((f32[4,6,128]{2,1,0:T(8,128)S(1)}, f32[4,6,128]{2,1,0:T(8,128)S(1)}, u32[]{:S(2)}, u32[]{:S(2)}) %collective-permute-start.15) | collective-permute-done | bytes 12320 | tf_op jit(solution)/shard_map/ppermute | solution.py:53
  135.9 4.6 %collective-permute-start.16 = (f32[4,6,128]{2,1,0:T(8,128)S(1)}, f32[4,6,128]{2,1,0:T(8,128)S(1)}, u32[]{:S(2)}, u32[]{:S(2)}) collective-permute-start(f32[4,6,128]{2,1,0:T(8,128)S(1)} %add.15.refs_0_), channel_id=1, source_target_pairs={{0,2},{1,3},{2,0},{3,1},{4,6},{5,7},{6,4},{7,5},{8,10},{9,11},{10,... | collective-permute-start | bytes 36872 | tf_op jit(solution)/shard_map/ppermute | solution.py:53
  140.5 3.2 %collective-permute-done.16.refs_1_ = f32[4,6,128]{2,1,0:T(8,128)S(1)} collective-permute-done((f32[4,6,128]{2,1,0:T(8,128)S(1)}, f32[4,6,128]{2,1,0:T(8,128)S(1)}, u32[]{:S(2)}, u32[]{:S(2)}) %collective-permute-start.16) | collective-permute-done | bytes 12320 | tf_op jit(solution)/shard_map/ppermute | solution.py:53
  143.7 1.6 collective-permute-start.22
  147.2 7.0 %attend.2.refs_2_ = bf16[384,640]{1,0:T(8,128)(2,1)} custom-call(s32[2,2]{1,0:T(2,128)} %and_convert_fusion.seen_ref, bf16[1,384,640]{2,1,0:T(8,128)(2,1)} %get-tuple-element.46.q_ref, f32[1,640]{1,0:T(1,128)} %reshape.21.q_gain_ref, f32[1,640]{1,0:T(1,128)} %reshape.22.k_gain_ref, bf16[2,384,640]{2,1,0:T(8,128)(2,1)} %copy-done.1, ...), custom_call_target="tpu_custom_call" | custom-call | flops 70778880 | bytes 245760 | tf_op jit(solution)/shard_map/attend/pallas_call | solution.py:297
  154.3 1.4 collective-permute-start.19
  155.6 1.3 collective-permute-start.20
  156.9 6.4 %collective-permute-start.25 = (bf16[384,640]{1,0:T(8,128)(2,1)}, bf16[384,640]{1,0:T(8,128)(2,1)S(1)}, u32[]{:S(2)}, u32[]{:S(2)}) collective-permute-start(bf16[384,640]{1,0:T(8,128)(2,1)} %attend.2.refs_2_), channel_id=1, source_target_pairs={{0,3},{3,0},{4,7},{7,4},{8,11},{11,8},{12,15},{15,12},{16,19},{19,... | collective-permute-start | bytes 1474568 | tf_op jit(solution)/shard_map/ppermute | solution.py:330
  163.4 4.2 %collective-permute-done.19.refs_3_ = bf16[384,640]{1,0:T(8,128)(2,1)S(1)} collective-permute-done((bf16[384,640]{1,0:T(8,128)(2,1)}, bf16[384,640]{1,0:T(8,128)(2,1)S(1)}, u32[]{:S(2)}, u32[]{:S(2)}) %collective-permute-start.19) | collective-permute-done | bytes 491552 | tf_op jit(solution)/shard_map/ppermute | solution.py:323
  168.3 2.6 %collective-permute-done.20.refs_6_ = bf16[384,640]{1,0:T(8,128)(2,1)S(1)} collective-permute-done((bf16[384,640]{1,0:T(8,128)(2,1)}, bf16[384,640]{1,0:T(8,128)(2,1)S(1)}, u32[]{:S(2)}, u32[]{:S(2)}) %collective-permute-start.20) | collective-permute-done | bytes 491552 | tf_op jit(solution)/shard_map/ppermute | solution.py:323
  170.9 1.3 collective-permute-start.26
  172.2 7.0 %attend.3.refs_0_.refs_2_.refs_5_ = bf16[384,640]{1,0:T(8,128)(2,1)} custom-call(s32[2,2]{1,0:T(2,128)} %and_convert_fusion.seen_ref, bf16[1,384,640]{2,1,0:T(8,128)(2,1)} %get-tuple-element.49.q_ref, f32[1,640]{1,0:T(1,128)} %reshape.21.q_gain_ref, f32[1,640]{1,0:T(1,128)} %reshape.22.k_gain_ref, bf16[2,384,640]{2,1,0:T(8,128)(2,1)} %copy-done.5, ...), custom_call_target="tpu_custom_call" | custom-call | flops 70778880 | bytes 245760 | tf_op jit(solution)/shard_map/attend/pallas_call | solution.py:297
  180.4 1.7 collective-permute-start.23
  183.5 7.6 %collective-permute-done.26.refs_7_ = bf16[384,640]{1,0:T(8,128)(2,1)} collective-permute-done((bf16[384,640]{1,0:T(8,128)(2,1)S(1)}, bf16[384,640]{1,0:T(8,128)(2,1)}, u32[]{:S(2)}, u32[]{:S(2)}) %collective-permute-start.26) | collective-permute-done | bytes 491552 | tf_op jit(solution)/shard_map/ppermute | solution.py:323
  191.3 1.7 pad_maximum_fusion.refs_0_
  193.0 13.8 %collective-permute-start.30 = (bf16[384,640]{1,0:T(8,128)(2,1)}, bf16[384,640]{1,0:T(8,128)(2,1)}, u32[]{:S(2)}, u32[]{:S(2)}) collective-permute-start(bf16[384,640]{1,0:T(8,128)(2,1)} %attend.3.refs_0_.refs_2_.refs_5_), channel_id=1, source_target_pairs={{0,1},{1,2},{2,3},{4,5},{5,6},{6,7},{8,9},{9,10},{10,11},{12,13},{... | collective-permute-start | bytes 1474568 | tf_op jit(solution)/shard_map/ppermute | solution.py:323
  206.9 1.5 collective-permute-start.31
  208.4 8.4 %update_last.1 = bf16[384,1280]{1,0:T(8,128)(2,1)} custom-call(s32[11]{0:T(128)} %concatenate.15.place_ref, bf16[2,384,5120]{2,1,0:T(8,128)(2,1)} %latents_ref.4, bf16[2,384,5120]{2,1,0:T(8,128)(2,1)} %control_ref.5, f32[3,64,5120]{2,1,0:T(8,128)} %bitcast.21, bf16[4,4,2,80,640]{4,3,2,1,0:T(8,128)(2,1)} %copy-done, ...), custom_call_target="tpu_custom_call" | custom-call | flops 157286400 | bytes 778240 | tf_op jit(solution)/shard_map/update_last/pallas_call | solution.py:516
  217.1 6.0 %collective-permute-start.32 = (bf16[384,640]{1,0:T(8,128)(2,1)}, bf16[384,640]{1,0:T(8,128)(2,1)S(1)}, u32[]{:S(2)}, u32[]{:S(2)}) collective-permute-start(bf16[384,640]{1,0:T(8,128)(2,1)} %attend.3.refs_0_.refs_2_.refs_5_), channel_id=1, source_target_pairs={{0,3},{3,0},{4,7},{7,4},{8,11},{11,8},{12,15},{15,12},{16,19},{19,... | collective-permute-start | bytes 1474568 | tf_op jit(solution)/shard_map/ppermute | solution.py:330
  223.8 1.3 collective-permute-start.34
  225.8 6.9 %assemble.1.weight_ref = bf16[4,640,1280]{2,1,0:T(8,128)(2,1)} custom-call(s32[8]{0:T(128)} %stack.88.index_ref, bf16[4,4,2,80,640]{4,3,2,1,0:T(8,128)(2,1)} %copy-done, bf16[4,4,2,80,640]{4,3,2,1,0:T(8,128)(2,1)} %collective-permute-done.28.refs_1_), custom_call_target="tpu_custom_call" | custom-call | bytes 819200 | tf_op jit(solution)/shard_map/assemble/pallas_call | solution.py:611
  232.7 2.8 %collective-permute-done.32.refs_3_.refs_6_ = bf16[384,640]{1,0:T(8,128)(2,1)S(1)} collective-permute-done((bf16[384,640]{1,0:T(8,128)(2,1)}, bf16[384,640]{1,0:T(8,128)(2,1)S(1)}, u32[]{:S(2)}, u32[]{:S(2)}) %collective-permute-start.32) | collective-permute-done | bytes 491552 | tf_op jit(solution)/shard_map/ppermute | solution.py:330
  236.3 7.1 %update_begin.1.begun_ref = f32[1,384,1280]{2,1,0:T(8,128)} custom-call(s32[11]{0:T(128)} %concatenate.15.place_ref, bf16[4,640,1280]{2,1,0:T(8,128)(2,1)} %assemble.1.weight_ref, bf16[384,640]{1,0:T(8,128)(2,1)} %attend.3.refs_0_.refs_2_.refs_5_, bf16[384,640]{1,0:T(8,128)(2,1)} %collective-permute-done.30.refs_1_, ...), custom_call_target="tpu_custom_call" | custom-call | flops 117964800 | bytes 645120 | tf_op jit(solution)/shard_map/update_begin/pallas_call | solution.py:533
  243.4 2.5 collective-permute-done.34.refs_5_
  247.6 6.7 %update_rest.1 = f32[2,384,1280]{2,1,0:T(8,128)} custom-call(s32[11]{0:T(128)} %concatenate.15.place_ref, bf16[384,1280]{1,0:T(8,128)(2,1)} %copy-done.13, f32[1,384,1280]{2,1,0:T(8,128)} %update_begin.1.begun_ref, bf16[4,640,1280]{2,1,0:T(8,128)(2,1)} %assemble.1.weight_ref, bf16[2,384,5120]{2,1,0:T(8,128)(2,1)} %latents_ref.4, ...), custom_call_target="tpu_custom_call" | custom-call | flops 39321600 | bytes 378880 | tf_op jit(solution)/shard_map/update_rest/pallas_call | solution.py:557
  (109 shorter events, 17.5 us)
Async XLA Ops:
  1.4 8.5 %copy-start.26 = (s32[2,2]{1,0:T(2,128)S(1)}, s32[2,2]{1,0:T(2,128)}, u32[]{:S(2)}) copy-start(s32[2,2]{1,0:T(2,128)} %param.15) | copy-start | bytes 52
  1.4 8.5 %copy-start.27 = (s32[2]{0:T(128)S(1)}, s32[2]{0:T(128)}, u32[]{:S(2)}) copy-start(s32[2]{0:T(128)} %constant.26.clone) | copy-start | bytes 28
  1.5 31.0 %copy-start.3 = (bf16[960,640]{1,0:T(8,128)(2,1)}, bf16[960,640]{1,0:T(8,128)(2,1)S(1)}, u32[]{:S(2)}) copy-start(bf16[960,640]{1,0:T(8,128)(2,1)S(1)} %pad_maximum_fusion.2.refs_3_) | copy-start | bytes 3686404
  1.5 31.0 %collective-permute-start.1 = (bf16[960,640]{1,0:T(8,128)(2,1)S(1)}, bf16[960,640]{1,0:T(8,128)(2,1)}, u32[]{:S(2)}, u32[]{:S(2)}) collective-permute-start(bf16[960,640]{1,0:T(8,128)(2,1)S(1)} %pad_maximum_fusion.2.refs_3_), channel_id=1, source_target_pairs={{0,8},{4,12},{8,0},{12,4},{16,24},{20,28},{24,16},{28,20},{1,9},{5... | collective-permute-start | bytes 3686408 | tf_op jit(solution)/shard_map/ppermute | solution.py:64
  4.7 19.7 %copy-start.4 = (bf16[960,640]{1,0:T(8,128)(2,1)}, bf16[960,640]{1,0:T(8,128)(2,1)S(1)}, u32[]{:S(2)}) copy-start(bf16[960,640]{1,0:T(8,128)(2,1)S(1)} %pad_maximum_fusion.1.refs_2_) | copy-start | bytes 3686404
  4.7 30.1 %collective-permute-start = (bf16[960,640]{1,0:T(8,128)(2,1)S(1)}, bf16[960,640]{1,0:T(8,128)(2,1)}, u32[]{:S(2)}, u32[]{:S(2)}) collective-permute-start(bf16[960,640]{1,0:T(8,128)(2,1)S(1)} %pad_maximum_fusion.1.refs_2_), channel_id=1, source_target_pairs={{0,16},{4,20},{8,24},{12,28},{16,0},{20,4},{24,8},{28,12},{1,17},{... | collective-permute-start | bytes 3686408 | tf_op jit(solution)/shard_map/ppermute | solution.py:64
  6.3 55.7 %collective-permute-start.6 = (bf16[960,640]{1,0:T(8,128)(2,1)S(1)}, bf16[960,640]{1,0:T(8,128)(2,1)}, u32[]{:S(2)}, u32[]{:S(2)}) collective-permute-start(bf16[960,640]{1,0:T(8,128)(2,1)S(1)} %pad_maximum_fusion.2.refs_3_), channel_id=1, source_target_pairs={{0,16},{4,20},{8,24},{12,28},{16,0},{20,4},{24,8},{28,12},{1,17},{... | collective-permute-start | bytes 3686408 | tf_op jit(solution)/shard_map/ppermute | solution.py:64
  6.8 61.7 %collective-permute-start.5 = (bf16[960,640]{1,0:T(8,128)(2,1)S(1)}, bf16[960,640]{1,0:T(8,128)(2,1)}, u32[]{:S(2)}, u32[]{:S(2)}) collective-permute-start(bf16[960,640]{1,0:T(8,128)(2,1)S(1)} %pad_maximum_fusion.1.refs_2_), channel_id=1, source_target_pairs={{0,8},{4,12},{8,0},{12,4},{16,24},{20,28},{24,16},{28,20},{1,9},{5... | collective-permute-start | bytes 3686408 | tf_op jit(solution)/shard_map/ppermute | solution.py:64
  24.4 44.0 %collective-permute-start.3 = (bf16[960,640]{1,0:T(8,128)(2,1)S(1)}, bf16[960,640]{1,0:T(8,128)(2,1)}, u32[]{:S(2)}, u32[]{:S(2)}) collective-permute-start(bf16[960,640]{1,0:T(8,128)(2,1)S(1)} %pad_maximum_fusion.1.refs_2_), channel_id=1, source_target_pairs={{0,4},{4,0},{8,12},{12,8},{16,20},{20,16},{24,28},{28,24},{1,5},{5... | collective-permute-start | bytes 3686408 | tf_op jit(solution)/shard_map/ppermute | solution.py:64
  32.5 36.5 %collective-permute-start.4 = (bf16[960,640]{1,0:T(8,128)(2,1)S(1)}, bf16[960,640]{1,0:T(8,128)(2,1)}, u32[]{:S(2)}, u32[]{:S(2)}) collective-permute-start(bf16[960,640]{1,0:T(8,128)(2,1)S(1)} %pad_maximum_fusion.2.refs_3_), channel_id=1, source_target_pairs={{0,4},{4,0},{8,12},{12,8},{16,20},{20,16},{24,28},{28,24},{1,5},{5... | collective-permute-start | bytes 3686408 | tf_op jit(solution)/shard_map/ppermute | solution.py:64
  34.8 35.7 %collective-permute-start.8 = (bf16[960,640]{1,0:T(8,128)(2,1)}, bf16[960,640]{1,0:T(8,128)(2,1)}, u32[]{:S(2)}, u32[]{:S(2)}) collective-permute-start(bf16[960,640]{1,0:T(8,128)(2,1)} %collective-permute-done.1.refs_7_), channel_id=1, source_target_pairs={{0,4},{4,0},{8,12},{12,8},{16,20},{20,16},{24,28},{28,24},{1,5},{5... | collective-permute-start | bytes 3686408 | tf_op jit(solution)/shard_map/ppermute | solution.py:64
  34.8 33.6 %all-to-all-start = ((bf16[8,80,640]{2,1,0:T(8,128)(2,1)}), bf16[8,80,640]{2,1,0:T(8,128)(2,1)}, u32[]{:S(2)}, u32[]{:S(2)}) async-start(bf16[8,80,640]{2,1,0:T(8,128)(2,1)} %bitcast.13), calls=%async_computation | async-start | bytes 1638400 | tf_op jit(solution)/shard_map/all_to_all | solution.py:578
  62.0 9.0 %collective-permute-start.9 = (bf16[960,640]{1,0:T(8,128)(2,1)}, bf16[960,640]{1,0:T(8,128)(2,1)}, u32[]{:S(2)}, u32[]{:S(2)}) collective-permute-start(bf16[960,640]{1,0:T(8,128)(2,1)} %collective-permute-done.refs_8_), channel_id=1, source_target_pairs={{0,4},{4,0},{8,12},{12,8},{16,20},{20,16},{24,28},{28,24},{1,5},{5... | collective-permute-start | bytes 3686408 | tf_op jit(solution)/shard_map/ppermute | solution.py:64
  68.4 4.3 %collective-permute-start.10 = (bf16[960,640]{1,0:T(8,128)(2,1)}, bf16[960,640]{1,0:T(8,128)(2,1)}, u32[]{:S(2)}, u32[]{:S(2)}) collective-permute-start(bf16[960,640]{1,0:T(8,128)(2,1)} %collective-permute-done.6.refs_9_), channel_id=1, source_target_pairs={{0,4},{4,0},{8,12},{12,8},{16,20},{20,16},{24,28},{28,24},{1,5},{5... | collective-permute-start | bytes 3686408 | tf_op jit(solution)/shard_map/ppermute | solution.py:64
  68.4 4.9 %collective-permute-start.7 = (bf16[960,640]{1,0:T(8,128)(2,1)}, bf16[960,640]{1,0:T(8,128)(2,1)S(1)}, u32[]{:S(2)}, u32[]{:S(2)}) collective-permute-start(bf16[960,640]{1,0:T(8,128)(2,1)} %collective-permute-done.5.refs_6_), channel_id=1, source_target_pairs={{0,4},{4,0},{8,12},{12,8},{16,20},{20,16},{24,28},{28,24},{1,5},{5... | collective-permute-start | bytes 3686408 | tf_op jit(solution)/shard_map/ppermute | solution.py:64
  69.0 29.2 %collective-permute-start.11 = (bf16[960,640]{1,0:T(8,128)(2,1)}, bf16[960,640]{1,0:T(8,128)(2,1)S(1)}, u32[]{:S(2)}, u32[]{:S(2)}) collective-permute-start(bf16[960,640]{1,0:T(8,128)(2,1)} %collective-permute-done.1.refs_7_), channel_id=1, source_target_pairs={{0,16},{4,20},{8,24},{12,28},{16,0},{20,4},{24,8},{28,12},{1,17},{... | collective-permute-start | bytes 3686408 | tf_op jit(solution)/shard_map/ppermute | solution.py:64
  70.5 28.9 %collective-permute-start.2 = (bf16[960,640]{1,0:T(8,128)(2,1)}, bf16[960,640]{1,0:T(8,128)(2,1)S(1)}, u32[]{:S(2)}, u32[]{:S(2)}) collective-permute-start(bf16[960,640]{1,0:T(8,128)(2,1)} %collective-permute-done.refs_8_), channel_id=1, source_target_pairs={{0,8},{4,12},{8,0},{12,4},{16,24},{20,28},{24,16},{28,20},{1,9},{5... | collective-permute-start | bytes 3686408 | tf_op jit(solution)/shard_map/ppermute | solution.py:64
  98.2 2.9 %collective-permute-start.13 = (bf16[960,640]{1,0:T(8,128)(2,1)S(1)}, bf16[960,640]{1,0:T(8,128)(2,1)S(1)}, u32[]{:S(2)}, u32[]{:S(2)}) collective-permute-start(bf16[960,640]{1,0:T(8,128)(2,1)S(1)} %collective-permute-done.11.refs_3_), channel_id=1, source_target_pairs={{0,4},{4,0},{8,12},{12,8},{16,20},{20,16},{24,28},{28,24},{1,5},{5... | collective-permute-start | bytes 3686408 | tf_op jit(solution)/shard_map/ppermute | solution.py:64
  99.4 3.6 %collective-permute-start.12 = (bf16[960,640]{1,0:T(8,128)(2,1)S(1)}, bf16[960,640]{1,0:T(8,128)(2,1)}, u32[]{:S(2)}, u32[]{:S(2)}) collective-permute-start(bf16[960,640]{1,0:T(8,128)(2,1)S(1)} %collective-permute-done.2.refs_2_), channel_id=1, source_target_pairs={{0,4},{4,0},{8,12},{12,8},{16,20},{20,16},{24,28},{28,24},{1,5},{5... | collective-permute-start | bytes 3686408 | tf_op jit(solution)/shard_map/ppermute | solution.py:64
  113.6 3.1 %collective-permute-start.14 = (f32[2,6,128]{2,1,0:T(8,128)}, f32[2,6,128]{2,1,0:T(8,128)S(1)}, u32[]{:S(2)}, u32[]{:S(2)}) collective-permute-start(f32[2,6,128]{2,1,0:T(8,128)} %get-tuple-element.42), channel_id=1, source_target_pairs={{0,4},{4,8},{8,12},{12,16},{16,20},{20,24},{24,28},{1,5},{5,9},{9,... | collective-permute-start | bytes 18440 | tf_op jit(solution)/shard_map/ppermute | solution.py:33
  116.7 27.0 %all-to-all-start.1 = ((bf16[8,80,640]{2,1,0:T(8,128)(2,1)}), bf16[8,80,640]{2,1,0:T(8,128)(2,1)S(1)}, u32[]{:S(2)}, u32[]{:S(2)}) async-start(bf16[8,80,640]{2,1,0:T(8,128)(2,1)} %all-to-all-done), calls=%async_computation.1 | async-start | bytes 1638400 | tf_op jit(solution)/shard_map/all_to_all | solution.py:584
  121.5 24.8 %collective-permute-start.18 = (bf16[2,384,640]{2,1,0:T(8,128)(2,1)}, bf16[2,384,640]{2,1,0:T(8,128)(2,1)S(1)}, u32[]{:S(2)}, u32[]{:S(2)}) collective-permute-start(bf16[2,384,640]{2,1,0:T(8,128)(2,1)} %get-tuple-element.47.k2.v2), channel_id=1, source_target_pairs={{0,4},{4,8},{8,12},{12,16},{16,20},{20,24},{24,28},{1,5},{5,9},{9,... | collective-permute-start | bytes 2949128 | tf_op jit(solution)/shard_map/ppermute | solution.py:33
  123.7 33.2 %collective-permute-start.21 = (bf16[2,384,640]{2,1,0:T(8,128)(2,1)}, bf16[2,384,640]{2,1,0:T(8,128)(2,1)S(1)}, u32[]{:S(2)}, u32[]{:S(2)}) collective-permute-start(bf16[2,384,640]{2,1,0:T(8,128)(2,1)} %get-tuple-element.48.k1.v1.k2.v2), channel_id=1, source_target_pairs={{0,4},{4,8},{8,12},{12,16},{16,20},{20,24},{24,28},{1,5},{5,9},{9,... | collective-permute-start | bytes 2949128 | tf_op jit(solution)/shard_map/ppermute | solution.py:33
  129.1 6.8 %collective-permute-start.15 = (f32[4,6,128]{2,1,0:T(8,128)S(1)}, f32[4,6,128]{2,1,0:T(8,128)S(1)}, u32[]{:S(2)}, u32[]{:S(2)}) collective-permute-start(f32[4,6,128]{2,1,0:T(8,128)S(1)} %constant_dynamic-update-slice_fusion), channel_id=1, source_target_pairs={{0,1},{1,0},{2,3},{3,2},{4,5},{5,4},{6,7},{7,6},{8,9},{9,8},{10,11... | collective-permute-start | bytes 36872 | tf_op jit(solution)/shard_map/ppermute | solution.py:53
  135.9 10.4 %copy-start.21 = (f32[4,6,128]{2,1,0:T(8,128)}, f32[4,6,128]{2,1,0:T(8,128)S(1)}, u32[]{:S(2)}) copy-start(f32[4,6,128]{2,1,0:T(8,128)S(1)} %add.15.refs_0_) | copy-start | bytes 36868
  135.9 7.8 %collective-permute-start.16 = (f32[4,6,128]{2,1,0:T(8,128)S(1)}, f32[4,6,128]{2,1,0:T(8,128)S(1)}, u32[]{:S(2)}, u32[]{:S(2)}) collective-permute-start(f32[4,6,128]{2,1,0:T(8,128)S(1)} %add.15.refs_0_), channel_id=1, source_target_pairs={{0,2},{1,3},{2,0},{3,1},{4,6},{5,7},{6,4},{7,5},{8,10},{9,11},{10,... | collective-permute-start | bytes 36872 | tf_op jit(solution)/shard_map/ppermute | solution.py:53
  143.7 35.5 %copy-start.6 = (bf16[8,80,640]{2,1,0:T(8,128)(2,1)}, bf16[8,80,640]{2,1,0:T(8,128)(2,1)S(1)}, u32[]{:S(2)}) copy-start(bf16[8,80,640]{2,1,0:T(8,128)(2,1)S(1)} %all-to-all-done.1) | copy-start | bytes 2457604
  143.7 35.5 %collective-permute-start.22 = (bf16[4,2,80,640]{3,2,1,0:T(8,128)(2,1)S(1)}, bf16[4,2,80,640]{3,2,1,0:T(8,128)(2,1)}, u32[]{:S(2)}, u32[]{:S(2)}) collective-permute-start(bf16[4,2,80,640]{3,2,1,0:T(8,128)(2,1)S(1)} %bitcast.23), channel_id=1, source_target_pairs={{0,16},{4,20},{8,24},{12,28},{16,0},{20,4},{24,8},{28,12},{1,17},{... | collective-permute-start | bytes 2457608 | tf_op jit(solution)/shard_map/ppermute | solution.py:64
  145.3 36.8 %collective-permute-start.17 = (bf16[4,2,80,640]{3,2,1,0:T(8,128)(2,1)S(1)}, bf16[4,2,80,640]{3,2,1,0:T(8,128)(2,1)}, u32[]{:S(2)}, u32[]{:S(2)}) collective-permute-start(bf16[4,2,80,640]{3,2,1,0:T(8,128)(2,1)S(1)} %bitcast.24), channel_id=1, source_target_pairs={{0,8},{4,12},{8,0},{12,4},{16,24},{20,28},{24,16},{28,20},{1,9},{5... | collective-permute-start | bytes 2457608 | tf_op jit(solution)/shard_map/ppermute | solution.py:64
  154.3 13.3 %collective-permute-start.19 = (bf16[384,640]{1,0:T(8,128)(2,1)}, bf16[384,640]{1,0:T(8,128)(2,1)S(1)}, u32[]{:S(2)}, u32[]{:S(2)}) collective-permute-start(bf16[384,640]{1,0:T(8,128)(2,1)} %attend.2.refs_2_), channel_id=1, source_target_pairs={{0,1},{1,2},{2,3},{4,5},{5,6},{6,7},{8,9},{9,10},{10,11},{12,13},{... | collective-permute-start | bytes 1474568 | tf_op jit(solution)/shard_map/ppermute | solution.py:323
  155.6 15.3 %collective-permute-start.20 = (bf16[384,640]{1,0:T(8,128)(2,1)}, bf16[384,640]{1,0:T(8,128)(2,1)S(1)}, u32[]{:S(2)}, u32[]{:S(2)}) collective-permute-start(bf16[384,640]{1,0:T(8,128)(2,1)} %attend.2.refs_2_), channel_id=1, source_target_pairs={{1,0},{2,1},{3,2},{5,4},{6,5},{7,6},{9,8},{10,9},{11,10},{13,12},{... | collective-permute-start | bytes 1474568 | tf_op jit(solution)/shard_map/ppermute | solution.py:323
  156.9 15.3 %copy-start.5 = (bf16[2,384,640]{2,1,0:T(8,128)(2,1)}, bf16[2,384,640]{2,1,0:T(8,128)(2,1)S(1)}, u32[]{:S(2)}) copy-start(bf16[2,384,640]{2,1,0:T(8,128)(2,1)S(1)} %collective-permute-done.21.k0.v0) | copy-start | bytes 2949124
  156.9 26.6 %collective-permute-start.25 = (bf16[384,640]{1,0:T(8,128)(2,1)}, bf16[384,640]{1,0:T(8,128)(2,1)S(1)}, u32[]{:S(2)}, u32[]{:S(2)}) collective-permute-start(bf16[384,640]{1,0:T(8,128)(2,1)} %attend.2.refs_2_), channel_id=1, source_target_pairs={{0,3},{3,0},{4,7},{7,4},{8,11},{11,8},{12,15},{15,12},{16,19},{19,... | collective-permute-start | bytes 1474568 | tf_op jit(solution)/shard_map/ppermute | solution.py:330
  167.6 11.7 %copy-start.16 = (bf16[384,640]{1,0:T(8,128)(2,1)}, bf16[384,640]{1,0:T(8,128)(2,1)S(1)}, u32[]{:S(2)}) copy-start(bf16[384,640]{1,0:T(8,128)(2,1)S(1)} %collective-permute-done.19.refs_3_) | copy-start | bytes 1474564
  167.6 15.9 %collective-permute-start.24 = (bf16[384,640]{1,0:T(8,128)(2,1)S(1)}, bf16[384,640]{1,0:T(8,128)(2,1)S(1)}, u32[]{:S(2)}, u32[]{:S(2)}) collective-permute-start(bf16[384,640]{1,0:T(8,128)(2,1)S(1)} %collective-permute-done.19.refs_3_), channel_id=1, source_target_pairs={{1,2},{2,3},{5,6},{6,7},{9,10},{10,11},{13,14},{14,15},{17,18},{18... | collective-permute-start | bytes 1474568 | tf_op jit(solution)/shard_map/ppermute | solution.py:323
  170.9 20.3 %collective-permute-start.26 = (bf16[384,640]{1,0:T(8,128)(2,1)S(1)}, bf16[384,640]{1,0:T(8,128)(2,1)}, u32[]{:S(2)}, u32[]{:S(2)}) collective-permute-start(bf16[384,640]{1,0:T(8,128)(2,1)S(1)} %collective-permute-done.20.refs_6_), channel_id=1, source_target_pairs={{1,0},{2,1},{5,4},{6,5},{9,8},{10,9},{13,12},{14,13},{17,16},{18,1... | collective-permute-start | bytes 1474568 | tf_op jit(solution)/shard_map/ppermute | solution.py:323
  179.3 12.0 %copy-start.7 = (bf16[8,80,640]{2,1,0:T(8,128)(2,1)S(1)}, bf16[8,80,640]{2,1,0:T(8,128)(2,1)}, u32[]{:S(2)}) copy-start(bf16[8,80,640]{2,1,0:T(8,128)(2,1)} %copy-done.6) | copy-start | bytes 2457604
  180.4 10.8 %collective-permute-start.23 = (bf16[2,2,80,640]{3,2,1,0:T(8,128)(2,1)S(1)}, bf16[2,2,80,640]{3,2,1,0:T(8,128)(2,1)S(1)}, u32[]{:S(2)}, u32[]{:S(2)}) collective-permute-start(bf16[2,2,80,640]{3,2,1,0:T(8,128)(2,1)S(1)} %slice.14), channel_id=1, source_target_pairs={{0,8},{4,12},{8,0},{12,4},{16,24},{20,28},{24,16},{28,20},{1,9},{5... | collective-permute-start | bytes 1228808 | tf_op jit(solution)/shard_map/ppermute | solution.py:64
  183.1 8.1 %collective-permute-start.27 = (bf16[2,2,80,640]{3,2,1,0:T(8,128)(2,1)S(1)}, bf16[2,2,80,640]{3,2,1,0:T(8,128)(2,1)S(1)}, u32[]{:S(2)}, u32[]{:S(2)}) collective-permute-start(bf16[2,2,80,640]{3,2,1,0:T(8,128)(2,1)S(1)} %slice.15), channel_id=1, source_target_pairs={{0,16},{4,20},{8,24},{12,28},{16,0},{20,4},{24,8},{28,12},{1,17},{... | collective-permute-start | bytes 1228808 | tf_op jit(solution)/shard_map/ppermute | solution.py:64
  183.5 9.4 %copy-start.8 = (bf16[384,640]{1,0:T(8,128)(2,1)}, bf16[384,640]{1,0:T(8,128)(2,1)S(1)}, u32[]{:S(2)}) copy-start(bf16[384,640]{1,0:T(8,128)(2,1)S(1)} %collective-permute-done.25.refs_5_.refs_8_) | copy-start | bytes 1474564
  193.0 15.5 %copy-start = (bf16[4,4,2,80,640]{4,3,2,1,0:T(8,128)(2,1)}, bf16[4,4,2,80,640]{4,3,2,1,0:T(8,128)(2,1)S(1)}, u32[]{:S(2)}) copy-start(bf16[4,4,2,80,640]{4,3,2,1,0:T(8,128)(2,1)S(1)} %pad_maximum_fusion.refs_0_) | copy-start | bytes 9830404
  193.0 15.5 %collective-permute-start.28 = (bf16[4,4,2,80,640]{4,3,2,1,0:T(8,128)(2,1)S(1)}, bf16[4,4,2,80,640]{4,3,2,1,0:T(8,128)(2,1)}, u32[]{:S(2)}, u32[]{:S(2)}) collective-permute-start(bf16[4,4,2,80,640]{4,3,2,1,0:T(8,128)(2,1)S(1)} %pad_maximum_fusion.refs_0_), channel_id=1, source_target_pairs={{0,4},{4,0},{8,12},{12,8},{16,20},{20,16},{24,28},{28,24},{1,5},{5... | collective-permute-start | bytes 9830408 | tf_op jit(solution)/shard_map/ppermute | solution.py:64
  193.0 30.0 %collective-permute-start.30 = (bf16[384,640]{1,0:T(8,128)(2,1)}, bf16[384,640]{1,0:T(8,128)(2,1)}, u32[]{:S(2)}, u32[]{:S(2)}) collective-permute-start(bf16[384,640]{1,0:T(8,128)(2,1)} %attend.3.refs_0_.refs_2_.refs_5_), channel_id=1, source_target_pairs={{0,1},{1,2},{2,3},{4,5},{5,6},{6,7},{8,9},{9,10},{10,11},{12,13},{... | collective-permute-start | bytes 1474568 | tf_op jit(solution)/shard_map/ppermute | solution.py:323
  206.9 16.9 %collective-permute-start.31 = (bf16[384,640]{1,0:T(8,128)(2,1)}, bf16[384,640]{1,0:T(8,128)(2,1)}, u32[]{:S(2)}, u32[]{:S(2)}) collective-permute-start(bf16[384,640]{1,0:T(8,128)(2,1)} %attend.3.refs_0_.refs_2_.refs_5_), channel_id=1, source_target_pairs={{1,0},{2,1},{3,2},{5,4},{6,5},{7,6},{9,8},{10,9},{11,10},{13,12},{... | collective-permute-start | bytes 1474568 | tf_op jit(solution)/shard_map/ppermute | solution.py:323
  216.8 29.1 %collective-permute-start.29 = (bf16[384,1280]{1,0:T(8,128)(2,1)}, bf16[384,1280]{1,0:T(8,128)(2,1)S(1)}, u32[]{:S(2)}, u32[]{:S(2)}) collective-permute-start(bf16[384,1280]{1,0:T(8,128)(2,1)} %update_last.1), channel_id=1, source_target_pairs={{0,4},{4,8},{8,12},{12,16},{16,20},{20,24},{24,28},{28,0},{1,5},{5... | collective-permute-start | bytes 2949128 | tf_op jit(solution)/shard_map/ppermute | solution.py:39
  217.1 18.4 %collective-permute-start.32 = (bf16[384,640]{1,0:T(8,128)(2,1)}, bf16[384,640]{1,0:T(8,128)(2,1)S(1)}, u32[]{:S(2)}, u32[]{:S(2)}) collective-permute-start(bf16[384,640]{1,0:T(8,128)(2,1)} %attend.3.refs_0_.refs_2_.refs_5_), channel_id=1, source_target_pairs={{0,3},{3,0},{4,7},{7,4},{8,11},{11,8},{12,15},{15,12},{16,19},{19,... | collective-permute-start | bytes 1474568 | tf_op jit(solution)/shard_map/ppermute | solution.py:330
  223.1 20.2 %collective-permute-start.33 = (bf16[384,640]{1,0:T(8,128)(2,1)}, bf16[384,640]{1,0:T(8,128)(2,1)S(1)}, u32[]{:S(2)}, u32[]{:S(2)}) collective-permute-start(bf16[384,640]{1,0:T(8,128)(2,1)} %collective-permute-done.30.refs_1_), channel_id=1, source_target_pairs={{1,2},{2,3},{5,6},{6,7},{9,10},{10,11},{13,14},{14,15},{17,18},{18... | collective-permute-start | bytes 1474568 | tf_op jit(solution)/shard_map/ppermute | solution.py:323
  223.8 22.1 %collective-permute-start.34 = (bf16[384,640]{1,0:T(8,128)(2,1)}, bf16[384,640]{1,0:T(8,128)(2,1)S(1)}, u32[]{:S(2)}, u32[]{:S(2)}) collective-permute-start(bf16[384,640]{1,0:T(8,128)(2,1)} %collective-permute-done.31.refs_4_), channel_id=1, source_target_pairs={{1,0},{2,1},{5,4},{6,5},{9,8},{10,9},{13,12},{14,13},{17,16},{18,1... | collective-permute-start | bytes 1474568 | tf_op jit(solution)/shard_map/ppermute | solution.py:323
  (17 other events, 60.8 us)

commit v4 on v3

--- a/solution.py
+++ b/solution.py
@@ -171,13 +171,13 @@
     *out_refs, square_ref = out_refs
     column = 0
     for n, group_count in enumerate(groups):
-        outs = out_refs[n * spans : (n + 1) * spans]
-        _, span_rows, cols = outs[0].shape
+        out_ref = out_refs[n]
+        _, _, span_rows, cols = out_ref.shape
         for g in range(group_count):
             rounded = total[:, column : column + cols].astype(BF16)
             column += cols
-            for i, out_ref in enumerate(outs):
-                out_ref[g] = rounded[i * span_rows : (i + 1) * span_rows]
+            for i in range(spans):
+                out_ref[i, g] = rounded[i * span_rows : (i + 1) * span_rows]
         floats = rounded.astype(F32)
         squares = jnp.sum(floats * floats, axis=-1, keepdims=True)
         for t in range(squares.shape[0] // HD):
@@ -193,9 +193,7 @@
     in_vmem = pl.BlockSpec(memory_space=pltpu.VMEM)
     if spans:
         out_shape = [
-            jax.ShapeDtypeStruct((count, rows // spans, local), BF16)
-            for count in groups
-            for _ in range(spans)
+            jax.ShapeDtypeStruct((spans, count, rows // spans, local), BF16) for count in groups
         ]
         out_shape.append(jax.ShapeDtypeStruct((len(groups), rows // HD, HD), F32))
     else:
@@ -222,10 +220,7 @@
         ),
         name="project_final" if spans else "project_begin",
     )(indices, normed, *weights, *([begun] if begun is not None else []))
-    if not spans:
-        return result[0]
-    sets = [result[n * spans : (n + 1) * spans] for n in range(len(groups))]
-    return (*sets, result[-1])
+    return result if spans else result[0]
 
 
 def attention_kernel(
@@ -281,25 +276,24 @@
 
 
 def attend(span, seen, query, squares, gains, prior, own, total_width):
-    spans = len(own)
-    _, rows, cols = query.shape
+    spans, _, rows, cols = query.shape
     heads = cols // HD
     tiles = rows // HD
     window = [(spans + span - 2 + w) for w in range(3)]
     window = [(0 if position >= spans else 2, position % spans) for position in window]
     places = [(1, span * tiles)] + [(array, index * tiles) for array, index in window]
-    arrays = [(own if array == 0 else prior)[index] for array, index in window]
-
-    def part(which):
-        return pl.BlockSpec((None, rows, cols), lambda i: (which, 0, 0))
+    arrays = [own if array == 0 else prior for array, _ in window]
+
+    def part(which, index):
+        return pl.BlockSpec((None, None, rows, cols), lambda i: (index, which, 0, 0))
 
     gain_spec = pl.BlockSpec((1, cols), lambda i: (0, 0))
     return pl.pallas_call(
         functools.partial(attention_kernel, total_width, span, places),
         grid=(1,),
-        in_specs=[pl.BlockSpec(memory_space=pltpu.SMEM), part(0), gain_spec, gain_spec]
-        + [part(1)] * 3
-        + [part(0)] * 3
+        in_specs=[pl.BlockSpec(memory_space=pltpu.SMEM), part(0, span), gain_spec, gain_spec]
+        + [part(1, index) for _, index in window]
+        + [part(0, index) for _, index in window]
         + [pl.BlockSpec(memory_space=pltpu.VMEM)] * len(squares),
         out_specs=pl.BlockSpec((rows, cols), lambda i: (0, 0)),
         out_shape=jax.ShapeDtypeStruct((rows, cols), BF16),
@@ -722,7 +716,7 @@
         own, query, squares = project(normed, weights, layout, zero, (2, 1), spans=spans)
         share = out_shares(w_out)
 
-    prior = [from_behind(span, "queue", 1) for span in reversed(own)][::-1]
+    prior = from_behind(own, "queue", 1)
     prior_squares = from_behind(squares, "queue", 1)
     share = out_blocks(after(share, prior_squares)) if cube else out_blocks(share)
     squares = sum_terms(jnp.concatenate([squares, prior_squares]), "head")
@@ -731,18 +725,18 @@
         return attend(span, seen, ready, squares, gain_rows, prior, own, total_width)
 
     groups = lax.axis_size("head")
-    attended_last = attended_of(spans - 1, query[-1])
+    attended_last = attended_of(spans - 1, query)
     last = along_line(attended_last, "head")
     sent = [last[1], last[groups]]
     begin_rest = [attended_last, *sent]
     if cube:
         share = after(share, *squares)
         first = {m: exchange(share, m) for m in (2, 4)}
-    rest = [attended_of(span, after(query[span], *begin_rest)) for span in range(spans - 1)]
+    rest = [attended_of(span, after(query, *begin_rest)) for span in range(spans - 1)]
     rest = rest[0] if len(rest) == 1 else jnp.concatenate(rest, axis=0)
     line = along_line(rest, "head")
     if cube:
-        first = {m: after(block, rest, *prior) for m, block in first.items()}
+        first = {m: after(block, rest) for m, block in first.items()}
         half = share.shape[0] // 2
         across = [exchange(first[4][:half], 2), exchange(first[2][half:], 4)]
         across = jnp.concatenate([after(part, *last[1:]) for part in across])

time: 255 us -> 276 us (1.082)
  starting transfers between devices: 71.9 us -> 90.7 us
    ppermute x19, starting transfers between devices: 12.5 us -> 38.1 us  [exchange(): return lax.ppermute(value, 'queue', [(i, i ^ bit) for i in range(peers)])]
    ppermute x19, waiting for transfers between devices: 43.1 us -> 50.6 us  [exchange(): return lax.ppermute(value, 'queue', [(i, i ^ bit) for i in range(peers)])]
    ppermute x8, waiting for transfers between devices: 17 us -> 11.7 us  [move(): return lax.ppermute(moved, axis, pairs)]
    ppermute x3 -> x2, starting transfers between devices: 8.89 us -> 4.24 us  [from_behind(): return lax.ppermute(value, axis, pairs)]
  transfers between devices with their start and end apart: 37 -> 36, of which waited for: 18 -> 20; matrix products, arithmetic and copies ran while one was open for 3% -> 3% of each run, Pallas kernels for 28% -> 26%
where the time goes in v4:
time: 276 us; the launch traced here: 275 us
  starting transfers between devices  90.7 us (33%)
  Pallas kernels  88.6 us (32%)
  waiting for transfers between devices  80.8 us (29%)
  local copies, waits for them, and re-layouts  11.2 us (4%)
  other arithmetic  3.22 us (1%)
    ppermute x19, waiting for transfers between devices, exchange(): return lax.ppermute(value, 'queue', [(i, i ^ bit) for i in range(peers)])  50.6 us
    ppermute x19, starting transfers between devices, exchange(): return lax.ppermute(value, 'queue', [(i, i ^ bit) for i in range(peers)])  38.1 us
    pallas_call x2, Pallas kernels, project(): pl.pallas_call(functools.partial(project_kernel, layout, begun is not Non...  31.6 us
    ppermute x8, starting transfers between devices, move(): return lax.ppermute(moved, axis, pairs)  21.1 us
    pallas_call x2, Pallas kernels, attend(): pl.pallas_call(functools.partial(attention_kernel, total_width, span, pla...  14.1 us
    pallas_call x1, Pallas kernels, modulated_norm(): pl.pallas_call(norm_kernel, grid_spec=pltpu.PrefetchScalarGridSpec(num_sc...  13.9 us
    ppermute x8, waiting for transfers between devices, move(): return lax.ppermute(moved, axis, pairs)  11.7 us
    ppermute x2, starting transfers between devices, along_line(): below[k] = above[k] = lax.ppermute(value, axis, pairs)  11.6 us
  transfers between devices with their start and end apart: 36, of which 20 were waited for; matrix products, arithmetic and copies ran while one was open for 3% of the time, Pallas kernels for 26%

profile of v4, /device:TPU:0, one launch (start us, length us, event | category | flops | bytes accessed | tf_op | source)
XLA Modules:
  0.0 275.2 jit_solution(3823123130722792538)
XLA Ops:
  0.0 1.3 fusion
  1.5 3.0 %collective-permute-start.1 = (bf16[960,640]{1,0:T(8,128)(2,1)S(1)}, bf16[960,640]{1,0:T(8,128)(2,1)}, u32[]{:S(2)}, u32[]{:S(2)}) collective-permute-start(bf16[960,640]{1,0:T(8,128)(2,1)S(1)} %pad_maximum_fusion.2.refs_3_), channel_id=1, source_target_pairs={{0,8},{4,12},{8,0},{12,4},{16,24},{20,28},{24,16},{28,20},{1,9},{5... | collective-permute-start | bytes 3686408 | tf_op jit(solution)/shard_map/ppermute | solution.py:64
  4.7 1.6 collective-permute-start
  10.6 13.9 %modulated_norm.1.refs_1_ = bf16[8,768,640]{2,1,0:T(8,128)(2,1)} custom-call(s32[2]{0:T(128)} %levels_ref.1, bf16[2,384,5120]{2,1,0:T(8,128)(2,1)} %latents_ref.4, bf16[2,384,5120]{2,1,0:T(8,128)(2,1)} %control_ref.5, f32[3,64,5120]{2,1,0:T(8,128)} %bitcast.20), custom_call_target="tpu_custom_call" | custom-call | flops 2457600 | bytes 1474560 | tf_op jit(solution)/shard_map/modulated_norm/pallas_call | solution.py:98
  24.5 8.0 %collective-permute-done.1.refs_7_ = bf16[960,640]{1,0:T(8,128)(2,1)} collective-permute-done((bf16[960,640]{1,0:T(8,128)(2,1)S(1)}, bf16[960,640]{1,0:T(8,128)(2,1)}, u32[]{:S(2)}, u32[]{:S(2)}) %collective-permute-start.1) | collective-permute-done | bytes 1228832 | tf_op jit(solution)/shard_map/ppermute | solution.py:64
  32.5 2.3 collective-permute-done.refs_8_
  34.8 3.7 %all-to-all-start = ((bf16[8,80,640]{2,1,0:T(8,128)(2,1)}), bf16[8,80,640]{2,1,0:T(8,128)(2,1)S(1)}, u32[]{:S(2)}, u32[]{:S(2)}) async-start(bf16[8,80,640]{2,1,0:T(8,128)(2,1)} %bitcast.26), calls=%async_computation | async-start | bytes 1638400 | tf_op jit(solution)/shard_map/all_to_all | solution.py:572
  38.5 23.5 %collective-permute-done.6.refs_9_ = bf16[960,640]{1,0:T(8,128)(2,1)} collective-permute-done((bf16[960,640]{1,0:T(8,128)(2,1)S(1)}, bf16[960,640]{1,0:T(8,128)(2,1)}, u32[]{:S(2)}, u32[]{:S(2)}) %collective-permute-start.6) | collective-permute-done | bytes 1228832 | tf_op jit(solution)/shard_map/ppermute | solution.py:64
  62.0 6.3 %all-to-all-done = bf16[8,80,640]{2,1,0:T(8,128)(2,1)S(1)} async-done(((bf16[8,80,640]{2,1,0:T(8,128)(2,1)}), bf16[8,80,640]{2,1,0:T(8,128)(2,1)S(1)}, u32[]{:S(2)}, u32[]{:S(2)}) %all-to-all-start) | async-done | bytes 819232 | tf_op jit(solution)/shard_map/all_to_all | solution.py:572
  68.9 1.5 collective-permute-start.11
  71.6 1.8 collective-permute-done.7.refs_10_
  73.4 20.9 %project_begin.1.refs_6_ = f32[768,1920]{1,0:T(8,128)} custom-call(s32[6]{0:T(128)} %stack.80.refs_0_, bf16[8,768,640]{2,1,0:T(8,128)(2,1)} %modulated_norm.1.refs_1_, bf16[960,640]{1,0:T(8,128)(2,1)} %copy-done.4, bf16[960,640]{1,0:T(8,128)(2,1)} %copy-done.3, bf16[960,640]{1,0:T(8,128)(2,1)} %collective-permute-done.3.refs_4_, ...), custom_call_target="tpu_custom_call" | custom-call | flops 707788800 | bytes 1658880 | tf_op jit(solution)/shard_map/project_begin/pallas_call | solution.py:201
  94.3 3.8 %collective-permute-done.11.refs_3_ = bf16[960,640]{1,0:T(8,128)(2,1)S(1)} collective-permute-done((bf16[960,640]{1,0:T(8,128)(2,1)}, bf16[960,640]{1,0:T(8,128)(2,1)S(1)}, u32[]{:S(2)}, u32[]{:S(2)}) %collective-permute-start.11) | collective-permute-done | bytes 1228832 | tf_op jit(solution)/shard_map/ppermute | solution.py:64
  99.3 1.7 collective-permute-done.13.refs_5_
  101.0 1.9 collective-permute-done.12.refs_4_
  102.9 10.7 %project_final.1 = (bf16[2,2,384,640]{3,2,1,0:T(8,128)(2,1)}, bf16[2,1,384,640]{3,2,1,0:T(8,128)(2,1)}, f32[2,6,128]{2,1,0:T(8,128)}) custom-call(s32[2]{0:T(128)} %pad_add_fusion.refs_0_, bf16[8,768,640]{2,1,0:T(8,128)(2,1)} %modulated_norm.1.refs_1_, bf16[960,640]{1,0:T(8,128)(2,1)} %copy-done.10, bf16[960,640]{1,0:T(8,128)(2,1)} %copy-done.9, ...), custom_call_target="tpu_custom_call" | custom-call | flops 235929600 | bytes 798720 | tf_op jit(solution)/shard_map/project_final/pallas_call | solution.py:201
  113.6 2.2 collective-permute-start.18
  115.7 2.1 collective-permute-start.14
  117.8 1.6 collective-permute-done.14
  119.4 4.9 %all-to-all-start.1 = ((bf16[8,80,640]{2,1,0:T(8,128)(2,1)}), bf16[8,80,640]{2,1,0:T(8,128)(2,1)S(1)}, u32[]{:S(2)}, u32[]{:S(2)}) async-start(bf16[8,80,640]{2,1,0:T(8,128)(2,1)} %copy-done.7), calls=%async_computation.1 | async-start | bytes 1638400 | tf_op jit(solution)/shard_map/all_to_all | solution.py:578
  125.0 2.0 collective-permute-start.15
  127.0 5.6 %collective-permute-done.15 = f32[4,6,128]{2,1,0:T(8,128)S(1)} collective-permute-done((f32[4,6,128]{2,1,0:T(8,128)S(1)}, f32[4,6,128]{2,1,0:T(8,128)S(1)}, u32[]{:S(2)}, u32[]{:S(2)}) %collective-permute-start.15) | collective-permute-done | bytes 12320 | tf_op jit(solution)/shard_map/ppermute | solution.py:53
  132.6 4.6 %collective-permute-start.16 = (f32[4,6,128]{2,1,0:T(8,128)S(1)}, f32[4,6,128]{2,1,0:T(8,128)S(1)}, u32[]{:S(2)}, u32[]{:S(2)}) collective-permute-start(f32[4,6,128]{2,1,0:T(8,128)S(1)} %add.15.refs_0_), channel_id=1, source_target_pairs={{0,2},{1,3},{2,0},{3,1},{4,6},{5,7},{6,4},{7,5},{8,10},{9,11},{10,... | collective-permute-start | bytes 36872 | tf_op jit(solution)/shard_map/ppermute | solution.py:53
  137.3 1.8 collective-permute-done.16.refs_1_
  139.1 27.0 %collective-permute-start.21 = (bf16[4,2,80,640]{3,2,1,0:T(8,128)(2,1)S(1)}, bf16[4,2,80,640]{3,2,1,0:T(8,128)(2,1)}, u32[]{:S(2)}, u32[]{:S(2)}) collective-permute-start(bf16[4,2,80,640]{3,2,1,0:T(8,128)(2,1)S(1)} %bitcast.23), channel_id=1, source_target_pairs={{0,16},{4,20},{8,24},{12,28},{16,0},{20,4},{24,8},{28,12},{1,17},{... | collective-permute-start | bytes 2457608 | tf_op jit(solution)/shard_map/ppermute | solution.py:64
  167.2 1.3 copy-done
  168.5 7.1 %attend.2.refs_2_ = bf16[384,640]{1,0:T(8,128)(2,1)} custom-call(s32[2,2]{1,0:T(2,128)} %and_convert_fusion.seen_ref, bf16[2,1,384,640]{3,2,1,0:T(8,128)(2,1)} %get-tuple-element.45.q_ref, f32[1,640]{1,0:T(1,128)} %reshape.21.q_gain_ref, f32[1,640]{1,0:T(1,128)} %reshape.22.k_gain_ref, bf16[2,2,384,640]{3,2,1,0:T(8,128)(2,1)} %copy-done, ...), custom_call_target="tpu_custom_call" | custom-call | flops 70778880 | bytes 245760 | tf_op jit(solution)/shard_map/attend/pallas_call | solution.py:291
  175.5 1.4 collective-permute-start.19
  176.9 1.3 collective-permute-start.20
  178.2 6.4 %collective-permute-start.24 = (bf16[384,640]{1,0:T(8,128)(2,1)}, bf16[384,640]{1,0:T(8,128)(2,1)S(1)}, u32[]{:S(2)}, u32[]{:S(2)}) collective-permute-start(bf16[384,640]{1,0:T(8,128)(2,1)} %attend.2.refs_2_), channel_id=1, source_target_pairs={{0,3},{3,0},{4,7},{7,4},{8,11},{11,8},{12,15},{15,12},{16,19},{19,... | collective-permute-start | bytes 1474568 | tf_op jit(solution)/shard_map/ppermute | solution.py:324
  184.6 4.2 %collective-permute-done.19.refs_3_ = bf16[384,640]{1,0:T(8,128)(2,1)S(1)} collective-permute-done((bf16[384,640]{1,0:T(8,128)(2,1)}, bf16[384,640]{1,0:T(8,128)(2,1)S(1)}, u32[]{:S(2)}, u32[]{:S(2)}) %collective-permute-start.19) | collective-permute-done | bytes 491552 | tf_op jit(solution)/shard_map/ppermute | solution.py:317
  189.5 2.9 %collective-permute-done.20.refs_6_ = bf16[384,640]{1,0:T(8,128)(2,1)S(1)} collective-permute-done((bf16[384,640]{1,0:T(8,128)(2,1)}, bf16[384,640]{1,0:T(8,128)(2,1)S(1)}, u32[]{:S(2)}, u32[]{:S(2)}) %collective-permute-start.20) | collective-permute-done | bytes 491552 | tf_op jit(solution)/shard_map/ppermute | solution.py:317
  192.4 1.3 collective-permute-start.25
  193.7 7.0 %attend.3.refs_0_.refs_2_.refs_5_ = bf16[384,640]{1,0:T(8,128)(2,1)} custom-call(s32[2,2]{1,0:T(2,128)} %and_convert_fusion.seen_ref, bf16[2,1,384,640]{3,2,1,0:T(8,128)(2,1)} %get-tuple-element.45.q_ref, f32[1,640]{1,0:T(1,128)} %reshape.21.q_gain_ref, f32[1,640]{1,0:T(1,128)} %reshape.22.k_gain_ref, bf16[2,2,384,640]{3,2,1,0:T(8,128)(2,1)} %copy-done, ...), custom_call_target="tpu_custom_call" | custom-call | flops 70778880 | bytes 245760 | tf_op jit(solution)/shard_map/attend/pallas_call | solution.py:291
  201.9 2.2 collective-permute-start.22
  205.2 4.8 %collective-permute-done.22 = bf16[2,2,80,640]{3,2,1,0:T(8,128)(2,1)S(1)} collective-permute-done((bf16[2,2,80,640]{3,2,1,0:T(8,128)(2,1)S(1)}, bf16[2,2,80,640]{3,2,1,0:T(8,128)(2,1)S(1)}, u32[]{:S(2)}, u32[]{:S(2)}) %collective-permute-start.22) | collective-permute-done | bytes 409632 | tf_op jit(solution)/shard_map/ppermute | solution.py:64
  210.0 2.1 collective-permute-done.25.refs_7_
  213.2 1.7 pad_maximum_fusion.refs_0_
  215.0 13.0 %collective-permute-start.29 = (bf16[384,640]{1,0:T(8,128)(2,1)}, bf16[384,640]{1,0:T(8,128)(2,1)}, u32[]{:S(2)}, u32[]{:S(2)}) collective-permute-start(bf16[384,640]{1,0:T(8,128)(2,1)} %attend.3.refs_0_.refs_2_.refs_5_), channel_id=1, source_target_pairs={{0,1},{1,2},{2,3},{4,5},{5,6},{6,7},{8,9},{9,10},{10,11},{12,13},{... | collective-permute-start | bytes 1474568 | tf_op jit(solution)/shard_map/ppermute | solution.py:317
  228.0 1.5 collective-permute-start.30
  229.5 8.4 %update_last.1 = bf16[384,1280]{1,0:T(8,128)(2,1)} custom-call(s32[11]{0:T(128)} %concatenate.15.place_ref, bf16[2,384,5120]{2,1,0:T(8,128)(2,1)} %latents_ref.4, bf16[2,384,5120]{2,1,0:T(8,128)(2,1)} %control_ref.5, f32[3,64,5120]{2,1,0:T(8,128)} %bitcast.21, bf16[4,4,2,80,640]{4,3,2,1,0:T(8,128)(2,1)} %copy-done.1, ...), custom_call_target="tpu_custom_call" | custom-call | flops 157286400 | bytes 778240 | tf_op jit(solution)/shard_map/update_last/pallas_call | solution.py:510
  238.2 5.2 %collective-permute-start.31 = (bf16[384,640]{1,0:T(8,128)(2,1)}, bf16[384,640]{1,0:T(8,128)(2,1)S(1)}, u32[]{:S(2)}, u32[]{:S(2)}) collective-permute-start(bf16[384,640]{1,0:T(8,128)(2,1)} %attend.3.refs_0_.refs_2_.refs_5_), channel_id=1, source_target_pairs={{0,3},{3,0},{4,7},{7,4},{8,11},{11,8},{12,15},{15,12},{16,19},{19,... | collective-permute-start | bytes 1474568 | tf_op jit(solution)/shard_map/ppermute | solution.py:324
  244.1 1.3 collective-permute-start.33
  246.1 6.9 %assemble.1.weight_ref = bf16[4,640,1280]{2,1,0:T(8,128)(2,1)} custom-call(s32[8]{0:T(128)} %stack.88.index_ref, bf16[4,4,2,80,640]{4,3,2,1,0:T(8,128)(2,1)} %copy-done.1, bf16[4,4,2,80,640]{4,3,2,1,0:T(8,128)(2,1)} %collective-permute-done.27.refs_1_), custom_call_target="tpu_custom_call" | custom-call | bytes 819200 | tf_op jit(solution)/shard_map/assemble/pallas_call | solution.py:605
  253.0 3.2 %collective-permute-done.31.refs_3_.refs_6_ = bf16[384,640]{1,0:T(8,128)(2,1)S(1)} collective-permute-done((bf16[384,640]{1,0:T(8,128)(2,1)}, bf16[384,640]{1,0:T(8,128)(2,1)S(1)}, u32[]{:S(2)}, u32[]{:S(2)}) %collective-permute-start.31) | collective-permute-done | bytes 491552 | tf_op jit(solution)/shard_map/ppermute | solution.py:324
  256.9 7.1 %update_begin.1.begun_ref = f32[1,384,1280]{2,1,0:T(8,128)} custom-call(s32[11]{0:T(128)} %concatenate.15.place_ref, bf16[4,640,1280]{2,1,0:T(8,128)(2,1)} %assemble.1.weight_ref, bf16[384,640]{1,0:T(8,128)(2,1)} %attend.3.refs_0_.refs_2_.refs_5_, bf16[384,640]{1,0:T(8,128)(2,1)} %collective-permute-done.29.refs_1_, ...), custom_call_target="tpu_custom_call" | custom-call | flops 117964800 | bytes 645120 | tf_op jit(solution)/shard_map/update_begin/pallas_call | solution.py:527
  264.1 2.5 collective-permute-done.33.refs_5_
  268.2 6.7 %update_rest.1 = f32[2,384,1280]{2,1,0:T(8,128)} custom-call(s32[11]{0:T(128)} %concatenate.15.place_ref, bf16[384,1280]{1,0:T(8,128)(2,1)} %copy-done.12, f32[1,384,1280]{2,1,0:T(8,128)} %update_begin.1.begun_ref, bf16[4,640,1280]{2,1,0:T(8,128)(2,1)} %assemble.1.weight_ref, bf16[2,384,5120]{2,1,0:T(8,128)(2,1)} %latents_ref.4, ...), custom_call_target="tpu_custom_call" | custom-call | flops 39321600 | bytes 378880 | tf_op jit(solution)/shard_map/update_rest/pallas_call | solution.py:551
  (107 shorter events, 17.7 us)
Async XLA Ops:
  1.4 8.6 %copy-start.26 = (s32[2,2]{1,0:T(2,128)S(1)}, s32[2,2]{1,0:T(2,128)}, u32[]{:S(2)}) copy-start(s32[2,2]{1,0:T(2,128)} %param.15) | copy-start | bytes 52
  1.4 8.6 %copy-start.27 = (s32[2]{0:T(128)S(1)}, s32[2]{0:T(128)}, u32[]{:S(2)}) copy-start(s32[2]{0:T(128)} %constant.26.clone) | copy-start | bytes 28
  1.5 31.0 %copy-start.3 = (bf16[960,640]{1,0:T(8,128)(2,1)}, bf16[960,640]{1,0:T(8,128)(2,1)S(1)}, u32[]{:S(2)}) copy-start(bf16[960,640]{1,0:T(8,128)(2,1)S(1)} %pad_maximum_fusion.2.refs_3_) | copy-start | bytes 3686404
  1.5 31.0 %collective-permute-start.1 = (bf16[960,640]{1,0:T(8,128)(2,1)S(1)}, bf16[960,640]{1,0:T(8,128)(2,1)}, u32[]{:S(2)}, u32[]{:S(2)}) collective-permute-start(bf16[960,640]{1,0:T(8,128)(2,1)S(1)} %pad_maximum_fusion.2.refs_3_), channel_id=1, source_target_pairs={{0,8},{4,12},{8,0},{12,4},{16,24},{20,28},{24,16},{28,20},{1,9},{5... | collective-permute-start | bytes 3686408 | tf_op jit(solution)/shard_map/ppermute | solution.py:64
  4.7 19.8 %copy-start.4 = (bf16[960,640]{1,0:T(8,128)(2,1)}, bf16[960,640]{1,0:T(8,128)(2,1)S(1)}, u32[]{:S(2)}) copy-start(bf16[960,640]{1,0:T(8,128)(2,1)S(1)} %pad_maximum_fusion.1.refs_2_) | copy-start | bytes 3686404
  4.7 30.1 %collective-permute-start = (bf16[960,640]{1,0:T(8,128)(2,1)S(1)}, bf16[960,640]{1,0:T(8,128)(2,1)}, u32[]{:S(2)}, u32[]{:S(2)}) collective-permute-start(bf16[960,640]{1,0:T(8,128)(2,1)S(1)} %pad_maximum_fusion.1.refs_2_), channel_id=1, source_target_pairs={{0,16},{4,20},{8,24},{12,28},{16,0},{20,4},{24,8},{28,12},{1,17},{... | collective-permute-start | bytes 3686408 | tf_op jit(solution)/shard_map/ppermute | solution.py:64
  6.3 55.7 %collective-permute-start.6 = (bf16[960,640]{1,0:T(8,128)(2,1)S(1)}, bf16[960,640]{1,0:T(8,128)(2,1)}, u32[]{:S(2)}, u32[]{:S(2)}) collective-permute-start(bf16[960,640]{1,0:T(8,128)(2,1)S(1)} %pad_maximum_fusion.2.refs_3_), channel_id=1, source_target_pairs={{0,16},{4,20},{8,24},{12,28},{16,0},{20,4},{24,8},{28,12},{1,17},{... | collective-permute-start | bytes 3686408 | tf_op jit(solution)/shard_map/ppermute | solution.py:64
  6.8 61.6 %collective-permute-start.5 = (bf16[960,640]{1,0:T(8,128)(2,1)S(1)}, bf16[960,640]{1,0:T(8,128)(2,1)}, u32[]{:S(2)}, u32[]{:S(2)}) collective-permute-start(bf16[960,640]{1,0:T(8,128)(2,1)S(1)} %pad_maximum_fusion.1.refs_2_), channel_id=1, source_target_pairs={{0,8},{4,12},{8,0},{12,4},{16,24},{20,28},{24,16},{28,20},{1,9},{5... | collective-permute-start | bytes 3686408 | tf_op jit(solution)/shard_map/ppermute | solution.py:64
  24.4 43.9 %collective-permute-start.3 = (bf16[960,640]{1,0:T(8,128)(2,1)S(1)}, bf16[960,640]{1,0:T(8,128)(2,1)}, u32[]{:S(2)}, u32[]{:S(2)}) collective-permute-start(bf16[960,640]{1,0:T(8,128)(2,1)S(1)} %pad_maximum_fusion.1.refs_2_), channel_id=1, source_target_pairs={{0,4},{4,0},{8,12},{12,8},{16,20},{20,16},{24,28},{28,24},{1,5},{5... | collective-permute-start | bytes 3686408 | tf_op jit(solution)/shard_map/ppermute | solution.py:64
  32.5 36.3 %collective-permute-start.4 = (bf16[960,640]{1,0:T(8,128)(2,1)S(1)}, bf16[960,640]{1,0:T(8,128)(2,1)}, u32[]{:S(2)}, u32[]{:S(2)}) collective-permute-start(bf16[960,640]{1,0:T(8,128)(2,1)S(1)} %pad_maximum_fusion.2.refs_3_), channel_id=1, source_target_pairs={{0,4},{4,0},{8,12},{12,8},{16,20},{20,16},{24,28},{28,24},{1,5},{5... | collective-permute-start | bytes 3686408 | tf_op jit(solution)/shard_map/ppermute | solution.py:64
  34.8 35.6 %collective-permute-start.8 = (bf16[960,640]{1,0:T(8,128)(2,1)}, bf16[960,640]{1,0:T(8,128)(2,1)}, u32[]{:S(2)}, u32[]{:S(2)}) collective-permute-start(bf16[960,640]{1,0:T(8,128)(2,1)} %collective-permute-done.1.refs_7_), channel_id=1, source_target_pairs={{0,4},{4,0},{8,12},{12,8},{16,20},{20,16},{24,28},{28,24},{1,5},{5... | collective-permute-start | bytes 3686408 | tf_op jit(solution)/shard_map/ppermute | solution.py:64
  34.8 33.5 %all-to-all-start = ((bf16[8,80,640]{2,1,0:T(8,128)(2,1)}), bf16[8,80,640]{2,1,0:T(8,128)(2,1)S(1)}, u32[]{:S(2)}, u32[]{:S(2)}) async-start(bf16[8,80,640]{2,1,0:T(8,128)(2,1)} %bitcast.26), calls=%async_computation | async-start | bytes 1638400 | tf_op jit(solution)/shard_map/all_to_all | solution.py:572
  62.0 8.9 %collective-permute-start.9 = (bf16[960,640]{1,0:T(8,128)(2,1)}, bf16[960,640]{1,0:T(8,128)(2,1)}, u32[]{:S(2)}, u32[]{:S(2)}) collective-permute-start(bf16[960,640]{1,0:T(8,128)(2,1)} %collective-permute-done.refs_8_), channel_id=1, source_target_pairs={{0,4},{4,0},{8,12},{12,8},{16,20},{20,16},{24,28},{28,24},{1,5},{5... | collective-permute-start | bytes 3686408 | tf_op jit(solution)/shard_map/ppermute | solution.py:64
  68.3 26.0 %copy-start.7 = (bf16[8,80,640]{2,1,0:T(8,128)(2,1)}, bf16[8,80,640]{2,1,0:T(8,128)(2,1)S(1)}, u32[]{:S(2)}) copy-start(bf16[8,80,640]{2,1,0:T(8,128)(2,1)S(1)} %all-to-all-done) | copy-start | bytes 2457604
  68.3 3.3 %collective-permute-start.10 = (bf16[960,640]{1,0:T(8,128)(2,1)}, bf16[960,640]{1,0:T(8,128)(2,1)}, u32[]{:S(2)}, u32[]{:S(2)}) collective-permute-start(bf16[960,640]{1,0:T(8,128)(2,1)} %collective-permute-done.6.refs_9_), channel_id=1, source_target_pairs={{0,4},{4,0},{8,12},{12,8},{16,20},{20,16},{24,28},{28,24},{1,5},{5... | collective-permute-start | bytes 3686408 | tf_op jit(solution)/shard_map/ppermute | solution.py:64
  68.3 5.0 %collective-permute-start.7 = (bf16[960,640]{1,0:T(8,128)(2,1)}, bf16[960,640]{1,0:T(8,128)(2,1)}, u32[]{:S(2)}, u32[]{:S(2)}) collective-permute-start(bf16[960,640]{1,0:T(8,128)(2,1)} %collective-permute-done.5.refs_6_), channel_id=1, source_target_pairs={{0,4},{4,0},{8,12},{12,8},{16,20},{20,16},{24,28},{28,24},{1,5},{5... | collective-permute-start | bytes 3686408 | tf_op jit(solution)/shard_map/ppermute | solution.py:64
  68.9 29.2 %collective-permute-start.11 = (bf16[960,640]{1,0:T(8,128)(2,1)}, bf16[960,640]{1,0:T(8,128)(2,1)S(1)}, u32[]{:S(2)}, u32[]{:S(2)}) collective-permute-start(bf16[960,640]{1,0:T(8,128)(2,1)} %collective-permute-done.1.refs_7_), channel_id=1, source_target_pairs={{0,16},{4,20},{8,24},{12,28},{16,0},{20,4},{24,8},{28,12},{1,17},{... | collective-permute-start | bytes 3686408 | tf_op jit(solution)/shard_map/ppermute | solution.py:64
  70.4 28.9 %collective-permute-start.2 = (bf16[960,640]{1,0:T(8,128)(2,1)}, bf16[960,640]{1,0:T(8,128)(2,1)S(1)}, u32[]{:S(2)}, u32[]{:S(2)}) collective-permute-start(bf16[960,640]{1,0:T(8,128)(2,1)} %collective-permute-done.refs_8_), channel_id=1, source_target_pairs={{0,8},{4,12},{8,0},{12,4},{16,24},{20,28},{24,16},{28,20},{1,9},{5... | collective-permute-start | bytes 3686408 | tf_op jit(solution)/shard_map/ppermute | solution.py:64
  98.1 2.9 %collective-permute-start.13 = (bf16[960,640]{1,0:T(8,128)(2,1)S(1)}, bf16[960,640]{1,0:T(8,128)(2,1)S(1)}, u32[]{:S(2)}, u32[]{:S(2)}) collective-permute-start(bf16[960,640]{1,0:T(8,128)(2,1)S(1)} %collective-permute-done.11.refs_3_), channel_id=1, source_target_pairs={{0,4},{4,0},{8,12},{12,8},{16,20},{20,16},{24,28},{28,24},{1,5},{5... | collective-permute-start | bytes 3686408 | tf_op jit(solution)/shard_map/ppermute | solution.py:64
  99.3 3.6 %collective-permute-start.12 = (bf16[960,640]{1,0:T(8,128)(2,1)S(1)}, bf16[960,640]{1,0:T(8,128)(2,1)}, u32[]{:S(2)}, u32[]{:S(2)}) collective-permute-start(bf16[960,640]{1,0:T(8,128)(2,1)S(1)} %collective-permute-done.2.refs_2_), channel_id=1, source_target_pairs={{0,4},{4,0},{8,12},{12,8},{16,20},{20,16},{24,28},{28,24},{1,5},{5... | collective-permute-start | bytes 3686408 | tf_op jit(solution)/shard_map/ppermute | solution.py:64
  113.6 53.6 %collective-permute-start.18 = (bf16[2,2,384,640]{3,2,1,0:T(8,128)(2,1)}, bf16[2,2,384,640]{3,2,1,0:T(8,128)(2,1)S(1)}, u32[]{:S(2)}, u32[]{:S(2)}) collective-permute-start(bf16[2,2,384,640]{3,2,1,0:T(8,128)(2,1)} %get-tuple-element.44.k1.k2.v1.v2), channel_id=1, source_target_pairs={{0,4},{4,8},{8,12},{12,16},{16,20},{20,24},{24,28},{1,5},{5,9},{9,... | collective-permute-start | bytes 5898248 | tf_op jit(solution)/shard_map/ppermute | solution.py:33
  115.7 3.7 %collective-permute-start.14 = (f32[2,6,128]{2,1,0:T(8,128)}, f32[2,6,128]{2,1,0:T(8,128)S(1)}, u32[]{:S(2)}, u32[]{:S(2)}) collective-permute-start(f32[2,6,128]{2,1,0:T(8,128)} %get-tuple-element.40), channel_id=1, source_target_pairs={{0,4},{4,8},{8,12},{12,16},{16,20},{20,24},{24,28},{1,5},{5,9},{9,... | collective-permute-start | bytes 18440 | tf_op jit(solution)/shard_map/ppermute | solution.py:33
  119.4 19.7 %all-to-all-start.1 = ((bf16[8,80,640]{2,1,0:T(8,128)(2,1)}), bf16[8,80,640]{2,1,0:T(8,128)(2,1)S(1)}, u32[]{:S(2)}, u32[]{:S(2)}) async-start(bf16[8,80,640]{2,1,0:T(8,128)(2,1)} %copy-done.7), calls=%async_computation.1 | async-start | bytes 1638400 | tf_op jit(solution)/shard_map/all_to_all | solution.py:578
  125.0 7.6 %collective-permute-start.15 = (f32[4,6,128]{2,1,0:T(8,128)S(1)}, f32[4,6,128]{2,1,0:T(8,128)S(1)}, u32[]{:S(2)}, u32[]{:S(2)}) collective-permute-start(f32[4,6,128]{2,1,0:T(8,128)S(1)} %constant_dynamic-update-slice_fusion), channel_id=1, source_target_pairs={{0,1},{1,0},{2,3},{3,2},{4,5},{5,4},{6,7},{7,6},{8,9},{9,8},{10,11... | collective-permute-start | bytes 36872 | tf_op jit(solution)/shard_map/ppermute | solution.py:53
  132.6 34.5 %copy-start.21 = (f32[4,6,128]{2,1,0:T(8,128)}, f32[4,6,128]{2,1,0:T(8,128)S(1)}, u32[]{:S(2)}) copy-start(f32[4,6,128]{2,1,0:T(8,128)S(1)} %add.15.refs_0_) | copy-start | bytes 36868
  132.6 6.5 %collective-permute-start.16 = (f32[4,6,128]{2,1,0:T(8,128)S(1)}, f32[4,6,128]{2,1,0:T(8,128)S(1)}, u32[]{:S(2)}, u32[]{:S(2)}) collective-permute-start(f32[4,6,128]{2,1,0:T(8,128)S(1)} %add.15.refs_0_), channel_id=1, source_target_pairs={{0,2},{1,3},{2,0},{3,1},{4,6},{5,7},{6,4},{7,5},{8,10},{9,11},{10,... | collective-permute-start | bytes 36872 | tf_op jit(solution)/shard_map/ppermute | solution.py:53
  139.1 28.0 %copy-start.22 = (f32[4,6,128]{2,1,0:T(8,128)}, f32[4,6,128]{2,1,0:T(8,128)S(1)}, u32[]{:S(2)}) copy-start(f32[4,6,128]{2,1,0:T(8,128)S(1)} %collective-permute-done.16.refs_1_) | copy-start | bytes 36868
  139.1 36.4 %copy-start.5 = (bf16[8,80,640]{2,1,0:T(8,128)(2,1)}, bf16[8,80,640]{2,1,0:T(8,128)(2,1)S(1)}, u32[]{:S(2)}) copy-start(bf16[8,80,640]{2,1,0:T(8,128)(2,1)S(1)} %all-to-all-done.1) | copy-start | bytes 2457604
  139.1 61.6 %collective-permute-start.21 = (bf16[4,2,80,640]{3,2,1,0:T(8,128)(2,1)S(1)}, bf16[4,2,80,640]{3,2,1,0:T(8,128)(2,1)}, u32[]{:S(2)}, u32[]{:S(2)}) collective-permute-start(bf16[4,2,80,640]{3,2,1,0:T(8,128)(2,1)S(1)} %bitcast.23), channel_id=1, source_target_pairs={{0,16},{4,20},{8,24},{12,28},{16,0},{20,4},{24,8},{28,12},{1,17},{... | collective-permute-start | bytes 2457608 | tf_op jit(solution)/shard_map/ppermute | solution.py:64
  166.1 37.9 %collective-permute-start.17 = (bf16[4,2,80,640]{3,2,1,0:T(8,128)(2,1)S(1)}, bf16[4,2,80,640]{3,2,1,0:T(8,128)(2,1)}, u32[]{:S(2)}, u32[]{:S(2)}) collective-permute-start(bf16[4,2,80,640]{3,2,1,0:T(8,128)(2,1)S(1)} %bitcast.24), channel_id=1, source_target_pairs={{0,8},{4,12},{8,0},{12,4},{16,24},{20,28},{24,16},{28,20},{1,9},{5... | collective-permute-start | bytes 2457608 | tf_op jit(solution)/shard_map/ppermute | solution.py:64
  175.5 13.3 %collective-permute-start.19 = (bf16[384,640]{1,0:T(8,128)(2,1)}, bf16[384,640]{1,0:T(8,128)(2,1)S(1)}, u32[]{:S(2)}, u32[]{:S(2)}) collective-permute-start(bf16[384,640]{1,0:T(8,128)(2,1)} %attend.2.refs_2_), channel_id=1, source_target_pairs={{0,1},{1,2},{2,3},{4,5},{5,6},{6,7},{8,9},{9,10},{10,11},{12,13},{... | collective-permute-start | bytes 1474568 | tf_op jit(solution)/shard_map/ppermute | solution.py:317
  176.9 15.6 %collective-permute-start.20 = (bf16[384,640]{1,0:T(8,128)(2,1)}, bf16[384,640]{1,0:T(8,128)(2,1)S(1)}, u32[]{:S(2)}, u32[]{:S(2)}) collective-permute-start(bf16[384,640]{1,0:T(8,128)(2,1)} %attend.2.refs_2_), channel_id=1, source_target_pairs={{1,0},{2,1},{3,2},{5,4},{6,5},{7,6},{9,8},{10,9},{11,10},{13,12},{... | collective-permute-start | bytes 1474568 | tf_op jit(solution)/shard_map/ppermute | solution.py:317
  178.2 27.0 %collective-permute-start.24 = (bf16[384,640]{1,0:T(8,128)(2,1)}, bf16[384,640]{1,0:T(8,128)(2,1)S(1)}, u32[]{:S(2)}, u32[]{:S(2)}) collective-permute-start(bf16[384,640]{1,0:T(8,128)(2,1)} %attend.2.refs_2_), channel_id=1, source_target_pairs={{0,3},{3,0},{4,7},{7,4},{8,11},{11,8},{12,15},{15,12},{16,19},{19,... | collective-permute-start | bytes 1474568 | tf_op jit(solution)/shard_map/ppermute | solution.py:324
  188.8 11.9 %copy-start.15 = (bf16[384,640]{1,0:T(8,128)(2,1)}, bf16[384,640]{1,0:T(8,128)(2,1)S(1)}, u32[]{:S(2)}) copy-start(bf16[384,640]{1,0:T(8,128)(2,1)S(1)} %collective-permute-done.19.refs_3_) | copy-start | bytes 1474564
  188.8 21.1 %collective-permute-start.23 = (bf16[384,640]{1,0:T(8,128)(2,1)S(1)}, bf16[384,640]{1,0:T(8,128)(2,1)S(1)}, u32[]{:S(2)}, u32[]{:S(2)}) collective-permute-start(bf16[384,640]{1,0:T(8,128)(2,1)S(1)} %collective-permute-done.19.refs_3_), channel_id=1, source_target_pairs={{1,2},{2,3},{5,6},{6,7},{9,10},{10,11},{13,14},{14,15},{17,18},{18... | collective-permute-start | bytes 1474568 | tf_op jit(solution)/shard_map/ppermute | solution.py:317
  192.4 19.6 %collective-permute-start.25 = (bf16[384,640]{1,0:T(8,128)(2,1)S(1)}, bf16[384,640]{1,0:T(8,128)(2,1)S(1)}, u32[]{:S(2)}, u32[]{:S(2)}) collective-permute-start(bf16[384,640]{1,0:T(8,128)(2,1)S(1)} %collective-permute-done.20.refs_6_), channel_id=1, source_target_pairs={{1,0},{2,1},{5,4},{6,5},{9,8},{10,9},{13,12},{14,13},{17,16},{18,1... | collective-permute-start | bytes 1474568 | tf_op jit(solution)/shard_map/ppermute | solution.py:317
  200.8 12.5 %copy-start.6 = (bf16[8,80,640]{2,1,0:T(8,128)(2,1)S(1)}, bf16[8,80,640]{2,1,0:T(8,128)(2,1)}, u32[]{:S(2)}) copy-start(bf16[8,80,640]{2,1,0:T(8,128)(2,1)} %copy-done.5) | copy-start | bytes 2457604
  201.9 8.1 %collective-permute-start.22 = (bf16[2,2,80,640]{3,2,1,0:T(8,128)(2,1)S(1)}, bf16[2,2,80,640]{3,2,1,0:T(8,128)(2,1)S(1)}, u32[]{:S(2)}, u32[]{:S(2)}) collective-permute-start(bf16[2,2,80,640]{3,2,1,0:T(8,128)(2,1)S(1)} %slice.14), channel_id=1, source_target_pairs={{0,8},{4,12},{8,0},{12,4},{16,24},{20,28},{24,16},{28,20},{1,9},{5... | collective-permute-start | bytes 1228808 | tf_op jit(solution)/shard_map/ppermute | solution.py:64
  205.1 8.0 %collective-permute-start.26 = (bf16[2,2,80,640]{3,2,1,0:T(8,128)(2,1)S(1)}, bf16[2,2,80,640]{3,2,1,0:T(8,128)(2,1)S(1)}, u32[]{:S(2)}, u32[]{:S(2)}) collective-permute-start(bf16[2,2,80,640]{3,2,1,0:T(8,128)(2,1)S(1)} %slice.15), channel_id=1, source_target_pairs={{0,16},{4,20},{8,24},{12,28},{16,0},{20,4},{24,8},{28,12},{1,17},{... | collective-permute-start | bytes 1228808 | tf_op jit(solution)/shard_map/ppermute | solution.py:64
  205.2 9.7 %copy-start.8 = (bf16[384,640]{1,0:T(8,128)(2,1)}, bf16[384,640]{1,0:T(8,128)(2,1)S(1)}, u32[]{:S(2)}) copy-start(bf16[384,640]{1,0:T(8,128)(2,1)S(1)} %collective-permute-done.24.refs_5_.refs_8_) | copy-start | bytes 1474564
  214.9 14.6 %copy-start.1 = (bf16[4,4,2,80,640]{4,3,2,1,0:T(8,128)(2,1)}, bf16[4,4,2,80,640]{4,3,2,1,0:T(8,128)(2,1)S(1)}, u32[]{:S(2)}) copy-start(bf16[4,4,2,80,640]{4,3,2,1,0:T(8,128)(2,1)S(1)} %pad_maximum_fusion.refs_0_) | copy-start | bytes 9830404
  214.9 14.6 %collective-permute-start.27 = (bf16[4,4,2,80,640]{4,3,2,1,0:T(8,128)(2,1)S(1)}, bf16[4,4,2,80,640]{4,3,2,1,0:T(8,128)(2,1)}, u32[]{:S(2)}, u32[]{:S(2)}) collective-permute-start(bf16[4,4,2,80,640]{4,3,2,1,0:T(8,128)(2,1)S(1)} %pad_maximum_fusion.refs_0_), channel_id=1, source_target_pairs={{0,4},{4,0},{8,12},{12,8},{16,20},{20,16},{24,28},{28,24},{1,5},{5... | collective-permute-start | bytes 9830408 | tf_op jit(solution)/shard_map/ppermute | solution.py:64
  215.0 28.4 %collective-permute-start.29 = (bf16[384,640]{1,0:T(8,128)(2,1)}, bf16[384,640]{1,0:T(8,128)(2,1)}, u32[]{:S(2)}, u32[]{:S(2)}) collective-permute-start(bf16[384,640]{1,0:T(8,128)(2,1)} %attend.3.refs_0_.refs_2_.refs_5_), channel_id=1, source_target_pairs={{0,1},{1,2},{2,3},{4,5},{5,6},{6,7},{8,9},{9,10},{10,11},{12,13},{... | collective-permute-start | bytes 1474568 | tf_op jit(solution)/shard_map/ppermute | solution.py:317
  228.0 16.1 %collective-permute-start.30 = (bf16[384,640]{1,0:T(8,128)(2,1)}, bf16[384,640]{1,0:T(8,128)(2,1)}, u32[]{:S(2)}, u32[]{:S(2)}) collective-permute-start(bf16[384,640]{1,0:T(8,128)(2,1)} %attend.3.refs_0_.refs_2_.refs_5_), channel_id=1, source_target_pairs={{1,0},{2,1},{3,2},{5,4},{6,5},{7,6},{9,8},{10,9},{11,10},{13,12},{... | collective-permute-start | bytes 1474568 | tf_op jit(solution)/shard_map/ppermute | solution.py:317
  237.9 28.6 %collective-permute-start.28 = (bf16[384,1280]{1,0:T(8,128)(2,1)}, bf16[384,1280]{1,0:T(8,128)(2,1)S(1)}, u32[]{:S(2)}, u32[]{:S(2)}) collective-permute-start(bf16[384,1280]{1,0:T(8,128)(2,1)} %update_last.1), channel_id=1, source_target_pairs={{0,4},{4,8},{8,12},{12,16},{16,20},{20,24},{24,28},{28,0},{1,5},{5... | collective-permute-start | bytes 2949128 | tf_op jit(solution)/shard_map/ppermute | solution.py:39
  238.2 18.0 %collective-permute-start.31 = (bf16[384,640]{1,0:T(8,128)(2,1)}, bf16[384,640]{1,0:T(8,128)(2,1)S(1)}, u32[]{:S(2)}, u32[]{:S(2)}) collective-permute-start(bf16[384,640]{1,0:T(8,128)(2,1)} %attend.3.refs_0_.refs_2_.refs_5_), channel_id=1, source_target_pairs={{0,3},{3,0},{4,7},{7,4},{8,11},{11,8},{12,15},{15,12},{16,19},{19,... | collective-permute-start | bytes 1474568 | tf_op jit(solution)/shard_map/ppermute | solution.py:324
  243.4 20.6 %collective-permute-start.32 = (bf16[384,640]{1,0:T(8,128)(2,1)}, bf16[384,640]{1,0:T(8,128)(2,1)S(1)}, u32[]{:S(2)}, u32[]{:S(2)}) collective-permute-start(bf16[384,640]{1,0:T(8,128)(2,1)} %collective-permute-done.29.refs_1_), channel_id=1, source_target_pairs={{1,2},{2,3},{5,6},{6,7},{9,10},{10,11},{13,14},{14,15},{17,18},{18... | collective-permute-start | bytes 1474568 | tf_op jit(solution)/shard_map/ppermute | solution.py:317
  244.1 22.4 %collective-permute-start.33 = (bf16[384,640]{1,0:T(8,128)(2,1)}, bf16[384,640]{1,0:T(8,128)(2,1)S(1)}, u32[]{:S(2)}, u32[]{:S(2)}) collective-permute-start(bf16[384,640]{1,0:T(8,128)(2,1)} %collective-permute-done.30.refs_4_), channel_id=1, source_target_pairs={{1,0},{2,1},{5,4},{6,5},{9,8},{10,9},{13,12},{14,13},{17,16},{18,1... | collective-permute-start | bytes 1474568 | tf_op jit(solution)/shard_map/ppermute | solution.py:317
  (16 other events, 54.0 us)
